TPU v7x, 1024 devices: a whole 8x8x8 slice. The times are simulated.
1024 devices in a mesh: rep: 64 (over x, y_lo, core), fsdp: 16 (over y_hi, z).
Axes of the slice: x: 8, y: 8 (y_hi: 2, y_lo: 4; y = y_hi * 4 + y_lo), z: 8, core: 2. Of those that a mesh axis runs over, the one named last changes fastest.
Arguments:
- tokens: bfloat16 [131072, 5120], P(('rep', 'fsdp')), may hold values from -6 to 6
- momentum: float32 [64, 512, 5120], P('rep', 'fsdp'), may hold values from -6 to 6
- gradient: bfloat16 [64, 512, 5120], P('rep', 'fsdp'), may hold values from -6 to 6
- weight: bfloat16 [512, 5120], P('fsdp'), may hold values from -0.078125 to 0.078125
- kept_index: int32 [512, 80, 8], P('fsdp'), may hold values from 0 to 63, all different within a row
Outputs:
- new_weight: bfloat16 [512, 5120], P('fsdp')
- new_momentum: float32 [64, 512, 5120], P('rep', 'fsdp')
- projected: bfloat16 [131072, 512], P(('rep', 'fsdp'))
Inputs may be any that keep to these rules, and one draw needn't show every extreme that they name: `kept_index`: the 8 entries of each block are distinct frequencies.
All inputs are finite; a program needn't handle non-finite values.
Results may differ from a plain program's by a relative error of at most 0.005.
Values may be sent and summed in bfloat16 or wider, within the bound.
No kernel may reach another device: no remote copies, remote signals or barrier semaphores. Data moves between devices by JAX's collectives and lax.ppermute only.
A program may use at most 64 MiB of HBM per device.

v0:
```python
import jax
import jax.numpy as jnp
from jax import lax
from jax.sharding import PartitionSpec as P

GROUP = 64
KEEP = 8


step_size = 0.01
decay_rate = 0.1


def cosine_table():
    frequency = jnp.arange(GROUP, dtype=jnp.float32)[:, None]
    position = jnp.arange(GROUP, dtype=jnp.float32)[None, :]
    factor = jnp.where(frequency == 0.0, jnp.sqrt(1.0 / GROUP), jnp.sqrt(2.0 / GROUP)).astype(
        jnp.float32
    )
    return factor * jnp.cos(jnp.pi * (position + 0.5) * frequency / GROUP)


def apply_update(total, basis_rows, old_blocks):
    dense = jnp.einsum("ck,ckn->cn", total, basis_rows, precision=lax.Precision.HIGHEST)
    direction = dense / jnp.sqrt(jnp.mean(dense * dense, axis=-1, keepdims=True) + 1e-06)
    return (
        old_blocks.astype(jnp.float32) * (1.0 - step_size * decay_rate) - step_size * direction
    ).astype(jnp.bfloat16)


def body(tokens, momentum, gradient, weight, kept_index):
    highest = lax.Precision.HIGHEST
    row_count = weight.shape[0]
    width = weight.shape[1]
    block_count = row_count * (width // GROUP)
    accum = 0.9 * momentum[0] + gradient[0].astype(jnp.float32)
    blocks = accum.reshape(block_count, GROUP)
    index_flat = kept_index.reshape(block_count, KEEP)
    onehot = (index_flat[..., None] == jnp.arange(GROUP, dtype=jnp.int32)).astype(jnp.float32)
    basis_rows = jnp.einsum("ckj,jn->ckn", onehot, cosine_table(), precision=highest)
    kept = jnp.einsum("cn,ckn->ck", blocks, basis_rows, precision=highest)
    sent_part = jnp.einsum("ck,ckn->cn", kept, basis_rows, precision=highest)
    new_momentum = (blocks - sent_part).reshape(1, row_count, width)
    old_blocks = weight.reshape(block_count, GROUP)
    every_kept = lax.all_gather(kept[None], "rep", axis=0, tiled=True)
    total = jnp.sum(every_kept, axis=0)
    new_weight = apply_update(total, basis_rows, old_blocks).reshape(row_count, width)
    projected = lax.dot_general(
        tokens,
        lax.all_gather(new_weight, "fsdp", axis=0, tiled=True),
        (((1,), (1,)), ((), ())),
        preferred_element_type=jnp.float32,
    ).astype(jnp.bfloat16)
    return (new_weight, new_momentum, projected)


def solution(mesh):
    placed = (
        P(("rep", "fsdp"), None),
        P("rep", "fsdp", None),
        P("rep", "fsdp", None),
        P("fsdp", None),
        P("fsdp", None, None),
    )
    return jax.shard_map(
        body,
        mesh=mesh,
        in_specs=placed,
        out_specs=(P("fsdp", None), P("rep", "fsdp", None), P(("rep", "fsdp"), None)),
        check_vma=False,
    )
```

profile of v0, /device:TPU:1, one launch (start us, length us, event | category | flops | bytes accessed | tf_op | source)
XLA Modules:
  0.0 329.4 jit_solution(5283089403334003948)
XLA Ops:
  7.2 0.0 copy-start
  7.2 0.0 all-gather.6.cloned.1.call-start
  7.2 1.3 convert_add_fusion
  8.6 0.3 add.30
  8.9 0.0 copy-start.1
  8.9 0.0 copy-start.5
  9.0 0.4 copy.29
  9.3 0.6 copy-done.5
  10.0 0.1 eq.26
  10.1 6.3 %multiply_reduce_fusion.2 = (f32[2560,8]{0,1:T(8,128)}, f32[2560,8,64]{0,2,1:T(8,128)}) fusion(f32[2560,64]{0,1:T(8,128)S(1)} %copy.29, f32[64]{0:T(128)S(1)} %get-tuple-element.17, f32[64]{0:T(128)S(1)} %get-tuple-element.16, s32[2560,8]{0,1:T(8,128)S(1)} %eq.26), kind=kOutput, calls=%fused_computation.2 | convolution fusion | flops 1010556928 | bytes 6062592 | tf_op jit(solution)/shard_map/ckj,jn->ckn/dot_general | solution.py:40
  16.4 0.0 copy-done.1
  16.4 0.0 all-gather.6.cloned.1.call-update
  16.5 0.0 all-gather.4.cloned.1.call-start
  16.5 1.0 convert_multiply_fusion
  17.6 1.5 mul.60
  19.0 134.7 %all-gather.6.cloned.1.call-done = f32[163840,8]{0,1:T(8,128)} async-done(((f32[2560,8]{0,1:T(8,128)}), f32[163840,8]{0,1:T(8,128)}) %all-gather.6.cloned.1.call-update) | async-done | bytes 5242896 | tf_op jit(solution)/shard_map/all_gather | solution.py:45
  153.7 0.0 copy-start.4
  153.7 2.8 reduce_sum.18
  156.5 0.0 copy-done.4
  156.5 4.2 %multiply_reduce_fusion = (f32[2560,64]{0,1:T(8,128)S(1)}, f32[2560,64]{0,1:T(8,128)}) fusion(f32[2560,8,64]{0,2,1:T(8,128)} %get-tuple-element.15, f32[2560,8]{0,1:T(8,128)S(1)} %copy-done.4, f32[2560,8]{0,1:T(8,128)S(1)} %reduce_sum.18), kind=kLoop, calls=%fused_computation | loop fusion | flops 4915200 | bytes 6717440
  160.7 1.5 copy.23
  162.2 0.0 copy-start.3
  162.2 0.4 multiply_reduce_fusion.3
  162.7 0.9 copy-done.3
  163.5 1.3 subtract_convert_fusion
  164.8 2.3 reshape.46
  167.1 0.0 copy-start.2
  167.1 0.0 all-gather.4.cloned.1.call-update
  167.2 1.5 copy.28
  168.7 0.0 copy-done.2
  168.7 2.6 sub.7
  171.2 2.5 reshape.47
  173.8 144.0 %all-gather.4.cloned.1.call-done = bf16[512,5120]{1,0:T(8,128)(2,1)} async-done(((bf16[32,5120]{1,0:T(8,128)(2,1)}), bf16[512,5120]{1,0:T(8,128)(2,1)}) %all-gather.4.cloned.1.call-update) | async-done | bytes 5242896 | tf_op jit(solution)/shard_map/all_gather | solution.py:50
  317.8 0.0 copy-done
  317.8 4.0 %fusion.2 = bf16[128,512]{0,1:T(8,128)(2,1)S(1)} fusion(bf16[512,5120]{1,0:T(8,128)(2,1)} %all-gather.4.cloned.1.call-done, bf16[128,5120]{1,0:T(8,128)(2,1)S(1)} %copy-done), kind=kOutput, calls=%fused_computation.9 | convolution fusion | flops 671154176 | bytes 6684672 | tf_op jit(solution)/shard_map/dot_general | solution.py:48
  321.8 0.8 copy.12
  (3 shorter events, 0.0 us)
Async XLA Ops:
  7.2 310.6 %copy-start = (bf16[128,5120]{1,0:T(8,128)(2,1)S(1)}, bf16[128,5120]{1,0:T(8,128)(2,1)}, u32[]{:S(2)}) copy-start(bf16[128,5120]{1,0:T(8,128)(2,1)} %param.5) | copy-start | bytes 3932164
  7.2 146.6 %all-gather.6.cloned.1.call-start = ((), (), s32[]{:S(2)}) async-start(), calls=%async_computation.1 | async-start | bytes 5324800 | tf_op jit(solution)/shard_map/all_gather | solution.py:45
  8.9 7.5 %copy-start.1 = (f32[2560,64]{1,0:T(8,128)}, f32[2560,64]{1,0:T(8,128)S(1)}, u32[]{:S(2)}) copy-start(f32[2560,64]{1,0:T(8,128)S(1)} %add.30) | copy-start | bytes 1966084
  8.9 1.0 copy-start.5
  16.5 301.3 %all-gather.4.cloned.1.call-start = ((), (), s32[]{:S(2)}) async-start(), calls=%async_computation | async-start | bytes 5570560 | tf_op jit(solution)/shard_map/all_gather | solution.py:50
  153.7 2.8 copy-start.4
  162.2 1.3 copy-start.3
  167.1 1.5 copy-start.2
Sparse Core Ops, SparseCore 0:
  16.6 137.0 all-gather.5
  167.3 150.4 all-gather.3
where the time goes:
time: 331 us; the launch traced here: 329 us
  waiting for transfers between devices  279 us (84%)
  between operations  14.1 us (4%)
  other arithmetic  13.7 us (4%)
  local copies, waits for them, and re-layouts  12.5 us (4%)
  matrix products  10.3 us (3%)
    all_gather x1, waiting for transfers between devices, body(): lax.all_gather(new_weight, 'fsdp', axis=0, tiled=True)  144 us
    all_gather x1, waiting for transfers between devices, body(): every_kept = lax.all_gather(kept[None], 'rep', axis=0, tiled=True)  135 us
  transfers between devices with their start and end apart: 2, of which 2 were waited for; matrix products, arithmetic and copies ran while one was open for 3% of the time, Pallas kernels for 0%

commit v1 on v0

v1 whole, which is shorter than its diff:
```python
import functools
import math

import jax
import jax.numpy as jnp
import numpy as np
from jax import lax
from jax.experimental import pallas as pl
from jax.experimental.pallas import tpu as pltpu
from jax.sharding import Mesh
from jax.sharding import PartitionSpec as P

GROUP = 64
KEEP = 8
LANES = 128
STACK = 4
HIGHEST = lax.Precision.HIGHEST
STEP = 0.01
DECAY = 0.1
AXES = ("x", "ylo", "core", "yhi", "z")
F32 = jnp.float32
BF16 = jnp.bfloat16
NT = (((1,), (1,)), ((), ()))
NN = (((1,), (0,)), ((), ()))
TN = (((0,), (0,)), ((), ()))


def basis_pair():
    k = np.arange(GROUP)[:, None]
    n = np.arange(GROUP)[None, :]
    scale = np.where(k == 0, math.sqrt(1.0 / GROUP), math.sqrt(2.0 / GROUP))
    table = scale * np.cos(np.pi * (n + 0.5) * k / GROUP)
    return np.kron(np.eye(2), table).astype(np.float32)


def call(kernel, out_shape, args, flops, **kw):
    size = sum(a.size * a.dtype.itemsize for a in args)
    return pl.pallas_call(
        kernel,
        out_shape=out_shape,
        compiler_params=pltpu.CompilerParams(vmem_limit_bytes=48 * 1024 * 1024),
        cost_estimate=pl.CostEstimate(flops=flops, bytes_accessed=size, transcendentals=0),
        **kw,
    )(*args)


def to_all(x, axes, parts):
    copies = lax.optimization_barrier(jnp.broadcast_to(x[None], (parts,) + x.shape))
    return lax.all_to_all(copies, axes, 0, 0, tiled=True)


def regroup(blocks, rows, target):
    fold = LANES // rows
    lane = lax.broadcasted_iota(jnp.int32, blocks[0].shape, 1) // rows
    merged = None
    for b in range(fold):
        moved = blocks[b]
        if b != target:
            moved = pltpu.roll(moved, ((b - target) % fold) * rows, axis=1)
        merged = moved if merged is None else jnp.where(lane == b, moved, merged)
    return merged


def local_kernel(cores, mom, grad, idx, b2, kept, idx_out, new_mom, kept_wide, idx_wide):
    rows = mom.shape[0]
    total_units = idx.shape[0] // KEEP
    units = total_units // cores
    deep = kept_wide.shape[1]
    table = b2[...]
    freq = lax.broadcasted_iota(jnp.int32, (GROUP, LANES), 0)
    kept_wide[...] = jnp.zeros_like(kept_wide)
    idx_wide[...] = jnp.zeros_like(idx_wide)
    for g in range(total_units // 2):
        tiles = []
        for t in range(STACK):
            cols = pl.ds((STACK * g + t) * LANES, LANES)
            tiles.append(0.9 * mom[:, cols] + grad[:, cols].astype(F32))
        block = jnp.concatenate(tiles, axis=0)
        spec = lax.dot_general(table, block, NT, precision=HIGHEST, preferred_element_type=F32)
        parts = []
        for c2 in range(2):
            whole = 2 * g + c2
            core, u = whole // units, whole % units
            half = spec[c2 * GROUP : (c2 + 1) * GROUP]
            sent = jnp.zeros_like(half)
            for j in range(KEEP):
                line = j * total_units + whole
                row = idx[line : line + 1, :]
                one = jnp.where(freq == row, half, 0.0)
                at = core * KEEP + j
                kept_wide[u % STACK, u // STACK, at : at + 1, :] = jnp.sum(one, axis=0, keepdims=True)
                idx_wide[u % STACK, u // STACK, at : at + 1, :] = row.astype(F32)
                sent = sent + one
            parts.append(sent)
        sent = lax.dot_general(jnp.concatenate(parts, axis=0), table, TN, precision=HIGHEST, preferred_element_type=F32)
        rest = block - sent
        for t in range(STACK):
            new_mom[:, pl.ds((STACK * g + t) * LANES, LANES)] = rest[t * rows : (t + 1) * rows]
    both = cores * KEEP
    for ur in range(deep):
        for t in range(STACK):
            lines = pl.ds(t * both * deep + ur, both, stride=deep)
            kept[lines, :] = regroup([kept_wide[b, ur] for b in range(STACK)], rows, t)
            idx_out[lines, :] = regroup([idx_wide[b, ur] for b in range(STACK)], rows, t)


def weight_kernel(tot, idx, b2, old, new, tot_wide, idx_wide):
    rows, width = old.shape
    deep = tot.shape[0] // (STACK * KEEP)
    span = KEEP * deep
    for source, wide in ((tot, tot_wide), (idx, idx_wide)):
        for b in range(STACK):
            wide[b] = regroup([source[t * span : (t + 1) * span, :] for t in range(STACK)], rows, b)
    freq = lax.broadcasted_iota(jnp.int32, (GROUP, LANES), 0)
    for g in range(width // (STACK * LANES)):
        parts = []
        for c2 in range(2):
            u = 2 * g + c2
            lines = pl.ds(u // STACK, KEEP, stride=deep)
            value = tot_wide[u % STACK, lines, :]
            where = idx_wide[u % STACK, lines, :].astype(jnp.int32)
            power = jnp.sum(value * value, axis=0, keepdims=True)
            value = value * lax.rsqrt(power / GROUP + 1e-06)
            spec = jnp.zeros((GROUP, LANES), F32)
            for j in range(KEEP):
                spec = jnp.where(freq == where[j : j + 1], value[j : j + 1], spec)
            parts.append(spec)
        direction = lax.dot_general(
            jnp.concatenate(parts, axis=0), b2[...], TN, precision=HIGHEST, preferred_element_type=F32
        )
        for t in range(STACK):
            cols = pl.ds((STACK * g + t) * LANES, LANES)
            kept_part = old[:, cols].astype(F32) * (1.0 - STEP * DECAY)
            new[:, cols] = (kept_part - STEP * direction[t * rows : (t + 1) * rows]).astype(BF16)


def tokens_kernel(mine, theirs, high, low, out):
    batch = mine.shape[0]
    for t in range(mine.shape[1] // LANES):
        cols = pl.ds(t * LANES, LANES)
        x = jnp.concatenate([mine[:, cols], theirs[:, cols]], axis=0)
        y = lax.dot_general(x, high[...], NT, preferred_element_type=F32)
        y = y + lax.dot_general(x, low[...], NT, preferred_element_type=F32)
        out[:, cols] = y.astype(BF16)


def direction_kernel(rows, units, both, tokens, out, vals, freqs, spec):
    shards = both.shape[0]
    lines = both.shape[1] // 2
    deep = lines // (STACK * KEEP)
    fold = LANES // rows
    for q in range(shards // fold):
        blocks = [both[fold * q + f].astype(F32) for f in range(fold)]
        for b in range(STACK):
            vals[b, q] = regroup([x[:lines] for x in blocks], rows, b)
            freqs[b, q] = regroup([x[lines:] for x in blocks], rows, b).astype(jnp.int32)
    freq = lax.broadcasted_iota(jnp.int32, (GROUP, LANES), 0)
    depth = 2 * STACK * GROUP
    for g in range(units // 2):
        slot = g % 2
        for t in range(STACK):
            for c2 in range(2):
                u = 2 * g + c2
                some = pl.ds(t * KEEP * deep + u // STACK, KEEP, stride=deep)
                for q in range(shards // fold):
                    cols = pl.ds(q * LANES, LANES)
                    value = vals[u % STACK, q, some, :]
                    where = freqs[u % STACK, q, some, :]
                    power = jnp.sum(value * value, axis=0, keepdims=True)
                    value = value * (lax.rsqrt(power / GROUP + 1e-06) * (-STEP))
                    s = jnp.zeros((GROUP, LANES), F32)
                    for j in range(KEEP):
                        s = jnp.where(freq == where[j : j + 1], value[j : j + 1], s)
                    spec[slot, pl.ds((2 * t + c2) * GROUP, GROUP), cols] = s.astype(BF16)
        y = lax.dot_general(tokens[:, pl.ds(g * depth, depth)], spec[slot], NN, preferred_element_type=F32)
        out[...] = y if g == 0 else out[...] + y


def old_kernel(shard_rows, mine, theirs, weight, change, own, other):
    nz, pair, width = weight.shape
    batch = mine.shape[0]
    step = 512
    x = [mine, theirs]
    y = [own, other]
    for p in range(2):
        acc = change[p * batch : (p + 1) * batch, :]
        for k in range(width // step):
            cols = pl.ds(k * step, step)
            w = jnp.concatenate(
                [weight[z, h * shard_rows : (h + 1) * shard_rows, cols] for h in range(pair // shard_rows) for z in range(nz)],
                axis=0,
            )
            part = lax.dot_general(x[p][:, cols], w, NT, preferred_element_type=F32)
            acc = acc + part * (1.0 - STEP * DECAY)
        y[p][...] = acc


def swap(x, axis):
    return lax.ppermute(x, axis, [(0, 1), (1, 0)])


def body(sizes, tokens, momentum, gradient, weight, kept_index):
    nx, nyl, nc, nyh, nz = sizes
    rows, width = weight.shape
    half = width // nc
    groups = width // (STACK * LANES)
    units = groups
    deep = -(-units // STACK)
    shards = nyh * nz
    batch = tokens.shape[0]
    pair = basis_pair()
    high = pair.astype(jnp.bfloat16)
    low = (pair - high.astype(np.float32)).astype(jnp.bfloat16)
    core = lax.axis_index("core")

    own = lax.dynamic_slice(weight, (0, core * half), (rows, half))
    far = swap(own, "yhi")
    first = lax.axis_index("yhi") == 0
    duo = jnp.concatenate([jnp.where(first, own, far), jnp.where(first, far, own)], axis=0)
    old_all = lax.all_gather(duo, "z", axis=0, tiled=False)

    mine = lax.dynamic_slice(tokens, (0, core * half), (batch, half))
    theirs = swap(lax.dynamic_slice(tokens, (0, (1 - core) * half), (batch, half)), "core")

    order = kept_index.reshape(rows, groups, STACK, 2, KEEP).transpose(4, 1, 3, 2, 0)
    lines = STACK * KEEP * deep
    kept, idx_all, new_momentum = call(
        functools.partial(local_kernel, nc),
        (
            jax.ShapeDtypeStruct((nc * lines, LANES), F32),
            jax.ShapeDtypeStruct((nc * lines, LANES), F32),
            jax.ShapeDtypeStruct((rows, width), F32),
        ),
        (momentum[0], gradient[0], order.reshape(KEEP * nc * units, LANES), jnp.asarray(pair)),
        flops=24 * rows * width * LANES,
        scratch_shapes=[pltpu.VMEM((STACK, deep, nc * KEEP, LANES), F32)] * 2,
    )
    idx_own = lax.dynamic_index_in_dim(idx_all.reshape(STACK, nc, KEEP * deep, LANES), core, 1, keepdims=False)
    idx_own = idx_own.reshape(lines, LANES)

    pieces = lax.all_to_all(kept.reshape(nyl * nc * nx, 1, deep * LANES), ("ylo", "core", "x"), 0, 0, tiled=True)
    total = to_all(jnp.sum(pieces, axis=0), ("ylo", "x"), nyl * nx).reshape(lines, LANES)
    both = to_all(jnp.concatenate([total.astype(BF16), idx_own.astype(BF16)], axis=0), ("yhi", "z"), shards)

    wide = pltpu.VMEM((STACK, KEEP * deep, LANES), F32)
    own_new = call(
        weight_kernel,
        jax.ShapeDtypeStruct((rows, half), BF16),
        (total, idx_own, jnp.asarray(pair), own),
        flops=12 * rows * half * LANES,
        scratch_shapes=[wide, wide],
    )
    other_new = swap(own_new, "core")
    left = core == 0
    new_weight = jnp.concatenate([jnp.where(left, own_new, other_new), jnp.where(left, other_new, own_new)], axis=1)

    turned = call(
        tokens_kernel,
        jax.ShapeDtypeStruct((nc * batch, half), BF16),
        (mine, theirs, jnp.asarray(high), jnp.asarray(low)),
        flops=4 * nc * batch * half * LANES,
    )
    change = call(
        functools.partial(direction_kernel, rows, units),
        jax.ShapeDtypeStruct((nc * batch, shards * rows), F32),
        (both, turned),
        flops=4 * nc * batch * half * shards * rows,
        scratch_shapes=[
            pltpu.VMEM((STACK, shards * rows // LANES, lines, LANES), F32),
            pltpu.VMEM((STACK, shards * rows // LANES, lines, LANES), jnp.int32),
            pltpu.VMEM((2, 2 * STACK * GROUP, shards * rows), BF16),
        ],
    )
    part = jax.ShapeDtypeStruct((batch, shards * rows), F32)
    here, there = call(
        functools.partial(old_kernel, rows),
        (part, part),
        (mine, theirs, old_all, change),
        flops=2 * nc * batch * half * shards * rows,
    )
    projected = (here + swap(there, "core")).astype(BF16)
    return new_weight, new_momentum[None], projected


def run(sizes, devices):
    fine = Mesh(devices.reshape(sizes), AXES)
    rep, fsdp = AXES[:3], AXES[3:]
    return jax.shard_map(
        functools.partial(body, sizes),
        mesh=fine,
        in_specs=(P(AXES, None), P(rep, fsdp, None), P(rep, fsdp, None), P(fsdp, None), P(fsdp, None, None)),
        out_specs=(P(fsdp, None), P(rep, fsdp, None), P(AXES, None)),
        check_vma=False,
    )


def solution(mesh):
    return run((8, 4, 2, 2, 8), mesh.devices)
```

time: 331 us -> 137 us (0.41)
  the two profiles are of different devices: /device:TPU:1 before, /device:TPU:17 now
where the time goes in v1:
time: 137 us; the launch traced here: 136 us
  starting transfers between devices  53.5 us (39%)
  waiting for transfers between devices  39.7 us (29%)
  Pallas kernels  16.3 us (12%)
  between operations  14.3 us (10%)
  local copies, waits for them, and re-layouts  8.13 us (6%)
  other arithmetic  4.05 us (3%)
    all_to_all x2, waiting for transfers between devices, to_all(): return lax.all_to_all(copies, axes, 0, 0, tiled=True)  22.7 us
    all_to_all x2, starting transfers between devices, to_all(): return lax.all_to_all(copies, axes, 0, 0, tiled=True)  21.5 us
    ppermute x4, starting transfers between devices, swap(): return lax.ppermute(x, axis, [(0, 1), (1, 0)])  16.9 us
    pallas_call x5, Pallas kernels, call(): pl.pallas_call(kernel, out_shape=out_shape, compiler_params=pltpu.Compile...  16.3 us
    all_to_all x1, starting transfers between devices, body(): lax.all_to_all(kept.reshape(nyl * nc * nx, 1, deep * LANES), ('ylo', 'cor...  15.1 us
    all_to_all x1, waiting for transfers between devices, body(): lax.all_to_all(kept.reshape(nyl * nc * nx, 1, deep * LANES), ('ylo', 'cor...  9.02 us
    ppermute x4, waiting for transfers between devices, swap(): return lax.ppermute(x, axis, [(0, 1), (1, 0)])  7.98 us
    unnamed x23, local copies, waits for them, and re-layouts  3.8 us
  transfers between devices with their start and end apart: 8, of which 6 were waited for; matrix products, arithmetic and copies ran while one was open for 4% of the time, Pallas kernels for 11%

profile of v1, /device:TPU:17, one launch (start us, length us, event | category | flops | bytes accessed | tf_op | source)
XLA Modules:
  0.0 135.9 jit_solution(8333485406451721319)
XLA Ops:
  7.2 0.0 copy-start.10
  7.2 0.0 all-gather.3.cloned.1.call-start
  7.2 0.9 constant_dynamic-slice_fusion.2.old
  8.2 7.0 %collective-permute-start.2 = (bf16[32,2560]{1,0:T(8,128)(2,1)S(1)}, bf16[32,2560]{1,0:T(8,128)(2,1)S(1)}, u32[]{:S(2)}, u32[]{:S(2)}) collective-permute-start(bf16[32,2560]{1,0:T(8,128)(2,1)S(1)} %constant_dynamic-slice_fusion.2.old), channel_id=1, source_target_pairs={{0,8},{8,0},{1,9},{9,1},{2,10},{10,2},{3,11},{11,3},{4,12},{12,4},... | collective-permute-start | bytes 491528 | tf_op jit(solution)/shard_map/ppermute | solution.py:199
  15.2 6.5 %collective-permute-done.2 = bf16[32,2560]{1,0:T(8,128)(2,1)S(1)} collective-permute-done((bf16[32,2560]{1,0:T(8,128)(2,1)S(1)}, bf16[32,2560]{1,0:T(8,128)(2,1)S(1)}, u32[]{:S(2)}, u32[]{:S(2)}) %collective-permute-start.2) | collective-permute-done | bytes 163872 | tf_op jit(solution)/shard_map/ppermute | solution.py:199
  21.7 1.0 broadcast_select_fusion.1
  22.7 0.0 copy-start.3
  22.7 0.0 copy-start.6
  22.7 0.0 copy-start.7
  22.7 0.7 pad_maximum_fusion.1
  23.5 0.0 all-gather.3.cloned.1.call-update
  23.5 0.0 copy-done.10
  23.5 0.2 copy.16
  23.7 0.1 copy.17
  23.8 0.2 reshape.32.idx
  24.0 0.0 copy-done.6
  24.0 0.0 copy-done.7
  24.0 6.5 %shard_map.103 = (f32[192,128]{1,0:T(8,128)}, f32[192,128]{1,0:T(8,128)S(1)}, f32[32,5120]{1,0:T(8,128)}) custom-call(f32[32,5120]{1,0:T(8,128)S(1)} %bitcast.19, bf16[32,5120]{1,0:T(8,128)(2,1)S(1)} %bitcast.20, s32[160,128]{1,0:T(8,128)S(1)} %reshape.32.idx, f32[128,128]{1,0:T(8,128)S(1)} %copy-done.3), custom_call_target="tpu_custom_call" | custom-call | flops 503316480 | bytes 1130496 | tf_op jit(solution)/shard_map/pallas_call | solution.py:38
  30.6 15.1 %all-to-all-start = ((f32[64,1,384]{2,1,0:T(1,128)}), f32[64,1,384]{2,1,0:T(1,128)S(1)}, u32[]{:S(2)}, u32[]{:S(2)}) async-start(f32[64,1,384]{2,1,0:T(1,128)} %bitcast.4), calls=%async_computation | async-start | bytes 196608 | tf_op jit(solution)/shard_map/all_to_all | solution.py:241
  45.7 9.0 %all-to-all-done = f32[64,1,384]{2,1,0:T(1,128)S(1)} async-done(((f32[64,1,384]{2,1,0:T(1,128)}), f32[64,1,384]{2,1,0:T(1,128)S(1)}, u32[]{:S(2)}, u32[]{:S(2)}) %all-to-all-start) | async-done | bytes 98336 | tf_op jit(solution)/shard_map/all_to_all | solution.py:241
  54.7 0.1 reduce_sum.9
  54.8 0.6 broadcast_in_dim.6
  55.4 4.2 %all-to-all-start.1 = ((f32[32,1,384]{2,1,0:T(1,128)}), f32[32,1,384]{2,1,0:T(1,128)S(1)}, u32[]{:S(2)}, u32[]{:S(2)}) async-start(f32[32,1,384]{2,1,0:T(1,128)} %broadcast_in_dim.6), calls=%async_computation.1 | async-start | bytes 98304 | tf_op jit(solution)/shard_map/all_to_all | solution.py:49
  59.7 8.3 %all-to-all-done.1 = f32[32,1,384]{2,1,0:T(1,128)S(1)} async-done(((f32[32,1,384]{2,1,0:T(1,128)}), f32[32,1,384]{2,1,0:T(1,128)S(1)}, u32[]{:S(2)}, u32[]{:S(2)}) %all-to-all-start.1) | async-done | bytes 49184 | tf_op jit(solution)/shard_map/all_to_all | solution.py:49
  67.9 1.0 broadcast_in_dim.8
  69.0 17.2 %all-to-all-start.2 = ((bf16[16,192,128]{2,1,0:T(8,128)(2,1)}), bf16[16,192,128]{2,1,0:T(8,128)(2,1)S(1)}, u32[]{:S(2)}, u32[]{:S(2)}) async-start(bf16[16,192,128]{2,1,0:T(8,128)(2,1)} %broadcast_in_dim.8), calls=%async_computation.2 | async-start | bytes 1572864 | tf_op jit(solution)/shard_map/all_to_all | solution.py:49
  86.2 0.8 shard_map.104
  87.0 0.0 copy-start.4
  87.0 0.0 copy-start.5
  87.0 4.7 %collective-permute-start = (bf16[32,2560]{1,0:T(8,128)(2,1)S(1)}, bf16[32,2560]{1,0:T(8,128)(2,1)S(1)}, u32[]{:S(2)}, u32[]{:S(2)}) collective-permute-start(bf16[32,2560]{1,0:T(8,128)(2,1)S(1)} %shard_map.104), channel_id=1, source_target_pairs={{0,16},{16,0},{1,17},{17,1},{2,18},{18,2},{3,19},{19,3},{4,20},{20... | collective-permute-start | bytes 491528 | tf_op jit(solution)/shard_map/ppermute | solution.py:199
  91.7 1.4 %constant_dynamic-slice_fusion = (bf16[128,2560]{1,0:T(8,128)(2,1)S(1)}, bf16[128,2560]{1,0:T(8,128)(2,1)S(1)}) fusion(bf16[128,5120]{1,0:T(8,128)(2,1)} %param.8, s32[]{:T(128)S(6)} %select_n.38, s32[]{:T(128)S(6)} %select_n.35), kind=kLoop, calls=%fused_computation.8 | loop fusion | bytes 2621448 | tf_op jit(solution)/shard_map/dynamic_slice | solution.py:223
  93.1 2.1 %collective-permute-start.1 = (bf16[128,2560]{1,0:T(8,128)(2,1)S(1)}, bf16[128,2560]{1,0:T(8,128)(2,1)S(1)}, u32[]{:S(2)}, u32[]{:S(2)}) collective-permute-start(bf16[128,2560]{1,0:T(8,128)(2,1)S(1)} %get-tuple-element.13), channel_id=1, source_target_pairs={{0,16},{16,0},{1,17},{17,1},{2,18},{18,2},{3,19},{19,3},{4,20},{20... | collective-permute-start | bytes 1966088 | tf_op jit(solution)/shard_map/ppermute | solution.py:199
  95.2 0.0 collective-permute-done
  95.2 0.8 broadcast_select_fusion.3
  96.0 1.1 collective-permute-done.1.theirs
  97.1 0.0 copy-done.5
  97.1 0.8 shard_map.105.tokens
  98.0 14.4 %all-to-all-done.2.both = bf16[16,192,128]{2,1,0:T(8,128)(2,1)S(1)} async-done(((bf16[16,192,128]{2,1,0:T(8,128)(2,1)}), bf16[16,192,128]{2,1,0:T(8,128)(2,1)S(1)}, u32[]{:S(2)}, u32[]{:S(2)}) %all-to-all-start.2) | async-done | bytes 786464 | tf_op jit(solution)/shard_map/all_to_all | solution.py:49
  112.4 6.3 %shard_map.106.change = f32[256,512]{1,0:T(8,128)S(1)} custom-call(bf16[16,192,128]{2,1,0:T(8,128)(2,1)S(1)} %all-to-all-done.2.both, bf16[256,2560]{1,0:T(8,128)(2,1)S(1)} %shard_map.105.tokens), custom_call_target="tpu_custom_call" | custom-call | flops 1342177280 | bytes 2097152 | tf_op jit(solution)/shard_map/pallas_call | solution.py:38
  118.7 0.8 copy-done.1
  119.5 1.7 %copy-done = bf16[512,2560]{1,0:T(8,128)(2,1)S(1)} copy-done((bf16[512,2560]{1,0:T(8,128)(2,1)S(1)}, bf16[512,2560]{1,0:T(8,128)(2,1)}, u32[]{:S(2)}) %copy-start) | copy-done | bytes 2621464
  121.3 1.0 copy-done.2
  122.3 1.8 %shard_map.107 = (f32[128,512]{1,0:T(8,128)S(1)}, f32[128,512]{1,0:T(8,128)S(1)}) custom-call(bf16[128,2560]{1,0:T(8,128)(2,1)S(1)} %get-tuple-element.14.mine, bf16[128,2560]{1,0:T(8,128)(2,1)S(1)} %collective-permute-done.1.theirs, bf16[8,64,2560]{2,1,0:T(8,128)(2,1)S(1)} %bitcast.14, f32[256,512]{1,0:T(8,128)S(1)} %copy-done.2), custom_call_target="tpu_custom_call" | custom-call | flops 671088640 | bytes 4456448 | tf_op jit(solution)/shard_map/pallas_call | solution.py:38
  124.1 3.1 %collective-permute-start.3 = (f32[128,512]{1,0:T(8,128)S(1)}, f32[128,512]{1,0:T(8,128)S(1)}, u32[]{:S(2)}, u32[]{:S(2)}) collective-permute-start(f32[128,512]{1,0:T(8,128)S(1)} %get-tuple-element.12), channel_id=1, source_target_pairs={{0,16},{16,0},{1,17},{17,1},{2,18},{18,2},{3,19},{19,3},{4,20},{20... | collective-permute-start | bytes 786440 | tf_op jit(solution)/shard_map/ppermute | solution.py:199
  127.3 0.0 copy-done.8
  127.3 0.7 pad_maximum_fusion
  128.0 0.4 collective-permute-done.3
  128.4 0.7 add_convert_fusion
  (13 shorter events, 0.0 us)
Async XLA Ops:
  7.2 16.3 %copy-start.10 = (s32[32,80,8]{1,2,0:T(8,128)S(1)}, s32[32,80,8]{1,2,0:T(8,128)}, u32[]{:S(2)}) copy-start(s32[32,80,8]{1,2,0:T(8,128)} %param.12) | copy-start | bytes 245764
  7.2 112.3 %all-gather.3.cloned.1.call-start = ((), (), s32[]{:S(2)}) async-start(), calls=%async_computation.3 | async-start | bytes 2949120 | tf_op jit(solution)/shard_map/all_gather | solution.py:220
  8.2 13.5 %collective-permute-start.2 = (bf16[32,2560]{1,0:T(8,128)(2,1)S(1)}, bf16[32,2560]{1,0:T(8,128)(2,1)S(1)}, u32[]{:S(2)}, u32[]{:S(2)}) collective-permute-start(bf16[32,2560]{1,0:T(8,128)(2,1)S(1)} %constant_dynamic-slice_fusion.2.old), channel_id=1, source_target_pairs={{0,8},{8,0},{1,9},{9,1},{2,10},{10,2},{3,11},{11,3},{4,12},{12,4},... | collective-permute-start | bytes 491528 | tf_op jit(solution)/shard_map/ppermute | solution.py:199
  22.7 1.3 copy-start.3
  22.7 1.3 copy-start.6
  22.7 1.3 copy-start.7
  30.6 24.1 %all-to-all-start = ((f32[64,1,384]{2,1,0:T(1,128)}), f32[64,1,384]{2,1,0:T(1,128)S(1)}, u32[]{:S(2)}, u32[]{:S(2)}) async-start(f32[64,1,384]{2,1,0:T(1,128)} %bitcast.4), calls=%async_computation | async-start | bytes 196608 | tf_op jit(solution)/shard_map/all_to_all | solution.py:241
  55.4 12.5 %all-to-all-start.1 = ((f32[32,1,384]{2,1,0:T(1,128)}), f32[32,1,384]{2,1,0:T(1,128)S(1)}, u32[]{:S(2)}, u32[]{:S(2)}) async-start(f32[32,1,384]{2,1,0:T(1,128)} %broadcast_in_dim.6), calls=%async_computation.1 | async-start | bytes 98304 | tf_op jit(solution)/shard_map/all_to_all | solution.py:49
  69.0 43.4 %all-to-all-start.2 = ((bf16[16,192,128]{2,1,0:T(8,128)(2,1)}), bf16[16,192,128]{2,1,0:T(8,128)(2,1)S(1)}, u32[]{:S(2)}, u32[]{:S(2)}) async-start(bf16[16,192,128]{2,1,0:T(8,128)(2,1)} %broadcast_in_dim.8), calls=%async_computation.2 | async-start | bytes 1572864 | tf_op jit(solution)/shard_map/all_to_all | solution.py:49
  87.0 10.1 %copy-start.4 = (bf16[128,128]{1,0:T(8,128)(2,1)S(1)}, bf16[128,128]{1,0:T(8,128)(2,1)}, u32[]{:S(2)}) copy-start(bf16[128,128]{1,0:T(8,128)(2,1)} %constant.32.clone.high) | copy-start | bytes 98308
  87.0 10.1 %copy-start.5 = (bf16[128,128]{1,0:T(8,128)(2,1)S(1)}, bf16[128,128]{1,0:T(8,128)(2,1)}, u32[]{:S(2)}) copy-start(bf16[128,128]{1,0:T(8,128)(2,1)} %constant.33.clone.low) | copy-start | bytes 98308
  87.0 8.2 %collective-permute-start = (bf16[32,2560]{1,0:T(8,128)(2,1)S(1)}, bf16[32,2560]{1,0:T(8,128)(2,1)S(1)}, u32[]{:S(2)}, u32[]{:S(2)}) collective-permute-start(bf16[32,2560]{1,0:T(8,128)(2,1)S(1)} %shard_map.104), channel_id=1, source_target_pairs={{0,16},{16,0},{1,17},{17,1},{2,18},{18,2},{3,19},{19,3},{4,20},{20... | collective-permute-start | bytes 491528 | tf_op jit(solution)/shard_map/ppermute | solution.py:199
  93.1 4.0 %collective-permute-start.1 = (bf16[128,2560]{1,0:T(8,128)(2,1)S(1)}, bf16[128,2560]{1,0:T(8,128)(2,1)S(1)}, u32[]{:S(2)}, u32[]{:S(2)}) collective-permute-start(bf16[128,2560]{1,0:T(8,128)(2,1)S(1)} %get-tuple-element.13), channel_id=1, source_target_pairs={{0,16},{16,0},{1,17},{17,1},{2,18},{18,2},{3,19},{19,3},{4,20},{20... | collective-permute-start | bytes 1966088 | tf_op jit(solution)/shard_map/ppermute | solution.py:199
  118.7 0.8 copy-start.1
  119.5 1.7 %copy-start = (bf16[512,2560]{1,0:T(8,128)(2,1)S(1)}, bf16[512,2560]{1,0:T(8,128)(2,1)}, u32[]{:S(2)}) copy-start(bf16[512,2560]{1,0:T(8,128)(2,1)} %all-gather.3.cloned.1.call-done) | copy-start | bytes 7864324
  121.2 1.0 copy-start.2
  122.3 5.0 %copy-start.8 = (bf16[32,2560]{1,0:T(8,128)(2,1)S(1)}, bf16[32,2560]{1,0:T(8,128)(2,1)}, u32[]{:S(2)}) copy-start(bf16[32,2560]{1,0:T(8,128)(2,1)} %get-tuple-element.17) | copy-start | bytes 491524
  122.3 5.0 %copy-start.9 = (bf16[32,2560]{1,0:T(8,128)(2,1)S(1)}, bf16[32,2560]{1,0:T(8,128)(2,1)}, u32[]{:S(2)}) copy-start(bf16[32,2560]{1,0:T(8,128)(2,1)} %get-tuple-element.18) | copy-start | bytes 491524
  124.1 4.3 %collective-permute-start.3 = (f32[128,512]{1,0:T(8,128)S(1)}, f32[128,512]{1,0:T(8,128)S(1)}, u32[]{:S(2)}, u32[]{:S(2)}) collective-permute-start(f32[128,512]{1,0:T(8,128)S(1)} %get-tuple-element.12), channel_id=1, source_target_pairs={{0,16},{16,0},{1,17},{17,1},{2,18},{18,2},{3,19},{19,3},{4,20},{20... | collective-permute-start | bytes 786440 | tf_op jit(solution)/shard_map/ppermute | solution.py:199
Sparse Core Ops, SparseCore 0:
  23.6 59.1 all-gather.2

commit v2 on v1

v2 whole, which is shorter than its diff:
```python
import functools
import math

import jax
import jax.numpy as jnp
import numpy as np
from jax import lax
from jax.experimental import pallas as pl
from jax.experimental.pallas import tpu as pltpu
from jax.sharding import Mesh
from jax.sharding import PartitionSpec as P

GROUP = 64
KEEP = 8
LANES = 128
STACK = 4
HIGHEST = lax.Precision.HIGHEST
STEP = 0.01
DECAY = 0.1
AXES = ("x", "ylo", "core", "yhi", "z")
F32 = jnp.float32
BF16 = jnp.bfloat16
NT = (((1,), (1,)), ((), ()))
NN = (((1,), (0,)), ((), ()))
TN = (((0,), (0,)), ((), ()))


def basis_pair():
    k = np.arange(GROUP)[:, None]
    n = np.arange(GROUP)[None, :]
    scale = np.where(k == 0, math.sqrt(1.0 / GROUP), math.sqrt(2.0 / GROUP))
    table = scale * np.cos(np.pi * (n + 0.5) * k / GROUP)
    return np.kron(np.eye(2), table).astype(np.float32)


def call(kernel, out_shape, args, flops, vmem=12, **kw):
    size = sum(a.size * a.dtype.itemsize for a in args)
    return pl.pallas_call(
        kernel,
        out_shape=out_shape,
        compiler_params=pltpu.CompilerParams(vmem_limit_bytes=vmem * 1024 * 1024),
        cost_estimate=pl.CostEstimate(flops=flops, bytes_accessed=size, transcendentals=0),
        **kw,
    )(*args)


def to_all(x, axes, parts):
    copies = lax.optimization_barrier(jnp.broadcast_to(x[None], (parts,) + x.shape))
    return lax.all_to_all(copies, axes, 0, 0, tiled=True)


def pick(sources, rows):
    lane = lax.broadcasted_iota(jnp.int32, sources[0][0].shape, 1) // rows
    merged = None
    for s, (block, group) in enumerate(sources):
        moved = block
        if group != s:
            moved = pltpu.roll(block, ((s - group) % len(sources)) * rows, axis=1)
        merged = moved if merged is None else jnp.where(lane == s, moved, merged)
    return merged


def regroup(blocks, rows, target):
    return pick([(block, target) for block in blocks], rows)


def split(x, axis, order):
    high = x.astype(BF16)
    low = (x - high.astype(F32)).astype(BF16)
    return jnp.concatenate([high, low, high] if order else [high, high, low], axis=axis)


def index_kernel(units, core, idx, out):
    total_units = idx.shape[0] // KEEP
    rows = LANES // STACK
    block = [idx[pl.ds(core[0] * units + u, KEEP, stride=total_units), :].astype(F32) for u in range(units)]
    full = units // STACK
    parts = []
    for r in range(full):
        for t in range(STACK):
            parts.append(regroup(block[r * STACK : (r + 1) * STACK], rows, t))
    if full * STACK < units:
        for t in range(0, STACK, 2):
            parts.append(pick([(block[full * STACK + s % 2], t + s // 2) for s in range(STACK)], rows))
    out[...] = jnp.concatenate(parts, axis=0).astype(BF16)


def join_kernel(own, far, own_idx, far_idx, out):
    rows, width = own.shape
    tiles = width // LANES
    size = out.shape[0] // 2
    for h, (weight, idx) in enumerate(((own, own_idx), (far, far_idx))):
        for c in range(tiles):
            out[h * size + c * rows : h * size + (c + 1) * rows, :] = weight[:, c * LANES : (c + 1) * LANES]
        out[h * size + tiles * rows : (h + 1) * size, :] = idx[...]


def local_kernel(cores, mom, grad, idx, b2, kept, new_mom, kept_wide):
    rows = mom.shape[0]
    total_units = idx.shape[0] // KEEP
    units = total_units // cores
    deep = kept_wide.shape[1]
    forward = split(b2[...], 1, False)
    back = split(b2[...], 0, False)
    freq = lax.broadcasted_iota(jnp.int32, (GROUP, LANES), 0)
    kept_wide[...] = jnp.zeros_like(kept_wide)
    for g in range(total_units // 2):
        tiles = []
        for t in range(STACK):
            cols = pl.ds((STACK * g + t) * LANES, LANES)
            tiles.append(0.9 * mom[:, cols] + grad[:, cols].astype(F32))
        block = jnp.concatenate(tiles, axis=0)
        spec = lax.dot_general(forward, split(block, 1, True), NT, preferred_element_type=F32)
        parts = []
        for c2 in range(2):
            whole = 2 * g + c2
            core, u = whole // units, whole % units
            half = spec[c2 * GROUP : (c2 + 1) * GROUP]
            sent = jnp.zeros_like(half)
            for j in range(KEEP):
                line = j * total_units + whole
                one = jnp.where(freq == idx[line : line + 1, :], half, 0.0)
                at = core * KEEP + j
                kept_wide[u % STACK, u // STACK, at : at + 1, :] = jnp.sum(one, axis=0, keepdims=True)
                sent = sent + one
            parts.append(sent)
        sent = lax.dot_general(split(jnp.concatenate(parts, axis=0), 0, True), back, TN, preferred_element_type=F32)
        rest = block - sent
        for t in range(STACK):
            new_mom[:, pl.ds((STACK * g + t) * LANES, LANES)] = rest[t * rows : (t + 1) * rows]
    both = cores * KEEP
    for ur in range(deep):
        for t in range(STACK):
            lines = pl.ds(t * both * deep + ur, both, stride=deep)
            kept[lines, :] = regroup([kept_wide[b, ur] for b in range(STACK)], rows, t)


def weight_kernel(core, tot, idx, b2, old, new, tot_wide):
    rows, width = old.shape
    deep = tot.shape[0] // (STACK * KEEP)
    span = KEEP * deep
    total_units = idx.shape[0] // KEEP
    units = 2 * width // (STACK * LANES)
    for b in range(STACK):
        tot_wide[b] = regroup([tot[t * span : (t + 1) * span, :] for t in range(STACK)], rows, b)
    freq = lax.broadcasted_iota(jnp.int32, (GROUP, LANES), 0)
    for g in range(units // 2):
        parts = []
        for c2 in range(2):
            u = 2 * g + c2
            value = tot_wide[u % STACK, pl.ds(u // STACK, KEEP, stride=deep), :]
            where = idx[pl.ds(core[0] * units + u, KEEP, stride=total_units), :]
            power = jnp.sum(value * value, axis=0, keepdims=True)
            value = value * lax.rsqrt(power / GROUP + 1e-06)
            spec = jnp.zeros((GROUP, LANES), F32)
            for j in range(KEEP):
                spec = jnp.where(freq == where[j : j + 1], value[j : j + 1], spec)
            parts.append(spec)
        direction = lax.dot_general(
            jnp.concatenate(parts, axis=0), b2[...], TN, precision=HIGHEST, preferred_element_type=F32
        )
        for t in range(STACK):
            cols = pl.ds((STACK * g + t) * LANES, LANES)
            kept_part = old[:, cols].astype(F32) * (1.0 - STEP * DECAY)
            new[:, cols] = (kept_part - STEP * direction[t * rows : (t + 1) * rows]).astype(BF16)


def tokens_kernel(mine, theirs, high, low, out):
    batch = mine.shape[0]
    for t in range(mine.shape[1] // LANES):
        cols = pl.ds(t * LANES, LANES)
        x = jnp.concatenate([mine[:, cols], theirs[:, cols]], axis=0)
        y = lax.dot_general(x, high[...], NT, preferred_element_type=F32)
        y = y + lax.dot_general(x, low[...], NT, preferred_element_type=F32)
        out[:, cols] = y.astype(BF16)


def pack_kernel(units, tot, out):
    deep = tot.shape[0] // (STACK * KEEP)
    full = units // STACK
    lane = lax.broadcasted_iota(jnp.int32, (KEEP, LANES), 1)
    blocks = [[tot[pl.ds(t * KEEP * deep + r, KEEP, stride=deep), :] for t in range(STACK)] for r in range(deep)]
    parts = []
    for r in range(full):
        parts += blocks[r]
    if full < deep:
        for t in range(0, STACK, 2):
            upper = pltpu.roll(blocks[full][t + 1], LANES // 2, axis=1)
            parts.append(jnp.where(lane < LANES // 2, blocks[full][t], upper))
    packed = jnp.concatenate(parts, axis=0).astype(BF16)
    for f in range(out.shape[0]):
        out[f] = packed


def product_kernel(rows, units, place, sums, tokens, mine, theirs, source, own, other, weight, vals, freqs, spec, sems):
    shards, lines, _ = sums.shape
    nz, size, _ = source.shape
    size = size // 2
    steps = units // 2
    high = STACK * rows
    fold = LANES // rows
    full = units // STACK

    def copy(h, k):
        at = h * size + (steps * high if k == steps else k * high)
        part = pl.ds(at, lines if k == steps else high)
        return pltpu.make_async_copy(source.at[:, part, :], weight.at[:, part, :], sems.at[h, k])

    for k in [steps] + list(range(steps)):
        for h in range(2):
            copy(h, k).start()

    def start_of(y):
        h = place[0] if y == 0 else 1 - place[0]
        return h * size

    def spread(blocks, out, q):
        for b in range(STACK):
            out[b, q] = regroup(blocks, rows, b)

    for q in range(shards // fold):
        spread([sums[fold * q + f].astype(F32) for f in range(fold)], vals, q)
    for h in range(2):
        copy(h, steps).wait()
    for q in range(shards // fold):
        blocks = []
        for f in range(fold * q, fold * (q + 1)):
            at = pl.multiple_of(start_of(f // nz) + steps * high, 16)
            blocks.append(weight[f % nz, pl.ds(at, lines), :].astype(F32))
        spread(blocks, freqs, q)
    pack = 16
    freq = lax.broadcasted_iota(jnp.int32, (GROUP, LANES), 0).astype(F32).astype(BF16)
    freq = [freq[k * pack : (k + 1) * pack] for k in range(GROUP // pack)]
    depth = 2 * STACK * GROUP
    batch = mine.shape[0]
    wide = nz * rows
    for g in range(steps):
        slot = g % 2
        for t in range(STACK):
            for c2 in range(2):
                u = 2 * g + c2
                if u // STACK < full:
                    lane, line = u % STACK, (u // STACK * STACK + t) * KEEP
                else:
                    lane, line = 2 * (t % 2) + u % STACK, (full * STACK + t // 2) * KEEP
                for q in range(shards // fold):
                    cols = pl.ds(q * LANES, LANES)
                    value = vals[lane, q, line : line + KEEP, :]
                    where = freqs[lane, q, line : line + KEEP, :]
                    power = jnp.sum(value * value, axis=0, keepdims=True)
                    value = value * (lax.rsqrt(power / GROUP + 1e-06) * (-STEP))
                    s = [jnp.zeros((pack, LANES), BF16)] * len(freq)
                    for j in range(KEEP):
                        v = jnp.broadcast_to(value[j : j + 1], (pack, LANES)).astype(BF16)
                        w = jnp.broadcast_to(where[j : j + 1], (pack, LANES)).astype(BF16)
                        s = [jnp.where(f == w, v, old) for f, old in zip(freq, s)]
                    spec[slot, pl.ds((2 * t + c2) * GROUP, GROUP), cols] = jnp.concatenate(s, axis=0)
        for h in range(2):
            copy(h, g).wait()
        cols = pl.ds(g * depth, depth)
        for y in range(2):
            at = start_of(y) + g * high
            tiles = []
            for c in range(STACK):
                line = pl.multiple_of(at + c * rows, 16)
                tiles.append(jnp.concatenate([weight[z, pl.ds(line, rows), :] for z in range(nz)], axis=0))
            w = jnp.concatenate(tiles, axis=1)
            lanes = pl.ds(y * wide, wide)
            for p, (x, out) in enumerate(((mine, own), (theirs, other))):
                part = lax.dot_general(x[:, cols], w, NT, preferred_element_type=F32) * (1.0 - STEP * DECAY)
                part += lax.dot_general(
                    tokens[p * batch : (p + 1) * batch, cols], spec[slot, :, lanes], NN, preferred_element_type=F32
                )
                out[:, lanes] = part if g == 0 else out[:, lanes] + part


def swap(x, axis):
    return lax.ppermute(x, axis, [(0, 1), (1, 0)])


def body(sizes, tokens, momentum, gradient, weight, kept_index):
    nx, nyl, nc, nyh, nz = sizes
    rows, width = weight.shape
    half = width // nc
    groups = width // (STACK * LANES)
    units = groups
    deep = -(-units // STACK)
    shards = nyh * nz
    batch = tokens.shape[0]
    pair = basis_pair()
    high = pair.astype(jnp.bfloat16)
    low = (pair - high.astype(np.float32)).astype(jnp.bfloat16)
    core = lax.axis_index("core")

    own = lax.dynamic_slice(weight, (0, core * half), (rows, half))
    far = swap(own, "yhi")
    order = kept_index.reshape(rows, groups, STACK, 2, KEEP).transpose(4, 1, 3, 2, 0).reshape(KEEP * nc * units, LANES)
    smem = pl.BlockSpec(memory_space=pltpu.SMEM)
    vmem = pl.BlockSpec(memory_space=pltpu.VMEM)
    core_ref = core.reshape(1)
    idx_own = call(
        functools.partial(index_kernel, units),
        jax.ShapeDtypeStruct((KEEP * units, LANES), BF16),
        (core_ref, order),
        flops=1000,
        in_specs=[smem, vmem],
    )
    idx_far = swap(idx_own, "yhi")
    lines = STACK * KEEP * deep
    kept, new_momentum = call(
        functools.partial(local_kernel, nc),
        (
            jax.ShapeDtypeStruct((nc * lines, LANES), F32),
            jax.ShapeDtypeStruct((rows, width), F32),
        ),
        (momentum[0], gradient[0], order, jnp.asarray(pair)),
        flops=12 * rows * width * LANES,
        scratch_shapes=[pltpu.VMEM((STACK, deep, nc * KEEP, LANES), F32)],
    )
    far, idx_far, kept = lax.optimization_barrier((far, idx_far, kept))
    size = half // LANES * rows + KEEP * units
    duo = call(
        join_kernel,
        jax.ShapeDtypeStruct((2 * size, LANES), BF16),
        (own, far, idx_own, idx_far),
        flops=1000,
    )
    duo, kept = lax.optimization_barrier((duo, kept))
    old_all = lax.all_gather(duo, "z", axis=0, tiled=False)

    pieces = lax.all_to_all(kept.reshape(nyl * nc * nx, 1, deep * LANES), ("ylo", "core", "x"), 0, 0, tiled=True)
    total = to_all(jnp.sum(pieces, axis=0), ("ylo", "x"), nyl * nx).reshape(lines, LANES)
    copies = call(
        functools.partial(pack_kernel, units),
        jax.ShapeDtypeStruct((shards, KEEP * units, LANES), BF16),
        (total,),
        flops=1000,
    )
    sums = lax.all_to_all(copies, ("yhi", "z"), 0, 0, tiled=True)

    mine = lax.dynamic_slice(tokens, (0, core * half), (batch, half))
    theirs = swap(lax.dynamic_slice(tokens, (0, (1 - core) * half), (batch, half)), "core")

    own_new = call(
        weight_kernel,
        jax.ShapeDtypeStruct((rows, half), BF16),
        (core_ref, total, order, jnp.asarray(pair), own),
        flops=12 * rows * half * LANES,
        in_specs=[smem, vmem, vmem, vmem, vmem],
        scratch_shapes=[pltpu.VMEM((STACK, KEEP * deep, LANES), F32)],
    )
    other_new = swap(own_new, "core")
    left = core == 0
    new_weight = jnp.concatenate([jnp.where(left, own_new, other_new), jnp.where(left, other_new, own_new)], axis=1)

    turned = call(
        tokens_kernel,
        jax.ShapeDtypeStruct((nc * batch, half), BF16),
        (mine, theirs, jnp.asarray(high), jnp.asarray(low)),
        flops=4 * nc * batch * half * LANES,
    )
    out_width = shards * rows
    part = jax.ShapeDtypeStruct((batch, out_width), F32)
    table = pltpu.VMEM((STACK, out_width // LANES, KEEP * units, LANES), F32)
    here, there = call(
        functools.partial(product_kernel, rows, units),
        (part, part),
        (lax.axis_index("yhi").reshape(1), sums, turned, mine, theirs, old_all),
        flops=6 * nc * batch * half * out_width,
        vmem=20,
        in_specs=[smem, vmem, vmem, vmem, vmem, pl.BlockSpec(memory_space=pl.ANY)],
        scratch_shapes=[
            pltpu.VMEM((nz, 2 * size, LANES), BF16),
            table,
            table,
            pltpu.VMEM((2, 2 * STACK * GROUP, out_width), BF16),
            pltpu.SemaphoreType.DMA((2, units // 2 + 1)),
        ],
    )
    projected = (here + swap(there, "core")).astype(BF16)
    return new_weight, new_momentum[None], projected


def run(sizes, devices):
    fine = Mesh(devices.reshape(sizes), AXES)
    rep, fsdp = AXES[:3], AXES[3:]
    return jax.shard_map(
        functools.partial(body, sizes),
        mesh=fine,
        in_specs=(P(AXES, None), P(rep, fsdp, None), P(rep, fsdp, None), P(fsdp, None), P(fsdp, None, None)),
        out_specs=(P(fsdp, None), P(rep, fsdp, None), P(AXES, None)),
        check_vma=False,
    )


def solution(mesh):
    return run((8, 4, 2, 2, 8), mesh.devices)
```

time: 137 us -> 122 us (0.89)
  the two profiles are of different devices: /device:TPU:17 before, /device:TPU:1 now
where the time goes in v2:
time: 122 us; the launch traced here: 121 us
  starting transfers between devices  40.4 us (33%)
  blocking collectives  23.3 us (19%)
  waiting for transfers between devices  22.2 us (18%)
  between operations  14.3 us (12%)
  Pallas kernels  13 us (11%)
  local copies, waits for them, and re-layouts  4.91 us (4%)
  other arithmetic  3.15 us (3%)
    all_to_all x1, blocking collectives, body(): lax.all_to_all(kept.reshape(nyl * nc * nx, 1, deep * LANES), ('ylo', 'cor...  23.3 us
    ppermute x5, starting transfers between devices, swap(): return lax.ppermute(x, axis, [(0, 1), (1, 0)])  22.1 us
    all_to_all x1, starting transfers between devices, body(): sums = lax.all_to_all(copies, ('yhi', 'z'), 0, 0, tiled=True)  14.4 us
    pallas_call x7, Pallas kernels, call(): pl.pallas_call(kernel, out_shape=out_shape, compiler_params=pltpu.Compile...  13 us
    all_to_all x1, waiting for transfers between devices, body(): sums = lax.all_to_all(copies, ('yhi', 'z'), 0, 0, tiled=True)  9.74 us
    all_to_all x1, waiting for transfers between devices, to_all(): return lax.all_to_all(copies, axes, 0, 0, tiled=True)  9.15 us
    all_to_all x1, starting transfers between devices, to_all(): return lax.all_to_all(copies, axes, 0, 0, tiled=True)  3.86 us
    unnamed x19, local copies, waits for them, and re-layouts  3.84 us
  transfers between devices with their start and end apart: 8, of which 4 were waited for; matrix products, arithmetic and copies ran while one was open for 4% of the time, Pallas kernels for 5%

profile of v2, /device:TPU:1, one launch (start us, length us, event | category | flops | bytes accessed | tf_op | source)
XLA Modules:
  0.0 121.2 jit_solution(17895041307402363135)
XLA Ops:
  7.2 0.0 copy-start
  7.2 0.0 copy-start.3
  7.2 0.0 copy-start.1
  7.2 0.0 copy-start.2
  7.2 0.0 all-gather.3.cloned.1.call-start
  7.3 0.9 copy-done
  8.2 8.7 %collective-permute-start = (bf16[32,2560]{1,0:T(8,128)(2,1)S(1)}, bf16[32,2560]{1,0:T(8,128)(2,1)S(1)}, u32[]{:S(2)}, u32[]{:S(2)}) collective-permute-start(bf16[32,2560]{1,0:T(8,128)(2,1)S(1)} %constant_dynamic-slice_fusion.2.own.old), channel_id=1, source_target_pairs={{0,8},{8,0},{1,9},{9,1},{2,10},{10,2},{3,11},{11,3},{4,12},{12,4},... | collective-permute-start | bytes 491528 | tf_op jit(solution)/shard_map/ppermute | solution.py:278
  16.9 1.1 copy.14
  18.0 0.1 copy.15
  18.1 0.2 reshape.31.idx
  18.3 0.1 shard_map.103.own_idx
  18.4 1.9 %collective-permute-start.1 = (bf16[80,128]{1,0:T(8,128)(2,1)S(1)}, bf16[80,128]{1,0:T(8,128)(2,1)S(1)}, u32[]{:S(2)}, u32[]{:S(2)}) collective-permute-start(bf16[80,128]{1,0:T(8,128)(2,1)S(1)} %shard_map.103.own_idx), channel_id=1, source_target_pairs={{0,8},{8,0},{1,9},{9,1},{2,10},{10,2},{3,11},{11,3},{4,12},{12,4},... | collective-permute-start | bytes 61448 | tf_op jit(solution)/shard_map/ppermute | solution.py:278
  20.3 0.0 copy-done.3
  20.3 0.0 copy-done.1
  20.4 0.0 copy-done.2
  20.4 4.0 %shard_map.104 = (f32[192,128]{1,0:T(8,128)S(1)}, f32[32,5120]{1,0:T(8,128)}) custom-call(f32[32,5120]{1,0:T(8,128)S(1)} %bitcast.11, bf16[32,5120]{1,0:T(8,128)(2,1)S(1)} %bitcast.14, s32[160,128]{1,0:T(8,128)S(1)} %reshape.31.idx, f32[128,128]{1,0:T(8,128)S(1)} %copy-done.3), custom_call_target="tpu_custom_call" | custom-call | flops 251658240 | bytes 1130496 | tf_op jit(solution)/shard_map/pallas_call | solution.py:38
  24.3 2.9 %collective-permute-done.1.far_idx = bf16[80,128]{1,0:T(8,128)(2,1)S(1)} collective-permute-done((bf16[80,128]{1,0:T(8,128)(2,1)S(1)}, bf16[80,128]{1,0:T(8,128)(2,1)S(1)}, u32[]{:S(2)}, u32[]{:S(2)}) %collective-permute-start.1) | collective-permute-done | bytes 20512 | tf_op jit(solution)/shard_map/ppermute | solution.py:278
  27.2 0.0 collective-permute-done.far
  27.2 0.8 shard_map.105
  28.0 0.0 all-gather.3.cloned.1.call-update
  28.0 23.3 %all_to_all.15 = f32[64,1,384]{2,1,0:T(1,128)S(1)} all-to-all(f32[64,1,384]{2,1,0:T(1,128)S(1)} %bitcast.15), channel_id=1, replica_groups=mesh['x'=8,'ylo'=4,'core'=2,'yhi'=2,'z'=8] {'ylo','core','x'}, dimensions={0} | all-to-all | bytes 196608 | tf_op jit(solution)/shard_map/all_to_all | solution.py:331
  51.4 0.1 reduce_sum.9
  51.5 0.6 broadcast_in_dim.4
  52.1 3.9 %all-to-all-start.1 = ((f32[32,1,384]{2,1,0:T(1,128)}), f32[32,1,384]{2,1,0:T(1,128)S(1)}, u32[]{:S(2)}, u32[]{:S(2)}) async-start(f32[32,1,384]{2,1,0:T(1,128)} %broadcast_in_dim.4), calls=%async_computation.1 | async-start | bytes 98304 | tf_op jit(solution)/shard_map/all_to_all | solution.py:49
  56.0 9.1 %all-to-all-done.1 = f32[32,1,384]{2,1,0:T(1,128)S(1)} async-done(((f32[32,1,384]{2,1,0:T(1,128)}), f32[32,1,384]{2,1,0:T(1,128)S(1)}, u32[]{:S(2)}, u32[]{:S(2)}) %all-to-all-start.1) | async-done | bytes 49184 | tf_op jit(solution)/shard_map/all_to_all | solution.py:49
  65.1 0.8 shard_map.106
  66.0 4.4 %collective-permute-start.2 = (bf16[32,2560]{1,0:T(8,128)(2,1)S(1)}, bf16[32,2560]{1,0:T(8,128)(2,1)}, u32[]{:S(2)}, u32[]{:S(2)}) collective-permute-start(bf16[32,2560]{1,0:T(8,128)(2,1)S(1)} %shard_map.106), channel_id=1, source_target_pairs={{0,16},{16,0},{1,17},{17,1},{2,18},{18,2},{3,19},{19,3},{4,20},{20... | collective-permute-start | bytes 491528 | tf_op jit(solution)/shard_map/ppermute | solution.py:278
  70.3 0.0 copy-done.7
  70.4 0.1 constant_dynamic-slice_fusion
  70.5 0.0 copy-start.4
  70.5 0.0 copy-start.5
  70.5 1.9 %collective-permute-start.3 = (bf16[128,2560]{1,0:T(8,128)(2,1)S(1)}, bf16[128,2560]{1,0:T(8,128)(2,1)S(1)}, u32[]{:S(2)}, u32[]{:S(2)}) collective-permute-start(bf16[128,2560]{1,0:T(8,128)(2,1)S(1)} %get-tuple-element.21), channel_id=1, source_target_pairs={{0,16},{16,0},{1,17},{17,1},{2,18},{18,2},{3,19},{19,3},{4,20},{20... | collective-permute-start | bytes 1966088 | tf_op jit(solution)/shard_map/ppermute | solution.py:278
  72.4 0.8 shard_map.107
  73.2 14.4 %all-to-all-start.2 = ((bf16[16,80,128]{2,1,0:T(8,128)(2,1)}), bf16[16,80,128]{2,1,0:T(8,128)(2,1)S(1)}, u32[]{:S(2)}, u32[]{:S(2)}) async-start(bf16[16,80,128]{2,1,0:T(8,128)(2,1)} %shard_map.107), calls=%async_computation.2 | async-start | bytes 655360 | tf_op jit(solution)/shard_map/all_to_all | solution.py:339
  87.7 0.0 collective-permute-done.2
  87.7 1.6 %broadcast_select_fusion.1 = (bf16[32,2560]{1,0:T(8,128)(2,1)S(1)}, bf16[32,2560]{1,0:T(8,128)(2,1)}) fusion(bf16[32,2560]{1,0:T(8,128)(2,1)S(1)} %shard_map.106, bf16[32,2560]{1,0:T(8,128)(2,1)} %collective-permute-done.2, pred[]{:T(512)S(6)} %eq.3), kind=kLoop, calls=%fused_computation.3 | loop fusion | flops 163840 | bytes 655361 | tf_op jit(solution)/shard_map/jit(_where)/select_n | solution.py:354
  89.3 0.0 collective-permute-done.3.theirs
  89.3 0.0 copy-done.4
  89.3 0.0 copy-done.5
  89.3 0.8 shard_map.108.tokens
  90.1 9.7 %all-to-all-done.2.sums = bf16[16,80,128]{2,1,0:T(8,128)(2,1)S(1)} async-done(((bf16[16,80,128]{2,1,0:T(8,128)(2,1)}), bf16[16,80,128]{2,1,0:T(8,128)(2,1)S(1)}, u32[]{:S(2)}, u32[]{:S(2)}) %all-to-all-start.2) | async-done | bytes 327712 | tf_op jit(solution)/shard_map/all_to_all | solution.py:339
  99.9 1.8 %copy-done.6 = bf16[11520,128]{1,0:T(8,128)(2,1)S(1)} copy-done((bf16[11520,128]{1,0:T(8,128)(2,1)S(1)}, bf16[11520,128]{1,0:T(8,128)(2,1)}, u32[]{:S(2)}) %copy-start.6) | copy-done | bytes 2949144
  101.7 5.7 %shard_map.109 = (f32[128,512]{1,0:T(8,128)S(1)}, f32[128,512]{1,0:T(8,128)S(1)}) custom-call(s32[1]{0:T(128)} %bitcast.8.place, bf16[16,80,128]{2,1,0:T(8,128)(2,1)S(1)} %all-to-all-done.2.sums, bf16[256,2560]{1,0:T(8,128)(2,1)S(1)} %shard_map.108.tokens, bf16[128,2560]{1,0:T(8,128)(2,1)S(1)} %get-tuple-element.22.mine, ...), custom_call_target="tpu_custom_call" | custom-call | flops 2013265920 | bytes 5898244 | tf_op jit(solution)/shard_map/pallas_call | solution.py:38
  107.4 5.1 %collective-permute-start.4 = (f32[128,512]{1,0:T(8,128)S(1)}, f32[128,512]{1,0:T(8,128)S(1)}, u32[]{:S(2)}, u32[]{:S(2)}) collective-permute-start(f32[128,512]{1,0:T(8,128)S(1)} %get-tuple-element.20), channel_id=1, source_target_pairs={{0,16},{16,0},{1,17},{17,1},{2,18},{18,2},{3,19},{19,3},{4,20},{20... | collective-permute-start | bytes 786440 | tf_op jit(solution)/shard_map/ppermute | solution.py:278
  112.5 0.0 copy-done.8
  112.6 0.7 pad_maximum_fusion
  113.3 0.4 collective-permute-done.4
  113.7 0.7 add_convert_fusion
  (5 shorter events, 0.0 us)
Async XLA Ops:
  7.2 1.0 copy-start
  7.2 13.2 %copy-start.3 = (f32[128,128]{1,0:T(8,128)S(1)}, f32[128,128]{1,0:T(8,128)}, u32[]{:S(2)}) copy-start(f32[128,128]{1,0:T(8,128)} %constant.26.clone.b2) | copy-start | bytes 196612
  7.2 13.2 %copy-start.1 = (f32[1,32,5120]{2,1,0:T(8,128)S(1)}, f32[1,32,5120]{2,1,0:T(8,128)}, u32[]{:S(2)}) copy-start(f32[1,32,5120]{2,1,0:T(8,128)} %param.9) | copy-start | bytes 1966084
  7.2 13.2 %copy-start.2 = (bf16[1,32,5120]{2,1,0:T(8,128)(2,1)S(1)}, bf16[1,32,5120]{2,1,0:T(8,128)(2,1)}, u32[]{:S(2)}) copy-start(bf16[1,32,5120]{2,1,0:T(8,128)(2,1)} %param.10) | copy-start | bytes 983044
  7.2 92.7 %all-gather.3.cloned.1.call-start = ((), (), s32[]{:S(2)}) async-start(), calls=%async_computation.3 | async-start | bytes 3317760 | tf_op jit(solution)/shard_map/all_gather | solution.py:329
  8.2 19.1 %collective-permute-start = (bf16[32,2560]{1,0:T(8,128)(2,1)S(1)}, bf16[32,2560]{1,0:T(8,128)(2,1)S(1)}, u32[]{:S(2)}, u32[]{:S(2)}) collective-permute-start(bf16[32,2560]{1,0:T(8,128)(2,1)S(1)} %constant_dynamic-slice_fusion.2.own.old), channel_id=1, source_target_pairs={{0,8},{8,0},{1,9},{9,1},{2,10},{10,2},{3,11},{11,3},{4,12},{12,4},... | collective-permute-start | bytes 491528 | tf_op jit(solution)/shard_map/ppermute | solution.py:278
  18.4 8.8 %collective-permute-start.1 = (bf16[80,128]{1,0:T(8,128)(2,1)S(1)}, bf16[80,128]{1,0:T(8,128)(2,1)S(1)}, u32[]{:S(2)}, u32[]{:S(2)}) collective-permute-start(bf16[80,128]{1,0:T(8,128)(2,1)S(1)} %shard_map.103.own_idx), channel_id=1, source_target_pairs={{0,8},{8,0},{1,9},{9,1},{2,10},{10,2},{3,11},{11,3},{4,12},{12,4},... | collective-permute-start | bytes 61448 | tf_op jit(solution)/shard_map/ppermute | solution.py:278
  24.3 46.0 %copy-start.7 = (bf16[128,5120]{1,0:T(8,128)(2,1)S(1)}, bf16[128,5120]{1,0:T(8,128)(2,1)}, u32[]{:S(2)}) copy-start(bf16[128,5120]{1,0:T(8,128)(2,1)} %param.8) | copy-start | bytes 3932164
  52.1 13.0 %all-to-all-start.1 = ((f32[32,1,384]{2,1,0:T(1,128)}), f32[32,1,384]{2,1,0:T(1,128)S(1)}, u32[]{:S(2)}, u32[]{:S(2)}) async-start(f32[32,1,384]{2,1,0:T(1,128)} %broadcast_in_dim.4), calls=%async_computation.1 | async-start | bytes 98304 | tf_op jit(solution)/shard_map/all_to_all | solution.py:49
  66.0 21.7 %collective-permute-start.2 = (bf16[32,2560]{1,0:T(8,128)(2,1)S(1)}, bf16[32,2560]{1,0:T(8,128)(2,1)}, u32[]{:S(2)}, u32[]{:S(2)}) collective-permute-start(bf16[32,2560]{1,0:T(8,128)(2,1)S(1)} %shard_map.106), channel_id=1, source_target_pairs={{0,16},{16,0},{1,17},{17,1},{2,18},{18,2},{3,19},{19,3},{4,20},{20... | collective-permute-start | bytes 491528 | tf_op jit(solution)/shard_map/ppermute | solution.py:278
  70.5 18.8 %copy-start.4 = (bf16[128,128]{1,0:T(8,128)(2,1)S(1)}, bf16[128,128]{1,0:T(8,128)(2,1)}, u32[]{:S(2)}) copy-start(bf16[128,128]{1,0:T(8,128)(2,1)} %constant.27.clone.high) | copy-start | bytes 98308
  70.5 18.8 %copy-start.5 = (bf16[128,128]{1,0:T(8,128)(2,1)S(1)}, bf16[128,128]{1,0:T(8,128)(2,1)}, u32[]{:S(2)}) copy-start(bf16[128,128]{1,0:T(8,128)(2,1)} %constant.28.clone.low) | copy-start | bytes 98308
  70.5 18.8 %collective-permute-start.3 = (bf16[128,2560]{1,0:T(8,128)(2,1)S(1)}, bf16[128,2560]{1,0:T(8,128)(2,1)S(1)}, u32[]{:S(2)}, u32[]{:S(2)}) collective-permute-start(bf16[128,2560]{1,0:T(8,128)(2,1)S(1)} %get-tuple-element.21), channel_id=1, source_target_pairs={{0,16},{16,0},{1,17},{17,1},{2,18},{18,2},{3,19},{19,3},{4,20},{20... | collective-permute-start | bytes 1966088 | tf_op jit(solution)/shard_map/ppermute | solution.py:278
  73.2 26.7 %all-to-all-start.2 = ((bf16[16,80,128]{2,1,0:T(8,128)(2,1)}), bf16[16,80,128]{2,1,0:T(8,128)(2,1)S(1)}, u32[]{:S(2)}, u32[]{:S(2)}) async-start(bf16[16,80,128]{2,1,0:T(8,128)(2,1)} %shard_map.107), calls=%async_computation.2 | async-start | bytes 655360 | tf_op jit(solution)/shard_map/all_to_all | solution.py:339
  99.9 1.8 %copy-start.6 = (bf16[11520,128]{1,0:T(8,128)(2,1)S(1)}, bf16[11520,128]{1,0:T(8,128)(2,1)}, u32[]{:S(2)}) copy-start(bf16[11520,128]{1,0:T(8,128)(2,1)} %all-gather.3.cloned.1.call-done) | copy-start | bytes 8847364
  101.7 10.8 %copy-start.8 = (bf16[32,2560]{1,0:T(8,128)(2,1)S(1)}, bf16[32,2560]{1,0:T(8,128)(2,1)}, u32[]{:S(2)}) copy-start(bf16[32,2560]{1,0:T(8,128)(2,1)} %get-tuple-element.24) | copy-start | bytes 491524
  107.4 6.3 %collective-permute-start.4 = (f32[128,512]{1,0:T(8,128)S(1)}, f32[128,512]{1,0:T(8,128)S(1)}, u32[]{:S(2)}, u32[]{:S(2)}) collective-permute-start(f32[128,512]{1,0:T(8,128)S(1)} %get-tuple-element.20), channel_id=1, source_target_pairs={{0,16},{16,0},{1,17},{17,1},{2,18},{18,2},{3,19},{19,3},{4,20},{20... | collective-permute-start | bytes 786440 | tf_op jit(solution)/shard_map/ppermute | solution.py:278
Sparse Core Ops, SparseCore 0:
  28.2 58.5 all-gather.2

commit v3 on v2

--- a/solution.py
+++ b/solution.py
@@ -34,12 +34,11 @@
 
 
 def call(kernel, out_shape, args, flops, vmem=12, **kw):
-    size = sum(a.size * a.dtype.itemsize for a in args)
     return pl.pallas_call(
         kernel,
         out_shape=out_shape,
         compiler_params=pltpu.CompilerParams(vmem_limit_bytes=vmem * 1024 * 1024),
-        cost_estimate=pl.CostEstimate(flops=flops, bytes_accessed=size, transcendentals=0),
+        cost_estimate=pl.CostEstimate(flops=flops, bytes_accessed=0, transcendentals=0),
         **kw,
     )(*args)
 
@@ -70,9 +69,13 @@
     return jnp.concatenate([high, low, high] if order else [high, high, low], axis=axis)
 
 
-def index_kernel(units, core, idx, out):
+def join_kernel(units, core, weight, idx, out):
+    rows, width = weight.shape
+    tiles = width // 2 // LANES
+    for c in range(tiles):
+        at = pl.multiple_of(core[0] * (width // 2) + c * LANES, LANES)
+        out[c * rows : (c + 1) * rows, :] = weight[:, pl.ds(at, LANES)]
     total_units = idx.shape[0] // KEEP
-    rows = LANES // STACK
     block = [idx[pl.ds(core[0] * units + u, KEEP, stride=total_units), :].astype(F32) for u in range(units)]
     full = units // STACK
     parts = []
@@ -82,17 +85,7 @@
     if full * STACK < units:
         for t in range(0, STACK, 2):
             parts.append(pick([(block[full * STACK + s % 2], t + s // 2) for s in range(STACK)], rows))
-    out[...] = jnp.concatenate(parts, axis=0).astype(BF16)
-
-
-def join_kernel(own, far, own_idx, far_idx, out):
-    rows, width = own.shape
-    tiles = width // LANES
-    size = out.shape[0] // 2
-    for h, (weight, idx) in enumerate(((own, own_idx), (far, far_idx))):
-        for c in range(tiles):
-            out[h * size + c * rows : h * size + (c + 1) * rows, :] = weight[:, c * LANES : (c + 1) * LANES]
-        out[h * size + tiles * rows : (h + 1) * size, :] = idx[...]
+    out[tiles * rows :, :] = jnp.concatenate(parts, axis=0).astype(BF16)
 
 
 def local_kernel(cores, mom, grad, idx, b2, kept, new_mom, kept_wide):
@@ -135,36 +128,6 @@
             kept[lines, :] = regroup([kept_wide[b, ur] for b in range(STACK)], rows, t)
 
 
-def weight_kernel(core, tot, idx, b2, old, new, tot_wide):
-    rows, width = old.shape
-    deep = tot.shape[0] // (STACK * KEEP)
-    span = KEEP * deep
-    total_units = idx.shape[0] // KEEP
-    units = 2 * width // (STACK * LANES)
-    for b in range(STACK):
-        tot_wide[b] = regroup([tot[t * span : (t + 1) * span, :] for t in range(STACK)], rows, b)
-    freq = lax.broadcasted_iota(jnp.int32, (GROUP, LANES), 0)
-    for g in range(units // 2):
-        parts = []
-        for c2 in range(2):
-            u = 2 * g + c2
-            value = tot_wide[u % STACK, pl.ds(u // STACK, KEEP, stride=deep), :]
-            where = idx[pl.ds(core[0] * units + u, KEEP, stride=total_units), :]
-            power = jnp.sum(value * value, axis=0, keepdims=True)
-            value = value * lax.rsqrt(power / GROUP + 1e-06)
-            spec = jnp.zeros((GROUP, LANES), F32)
-            for j in range(KEEP):
-                spec = jnp.where(freq == where[j : j + 1], value[j : j + 1], spec)
-            parts.append(spec)
-        direction = lax.dot_general(
-            jnp.concatenate(parts, axis=0), b2[...], TN, precision=HIGHEST, preferred_element_type=F32
-        )
-        for t in range(STACK):
-            cols = pl.ds((STACK * g + t) * LANES, LANES)
-            kept_part = old[:, cols].astype(F32) * (1.0 - STEP * DECAY)
-            new[:, cols] = (kept_part - STEP * direction[t * rows : (t + 1) * rows]).astype(BF16)
-
-
 def tokens_kernel(mine, theirs, high, low, out):
     batch = mine.shape[0]
     for t in range(mine.shape[1] // LANES):
@@ -175,27 +138,30 @@
         out[:, cols] = y.astype(BF16)
 
 
-def pack_kernel(units, tot, out):
-    deep = tot.shape[0] // (STACK * KEEP)
-    full = units // STACK
-    lane = lax.broadcasted_iota(jnp.int32, (KEEP, LANES), 1)
-    blocks = [[tot[pl.ds(t * KEEP * deep + r, KEEP, stride=deep), :] for t in range(STACK)] for r in range(deep)]
-    parts = []
-    for r in range(full):
-        parts += blocks[r]
-    if full < deep:
-        for t in range(0, STACK, 2):
-            upper = pltpu.roll(blocks[full][t + 1], LANES // 2, axis=1)
-            parts.append(jnp.where(lane < LANES // 2, blocks[full][t], upper))
-    packed = jnp.concatenate(parts, axis=0).astype(BF16)
-    for f in range(out.shape[0]):
-        out[f] = packed
-
-
-def product_kernel(rows, units, place, sums, tokens, mine, theirs, source, own, other, weight, vals, freqs, spec, sems):
-    shards, lines, _ = sums.shape
+def pack_kernel(units, rows, tot, out, flat):
+    fold = LANES // rows
+    shards = out.shape[1] // units * fold
+    deep = tot.shape[0] // shards
+    nq = shards // fold
+    for r in range(deep):
+        blocks = [tot[pl.ds(f * deep + r, nq, stride=fold * deep), :] for f in range(fold)]
+        for b in range(min(STACK, units - r * STACK)):
+            u = r * STACK + b
+            flat[u * nq : (u + 1) * nq, :] = regroup(blocks, rows, b)
+    packed = flat[...].astype(BF16)
+    for c in range(out.shape[0]):
+        out[c] = packed
+
+
+def product_kernel(
+    rows, units, place, sums, tokens, mine, theirs, idx, b2, old, source, own, other, new, weight, vals, freqs, spec, sems
+):
     nz, size, _ = source.shape
     size = size // 2
+    shards = 2 * nz
+    nq = shards * rows // LANES
+    lines = KEEP * units
+    stride = units * nq
     steps = units // 2
     high = STACK * rows
     fold = LANES // rows
@@ -218,8 +184,42 @@
         for b in range(STACK):
             out[b, q] = regroup(blocks, rows, b)
 
-    for q in range(shards // fold):
-        spread([sums[fold * q + f].astype(F32) for f in range(fold)], vals, q)
+    for k in range(STACK * KEEP):
+        vals[k * stride : (k + 1) * stride, :] = sums[k].astype(F32)
+
+    def coefficients(t, u, q):
+        value = vals[pl.ds(t * KEEP * stride + u * nq + q, KEEP, stride=stride), :]
+        power = jnp.sum(value * value, axis=0, keepdims=True)
+        return value * (lax.rsqrt(power / GROUP + 1e-06) * (-STEP))
+
+    shard = place[0] * nz + place[1]
+    lane = lax.broadcasted_iota(jnp.int32, (KEEP, LANES), 1) // rows
+    line = lax.broadcasted_iota(jnp.int32, (GROUP, LANES), 0)
+    total_units = idx.shape[0] // KEEP
+    batch = mine.shape[0]
+    for g in range(steps):
+        parts = []
+        for c2 in range(2):
+            u = 2 * g + c2
+            value = None
+            for t in range(STACK):
+                moved = pltpu.roll(coefficients(t, u, shard // fold), lax.rem(t - shard % fold + fold, fold) * rows, axis=1)
+                value = moved if value is None else jnp.where(lane == t, moved, value)
+            where = idx[pl.ds(place[2] * units + u, KEEP, stride=total_units), :]
+            s = jnp.zeros((GROUP, LANES), F32)
+            for j in range(KEEP):
+                s = jnp.where(line == where[j : j + 1], value[j : j + 1], s)
+            parts.append(s)
+        change = lax.dot_general(
+            split(jnp.concatenate(parts, axis=0), 0, True), b2[...], TN, preferred_element_type=F32
+        )
+        for t in range(STACK):
+            at = pl.multiple_of(place[2] * (old.shape[1] // 2) + (STACK * g + t) * LANES, LANES)
+            fresh = old[:, pl.ds(at, LANES)].astype(F32) * (1.0 - STEP * DECAY) + change[t * rows : (t + 1) * rows]
+            fresh = fresh.astype(BF16)
+            new[:, (STACK * g + t) * LANES : (STACK * g + t + 1) * LANES] = fresh
+            other[batch + g * rows : batch + (g + 1) * rows, t * LANES : (t + 1) * LANES] = fresh.astype(F32)
+
     for h in range(2):
         copy(h, steps).wait()
     for q in range(shards // fold):
@@ -232,7 +232,6 @@
     freq = lax.broadcasted_iota(jnp.int32, (GROUP, LANES), 0).astype(F32).astype(BF16)
     freq = [freq[k * pack : (k + 1) * pack] for k in range(GROUP // pack)]
     depth = 2 * STACK * GROUP
-    batch = mine.shape[0]
     wide = nz * rows
     for g in range(steps):
         slot = g % 2
@@ -245,10 +244,8 @@
                     lane, line = 2 * (t % 2) + u % STACK, (full * STACK + t // 2) * KEEP
                 for q in range(shards // fold):
                     cols = pl.ds(q * LANES, LANES)
-                    value = vals[lane, q, line : line + KEEP, :]
+                    value = coefficients(t, u, q)
                     where = freqs[lane, q, line : line + KEEP, :]
-                    power = jnp.sum(value * value, axis=0, keepdims=True)
-                    value = value * (lax.rsqrt(power / GROUP + 1e-06) * (-STEP))
                     s = [jnp.zeros((pack, LANES), BF16)] * len(freq)
                     for j in range(KEEP):
                         v = jnp.broadcast_to(value[j : j + 1], (pack, LANES)).astype(BF16)
@@ -271,7 +268,19 @@
                 part += lax.dot_general(
                     tokens[p * batch : (p + 1) * batch, cols], spec[slot, :, lanes], NN, preferred_element_type=F32
                 )
-                out[:, lanes] = part if g == 0 else out[:, lanes] + part
+                out[:batch, lanes] = part if g == 0 else out[:batch, lanes] + part
+
+
+def finish_kernel(core, own, received, new, projected, new_weight):
+    batch = own.shape[0]
+    rows, half = new.shape
+    projected[...] = (own[...] + received[:batch, : own.shape[1]]).astype(BF16)
+    new_weight[:, pl.ds(pl.multiple_of(core[0] * half, LANES), half)] = new[...]
+    for c in range(half // LANES):
+        t, g = c % STACK, c // STACK
+        at = pl.multiple_of((1 - core[0]) * half + c * LANES, LANES)
+        block = received[batch + g * rows : batch + (g + 1) * rows, t * LANES : (t + 1) * LANES]
+        new_weight[:, pl.ds(at, LANES)] = block.astype(BF16)
 
 
 def swap(x, axis):
@@ -292,92 +301,91 @@
     low = (pair - high.astype(np.float32)).astype(jnp.bfloat16)
     core = lax.axis_index("core")
 
-    own = lax.dynamic_slice(weight, (0, core * half), (rows, half))
-    far = swap(own, "yhi")
     order = kept_index.reshape(rows, groups, STACK, 2, KEEP).transpose(4, 1, 3, 2, 0).reshape(KEEP * nc * units, LANES)
     smem = pl.BlockSpec(memory_space=pltpu.SMEM)
     vmem = pl.BlockSpec(memory_space=pltpu.VMEM)
     core_ref = core.reshape(1)
-    idx_own = call(
-        functools.partial(index_kernel, units),
-        jax.ShapeDtypeStruct((KEEP * units, LANES), BF16),
-        (core_ref, order),
-        flops=1000,
-        in_specs=[smem, vmem],
-    )
-    idx_far = swap(idx_own, "yhi")
-    lines = STACK * KEEP * deep
+    size = half // LANES * rows + KEEP * units
+    near = call(
+        functools.partial(join_kernel, units),
+        jax.ShapeDtypeStruct((size, LANES), BF16),
+        (core_ref, weight, order),
+        flops=0,
+        in_specs=[smem, vmem, vmem],
+    )
+    far = swap(near, "yhi")
     kept, new_momentum = call(
         functools.partial(local_kernel, nc),
         (
-            jax.ShapeDtypeStruct((nc * lines, LANES), F32),
+            jax.ShapeDtypeStruct((nc * STACK * KEEP * deep, LANES), F32),
             jax.ShapeDtypeStruct((rows, width), F32),
         ),
         (momentum[0], gradient[0], order, jnp.asarray(pair)),
-        flops=12 * rows * width * LANES,
+        flops=0,
         scratch_shapes=[pltpu.VMEM((STACK, deep, nc * KEEP, LANES), F32)],
     )
-    far, idx_far, kept = lax.optimization_barrier((far, idx_far, kept))
-    size = half // LANES * rows + KEEP * units
-    duo = call(
-        join_kernel,
-        jax.ShapeDtypeStruct((2 * size, LANES), BF16),
-        (own, far, idx_own, idx_far),
-        flops=1000,
-    )
-    duo, kept = lax.optimization_barrier((duo, kept))
+    far, kept = lax.optimization_barrier((far, kept))
+    duo, kept = lax.optimization_barrier((jnp.concatenate([near, far], axis=0), kept))
     old_all = lax.all_gather(duo, "z", axis=0, tiled=False)
 
     pieces = lax.all_to_all(kept.reshape(nyl * nc * nx, 1, deep * LANES), ("ylo", "core", "x"), 0, 0, tiled=True)
-    total = to_all(jnp.sum(pieces, axis=0), ("ylo", "x"), nyl * nx).reshape(lines, LANES)
+    total = to_all(jnp.sum(pieces, axis=0), ("yhi", "z"), shards).reshape(shards * deep, LANES)
+    stride = units * shards * rows // LANES
     copies = call(
-        functools.partial(pack_kernel, units),
-        jax.ShapeDtypeStruct((shards, KEEP * units, LANES), BF16),
+        functools.partial(pack_kernel, units, rows),
+        jax.ShapeDtypeStruct((nyl * nx, stride, LANES), BF16),
         (total,),
-        flops=1000,
-    )
-    sums = lax.all_to_all(copies, ("yhi", "z"), 0, 0, tiled=True)
+        flops=0,
+        scratch_shapes=[pltpu.VMEM((stride, LANES), F32)],
+    )
+    sums = lax.all_to_all(copies, ("ylo", "x"), 0, 0, tiled=True)
 
     mine = lax.dynamic_slice(tokens, (0, core * half), (batch, half))
     theirs = swap(lax.dynamic_slice(tokens, (0, (1 - core) * half), (batch, half)), "core")
-
-    own_new = call(
-        weight_kernel,
-        jax.ShapeDtypeStruct((rows, half), BF16),
-        (core_ref, total, order, jnp.asarray(pair), own),
-        flops=12 * rows * half * LANES,
-        in_specs=[smem, vmem, vmem, vmem, vmem],
-        scratch_shapes=[pltpu.VMEM((STACK, KEEP * deep, LANES), F32)],
-    )
-    other_new = swap(own_new, "core")
-    left = core == 0
-    new_weight = jnp.concatenate([jnp.where(left, own_new, other_new), jnp.where(left, other_new, own_new)], axis=1)
-
     turned = call(
         tokens_kernel,
         jax.ShapeDtypeStruct((nc * batch, half), BF16),
         (mine, theirs, jnp.asarray(high), jnp.asarray(low)),
-        flops=4 * nc * batch * half * LANES,
+        flops=0,
     )
     out_width = shards * rows
-    part = jax.ShapeDtypeStruct((batch, out_width), F32)
-    table = pltpu.VMEM((STACK, out_width // LANES, KEEP * units, LANES), F32)
-    here, there = call(
+    back = jnp.asarray(np.concatenate([high, high, low], axis=0))
+    here, there, own_new = call(
         functools.partial(product_kernel, rows, units),
-        (part, part),
-        (lax.axis_index("yhi").reshape(1), sums, turned, mine, theirs, old_all),
-        flops=6 * nc * batch * half * out_width,
+        (
+            jax.ShapeDtypeStruct((batch, out_width), F32),
+            jax.ShapeDtypeStruct((batch + units // 2 * rows, max(out_width, STACK * LANES)), F32),
+            jax.ShapeDtypeStruct((rows, half), BF16),
+        ),
+        (
+            jnp.stack([lax.axis_index("yhi"), lax.axis_index("z"), core]),
+            sums,
+            turned,
+            mine,
+            theirs,
+            order,
+            back,
+            weight,
+            pltpu.with_memory_space_constraint(old_all, pltpu.HBM),
+        ),
+        flops=0,
         vmem=20,
-        in_specs=[smem, vmem, vmem, vmem, vmem, pl.BlockSpec(memory_space=pl.ANY)],
+        in_specs=[smem] + [vmem] * 7 + [pl.BlockSpec(memory_space=pltpu.HBM)],
         scratch_shapes=[
             pltpu.VMEM((nz, 2 * size, LANES), BF16),
-            table,
-            table,
+            pltpu.VMEM((STACK * KEEP * stride, LANES), F32),
+            pltpu.VMEM((STACK, out_width // LANES, KEEP * units, LANES), F32),
             pltpu.VMEM((2, 2 * STACK * GROUP, out_width), BF16),
             pltpu.SemaphoreType.DMA((2, units // 2 + 1)),
         ],
     )
-    projected = (here + swap(there, "core")).astype(BF16)
+    projected, new_weight = call(
+        finish_kernel,
+        (jax.ShapeDtypeStruct((batch, out_width), BF16), jax.ShapeDtypeStruct((rows, width), BF16)),
+        (core_ref, here, swap(there, "core"), own_new),
+        flops=0,
+        in_specs=[smem, vmem, vmem, vmem],
+    )
     return new_weight, new_momentum[None], projected
 
 

time: 122 us -> 118 us (0.967)
  blocking collectives: 23.3 us -> 0 us
  starting transfers between devices: 40.4 us -> 58.2 us
  waiting for transfers between devices: 22.2 us -> 27.6 us
  other arithmetic: 3.15 us -> 0.93 us
  local copies, waits for them, and re-layouts: 4.91 us -> 3.08 us
    all_to_all x1 -> x0, blocking collectives: 23.3 us -> none  [body(): lax.all_to_all(kept.reshape(nyl * nc * nx, 1, deep * LANES), ('ylo', 'cor...]
    all_to_all x1, starting transfers between devices: 3.86 us -> 17.8 us  [to_all(): return lax.all_to_all(copies, axes, 0, 0, tiled=True)]
    all_to_all x1 -> x2, waiting for transfers between devices: 9.74 us -> 19.1 us  [the longest x1 9.68 us: body(): lax.all_to_all(kept.reshape(nyl * nc * nx, 1, deep * LANES), ('ylo', 'cor...]
    all_to_all x1 -> x2, starting transfers between devices: 14.4 us -> 20.7 us  [the longest x1 16.8 us: body(): lax.all_to_all(kept.reshape(nyl * nc * nx, 1, deep * LANES), ('ylo', 'cor...]
    unnamed x19 -> x17, local copies, waits for them, and re-layouts: 3.84 us -> 1.22 us
    ppermute x5 -> x3, starting transfers between devices: 22.1 us -> 19.7 us  [swap(): return lax.ppermute(x, axis, [(0, 1), (1, 0)])]
    all_to_all x1, waiting for transfers between devices: 9.15 us -> 6.84 us  [to_all(): return lax.all_to_all(copies, axes, 0, 0, tiled=True)]
    ppermute x5 -> x3, waiting for transfers between devices: 3.28 us -> 1.61 us  [swap(): return lax.ppermute(x, axis, [(0, 1), (1, 0)])]
  transfers between devices with their start and end apart: 8 -> 7, of which waited for: 4 -> 4; matrix products, arithmetic and copies ran while one was open for 4% -> 1% of each run, Pallas kernels for 5% -> 5%
where the time goes in v3:
time: 118 us
  starting transfers between devices  58.2 us (49%)
  waiting for transfers between devices  27.6 us (23%)
  between operations  14.2 us (12%)
  Pallas kernels  13.8 us (12%)
  local copies, waits for them, and re-layouts  3.08 us (3%)
    ppermute x3, starting transfers between devices, swap(): return lax.ppermute(x, axis, [(0, 1), (1, 0)])  19.7 us
    all_to_all x1, starting transfers between devices, to_all(): return lax.all_to_all(copies, axes, 0, 0, tiled=True)  17.8 us
    all_to_all x1, starting transfers between devices, body(): lax.all_to_all(kept.reshape(nyl * nc * nx, 1, deep * LANES), ('ylo', 'cor...  16.8 us
    pallas_call x6, Pallas kernels, call(): pl.pallas_call(kernel, out_shape=out_shape, compiler_params=pltpu.Compile...  13.8 us
    all_to_all x1, waiting for transfers between devices, body(): lax.all_to_all(kept.reshape(nyl * nc * nx, 1, deep * LANES), ('ylo', 'cor...  9.68 us
    all_to_all x1, waiting for transfers between devices, body(): sums = lax.all_to_all(copies, ('ylo', 'x'), 0, 0, tiled=True)  9.41 us
    all_to_all x1, waiting for transfers between devices, to_all(): return lax.all_to_all(copies, axes, 0, 0, tiled=True)  6.84 us
    all_to_all x1, starting transfers between devices, body(): sums = lax.all_to_all(copies, ('ylo', 'x'), 0, 0, tiled=True)  3.88 us
  transfers between devices with their start and end apart: 7, of which 4 were waited for; matrix products, arithmetic and copies ran while one was open for 1% of the time, Pallas kernels for 5%

profile of v3, /device:TPU:1, one launch (start us, length us, event | category | flops | bytes accessed | tf_op | source)
XLA Modules:
  0.0 117.8 jit_solution(10525089688975365844)
XLA Ops:
  7.2 0.0 copy-start.4
  7.2 0.0 copy-start
  7.2 0.0 copy-start.2
  7.2 0.0 copy-start.1
  7.2 0.0 all-gather.3.cloned.1.call-start
  7.3 1.2 copy.15
  8.4 0.1 copy.16
  8.6 0.2 reshape.28.idx
  8.8 0.0 copy-done
  8.8 0.1 shard_map.112
  8.9 8.7 %collective-permute-start = (bf16[720,128]{1,0:T(8,128)(2,1)S(1)}, bf16[720,128]{1,0:T(8,128)(2,1)S(1)}, u32[]{:S(2)}, u32[]{:S(2)}) collective-permute-start(bf16[720,128]{1,0:T(8,128)(2,1)S(1)} %shard_map.112), channel_id=1, source_target_pairs={{0,8},{8,0},{1,9},{9,1},{2,10},{10,2},{3,11},{11,3},{4,12},{12,4},... | collective-permute-start | bytes 552968 | tf_op jit(solution)/shard_map/ppermute | solution.py:287
  17.6 0.0 copy-done.4
  17.6 0.0 copy-done.2
  17.6 0.0 copy-done.1
  17.6 0.0 copy-start.7
  17.6 4.0 %shard_map.113 = (f32[192,128]{1,0:T(8,128)}, f32[32,5120]{1,0:T(8,128)}) custom-call(f32[32,5120]{1,0:T(8,128)S(1)} %bitcast.12, bf16[32,5120]{1,0:T(8,128)(2,1)S(1)} %bitcast.13, s32[160,128]{1,0:T(8,128)S(1)} %reshape.28.idx, f32[128,128]{1,0:T(8,128)S(1)} %copy-done.4), custom_call_target="tpu_custom_call" | custom-call | tf_op jit(solution)/shard_map/pallas_call | solution.py:37
  21.6 0.0 collective-permute-done
  21.6 0.8 pad_maximum_fusion
  22.4 0.0 all-gather.3.cloned.1.call-update
  22.4 16.8 %all-to-all-start = ((f32[64,1,384]{2,1,0:T(1,128)}), f32[64,1,384]{2,1,0:T(1,128)S(1)}, u32[]{:S(2)}, u32[]{:S(2)}) async-start(f32[64,1,384]{2,1,0:T(1,128)} %bitcast.7), calls=%async_computation | async-start | bytes 196608 | tf_op jit(solution)/shard_map/all_to_all | solution.py:331
  39.3 9.7 %all-to-all-done = f32[64,1,384]{2,1,0:T(1,128)S(1)} async-done(((f32[64,1,384]{2,1,0:T(1,128)}), f32[64,1,384]{2,1,0:T(1,128)S(1)}, u32[]{:S(2)}, u32[]{:S(2)}) %all-to-all-start) | async-done | bytes 98336 | tf_op jit(solution)/shard_map/all_to_all | solution.py:331
  48.9 0.1 reduce_sum.9
  49.0 0.6 broadcast_in_dim.4
  49.7 17.8 %all-to-all-start.1 = ((f32[16,1,384]{2,1,0:T(1,128)}), f32[16,1,384]{2,1,0:T(1,128)S(1)}, u32[]{:S(2)}, u32[]{:S(2)}) async-start(f32[16,1,384]{2,1,0:T(1,128)} %broadcast_in_dim.4), calls=%async_computation.1 | async-start | bytes 49152 | tf_op jit(solution)/shard_map/all_to_all | solution.py:48
  67.5 0.0 copy-done.7
  67.5 0.0 copy-start.5
  67.5 0.0 copy-start.6
  67.5 0.9 constant_dynamic-slice_fusion
  68.4 3.6 %collective-permute-start.1 = (bf16[128,2560]{1,0:T(8,128)(2,1)}, bf16[128,2560]{1,0:T(8,128)(2,1)S(1)}, u32[]{:S(2)}, u32[]{:S(2)}) collective-permute-start(bf16[128,2560]{1,0:T(8,128)(2,1)} %get-tuple-element.25), channel_id=1, source_target_pairs={{0,16},{16,0},{1,17},{17,1},{2,18},{18,2},{3,19},{19,3},{4,20},{20... | collective-permute-start | bytes 1966088 | tf_op jit(solution)/shard_map/ppermute | solution.py:287
  72.0 6.8 %all-to-all-done.1 = f32[16,1,384]{2,1,0:T(1,128)S(1)} async-done(((f32[16,1,384]{2,1,0:T(1,128)}), f32[16,1,384]{2,1,0:T(1,128)S(1)}, u32[]{:S(2)}, u32[]{:S(2)}) %all-to-all-start.1) | async-done | bytes 24608 | tf_op jit(solution)/shard_map/all_to_all | solution.py:48
  78.9 0.8 shard_map.114
  79.7 3.9 %all-to-all-start.2 = ((bf16[32,40,128]{2,1,0:T(8,128)(2,1)}), bf16[32,40,128]{2,1,0:T(8,128)(2,1)S(1)}, u32[]{:S(2)}, u32[]{:S(2)}) async-start(bf16[32,40,128]{2,1,0:T(8,128)(2,1)} %shard_map.114), calls=%async_computation.2 | async-start | bytes 655360 | tf_op jit(solution)/shard_map/all_to_all | solution.py:341
  83.6 0.1 pad_add_fusion.place
  83.7 0.0 collective-permute-done.1.theirs
  83.7 0.0 copy-done.5
  83.7 0.0 copy-done.6
  83.7 0.0 copy-start.3
  83.7 0.8 shard_map.115.tokens
  84.5 9.4 %all-to-all-done.2.sums = bf16[32,40,128]{2,1,0:T(8,128)(2,1)S(1)} async-done(((bf16[32,40,128]{2,1,0:T(8,128)(2,1)}), bf16[32,40,128]{2,1,0:T(8,128)(2,1)S(1)}, u32[]{:S(2)}, u32[]{:S(2)}) %all-to-all-start.2) | async-done | bytes 327712 | tf_op jit(solution)/shard_map/all_to_all | solution.py:341
  94.0 0.0 all-gather.3.cloned.1.call-done
  94.0 0.0 copy-done.3
  94.0 7.2 %shard_map.116 = (f32[128,512]{1,0:T(8,128)S(1)}, f32[288,512]{1,0:T(8,128)S(1)}, bf16[32,2560]{1,0:T(8,128)(2,1)S(1)}) custom-call(s32[3]{0:T(128)S(1)} %pad_add_fusion.place, bf16[32,40,128]{2,1,0:T(8,128)(2,1)S(1)} %all-to-all-done.2.sums, bf16[256,2560]{1,0:T(8,128)(2,1)S(1)} %shard_map.115.tokens, bf16[128,2560]{1,0:T(8,128)(2,1)S(1)} %get-tuple-element.26.mine, ...), custom_call_target="tpu_custom_call" | custom-call | tf_op jit(solution)/shard_map/pallas_call | solution.py:37
  101.2 7.4 %collective-permute-start.2 = (f32[288,512]{1,0:T(8,128)S(1)}, f32[288,512]{1,0:T(8,128)S(1)}, u32[]{:S(2)}, u32[]{:S(2)}) collective-permute-start(f32[288,512]{1,0:T(8,128)S(1)} %get-tuple-element.20), channel_id=1, source_target_pairs={{0,16},{16,0},{1,17},{17,1},{2,18},{18,2},{3,19},{19,3},{4,20},{20... | collective-permute-start | bytes 1769480 | tf_op jit(solution)/shard_map/ppermute | solution.py:287
  108.6 1.6 %collective-permute-done.2.received = f32[288,512]{1,0:T(8,128)S(1)} collective-permute-done((f32[288,512]{1,0:T(8,128)S(1)}, f32[288,512]{1,0:T(8,128)S(1)}, u32[]{:S(2)}, u32[]{:S(2)}) %collective-permute-start.2) | collective-permute-done | bytes 589856 | tf_op jit(solution)/shard_map/ppermute | solution.py:287
  110.2 0.8 shard_map.117
Async XLA Ops:
  7.2 10.4 %copy-start.4 = (f32[128,128]{1,0:T(8,128)S(1)}, f32[128,128]{1,0:T(8,128)}, u32[]{:S(2)}) copy-start(f32[128,128]{1,0:T(8,128)} %constant.31.clone.b2) | copy-start | bytes 196612
  7.2 1.6 %copy-start = (bf16[32,5120]{1,0:T(8,128)(2,1)S(1)}, bf16[32,5120]{1,0:T(8,128)(2,1)}, u32[]{:S(2)}) copy-start(bf16[32,5120]{1,0:T(8,128)(2,1)} %old.1) | copy-start | bytes 983044
  7.2 10.4 %copy-start.2 = (bf16[1,32,5120]{2,1,0:T(8,128)(2,1)S(1)}, bf16[1,32,5120]{2,1,0:T(8,128)(2,1)}, u32[]{:S(2)}) copy-start(bf16[1,32,5120]{2,1,0:T(8,128)(2,1)} %param.11) | copy-start | bytes 983044
  7.2 10.4 %copy-start.1 = (f32[1,32,5120]{2,1,0:T(8,128)S(1)}, f32[1,32,5120]{2,1,0:T(8,128)}, u32[]{:S(2)}) copy-start(f32[1,32,5120]{2,1,0:T(8,128)} %param.10) | copy-start | bytes 1966084
  7.2 86.7 %all-gather.3.cloned.1.call-start = ((), (), s32[]{:S(2)}) async-start(), calls=%async_computation.3 | async-start | bytes 3317760 | tf_op jit(solution)/shard_map/all_gather | solution.py:329
  8.9 12.8 %collective-permute-start = (bf16[720,128]{1,0:T(8,128)(2,1)S(1)}, bf16[720,128]{1,0:T(8,128)(2,1)S(1)}, u32[]{:S(2)}, u32[]{:S(2)}) collective-permute-start(bf16[720,128]{1,0:T(8,128)(2,1)S(1)} %shard_map.112), channel_id=1, source_target_pairs={{0,8},{8,0},{1,9},{9,1},{2,10},{10,2},{3,11},{11,3},{4,12},{12,4},... | collective-permute-start | bytes 552968 | tf_op jit(solution)/shard_map/ppermute | solution.py:287
  17.6 49.8 %copy-start.7 = (bf16[128,5120]{1,0:T(8,128)(2,1)S(1)}, bf16[128,5120]{1,0:T(8,128)(2,1)}, u32[]{:S(2)}) copy-start(bf16[128,5120]{1,0:T(8,128)(2,1)} %param.9) | copy-start | bytes 3932164
  22.4 26.5 %all-to-all-start = ((f32[64,1,384]{2,1,0:T(1,128)}), f32[64,1,384]{2,1,0:T(1,128)S(1)}, u32[]{:S(2)}, u32[]{:S(2)}) async-start(f32[64,1,384]{2,1,0:T(1,128)} %bitcast.7), calls=%async_computation | async-start | bytes 196608 | tf_op jit(solution)/shard_map/all_to_all | solution.py:331
  49.7 29.2 %all-to-all-start.1 = ((f32[16,1,384]{2,1,0:T(1,128)}), f32[16,1,384]{2,1,0:T(1,128)S(1)}, u32[]{:S(2)}, u32[]{:S(2)}) async-start(f32[16,1,384]{2,1,0:T(1,128)} %broadcast_in_dim.4), calls=%async_computation.1 | async-start | bytes 49152 | tf_op jit(solution)/shard_map/all_to_all | solution.py:48
  67.5 16.2 %copy-start.5 = (bf16[128,128]{1,0:T(8,128)(2,1)S(1)}, bf16[128,128]{1,0:T(8,128)(2,1)}, u32[]{:S(2)}) copy-start(bf16[128,128]{1,0:T(8,128)(2,1)} %constant.33.clone.low) | copy-start | bytes 98308
  67.5 16.2 %copy-start.6 = (bf16[128,128]{1,0:T(8,128)(2,1)S(1)}, bf16[128,128]{1,0:T(8,128)(2,1)}, u32[]{:S(2)}) copy-start(bf16[128,128]{1,0:T(8,128)(2,1)} %constant.32.clone.high) | copy-start | bytes 98308
  68.4 15.2 %collective-permute-start.1 = (bf16[128,2560]{1,0:T(8,128)(2,1)}, bf16[128,2560]{1,0:T(8,128)(2,1)S(1)}, u32[]{:S(2)}, u32[]{:S(2)}) collective-permute-start(bf16[128,2560]{1,0:T(8,128)(2,1)} %get-tuple-element.25), channel_id=1, source_target_pairs={{0,16},{16,0},{1,17},{17,1},{2,18},{18,2},{3,19},{19,3},{4,20},{20... | collective-permute-start | bytes 1966088 | tf_op jit(solution)/shard_map/ppermute | solution.py:287
  79.7 14.3 %all-to-all-start.2 = ((bf16[32,40,128]{2,1,0:T(8,128)(2,1)}), bf16[32,40,128]{2,1,0:T(8,128)(2,1)S(1)}, u32[]{:S(2)}, u32[]{:S(2)}) async-start(bf16[32,40,128]{2,1,0:T(8,128)(2,1)} %shard_map.114), calls=%async_computation.2 | async-start | bytes 655360 | tf_op jit(solution)/shard_map/all_to_all | solution.py:341
  83.7 10.3 %copy-start.3 = (bf16[384,128]{1,0:T(8,128)(2,1)S(1)}, bf16[384,128]{1,0:T(8,128)(2,1)}, u32[]{:S(2)}) copy-start(bf16[384,128]{1,0:T(8,128)(2,1)} %constant.34.clone.b2) | copy-start | bytes 294916
  101.2 9.0 %collective-permute-start.2 = (f32[288,512]{1,0:T(8,128)S(1)}, f32[288,512]{1,0:T(8,128)S(1)}, u32[]{:S(2)}, u32[]{:S(2)}) collective-permute-start(f32[288,512]{1,0:T(8,128)S(1)} %get-tuple-element.20), channel_id=1, source_target_pairs={{0,16},{16,0},{1,17},{17,1},{2,18},{18,2},{3,19},{19,3},{4,20},{20... | collective-permute-start | bytes 1769480 | tf_op jit(solution)/shard_map/ppermute | solution.py:287
Sparse Core Ops, SparseCore 0:
  22.5 65.9 all-gather.2

commit v4 on v2

--- a/solution.py
+++ b/solution.py
@@ -34,12 +34,11 @@
 
 
 def call(kernel, out_shape, args, flops, vmem=12, **kw):
-    size = sum(a.size * a.dtype.itemsize for a in args)
     return pl.pallas_call(
         kernel,
         out_shape=out_shape,
         compiler_params=pltpu.CompilerParams(vmem_limit_bytes=vmem * 1024 * 1024),
-        cost_estimate=pl.CostEstimate(flops=flops, bytes_accessed=size, transcendentals=0),
+        cost_estimate=pl.CostEstimate(flops=flops, bytes_accessed=0, transcendentals=0),
         **kw,
     )(*args)
 
@@ -70,9 +69,13 @@
     return jnp.concatenate([high, low, high] if order else [high, high, low], axis=axis)
 
 
-def index_kernel(units, core, idx, out):
+def join_kernel(units, core, weight, idx, out):
+    rows, width = weight.shape
+    tiles = width // 2 // LANES
+    for c in range(tiles):
+        at = pl.multiple_of(core[0] * (width // 2) + c * LANES, LANES)
+        out[c * rows : (c + 1) * rows, :] = weight[:, pl.ds(at, LANES)]
     total_units = idx.shape[0] // KEEP
-    rows = LANES // STACK
     block = [idx[pl.ds(core[0] * units + u, KEEP, stride=total_units), :].astype(F32) for u in range(units)]
     full = units // STACK
     parts = []
@@ -82,17 +85,7 @@
     if full * STACK < units:
         for t in range(0, STACK, 2):
             parts.append(pick([(block[full * STACK + s % 2], t + s // 2) for s in range(STACK)], rows))
-    out[...] = jnp.concatenate(parts, axis=0).astype(BF16)
-
-
-def join_kernel(own, far, own_idx, far_idx, out):
-    rows, width = own.shape
-    tiles = width // LANES
-    size = out.shape[0] // 2
-    for h, (weight, idx) in enumerate(((own, own_idx), (far, far_idx))):
-        for c in range(tiles):
-            out[h * size + c * rows : h * size + (c + 1) * rows, :] = weight[:, c * LANES : (c + 1) * LANES]
-        out[h * size + tiles * rows : (h + 1) * size, :] = idx[...]
+    out[tiles * rows :, :] = jnp.concatenate(parts, axis=0).astype(BF16)
 
 
 def local_kernel(cores, mom, grad, idx, b2, kept, new_mom, kept_wide):
@@ -136,7 +129,7 @@
 
 
 def weight_kernel(core, tot, idx, b2, old, new, tot_wide):
-    rows, width = old.shape
+    rows, width = new.shape
     deep = tot.shape[0] // (STACK * KEEP)
     span = KEEP * deep
     total_units = idx.shape[0] // KEEP
@@ -157,11 +150,12 @@
                 spec = jnp.where(freq == where[j : j + 1], value[j : j + 1], spec)
             parts.append(spec)
         direction = lax.dot_general(
-            jnp.concatenate(parts, axis=0), b2[...], TN, precision=HIGHEST, preferred_element_type=F32
+            split(jnp.concatenate(parts, axis=0), 0, True), b2[...], TN, preferred_element_type=F32
         )
         for t in range(STACK):
             cols = pl.ds((STACK * g + t) * LANES, LANES)
-            kept_part = old[:, cols].astype(F32) * (1.0 - STEP * DECAY)
+            at = pl.multiple_of(core[0] * width + (STACK * g + t) * LANES, LANES)
+            kept_part = old[:, pl.ds(at, LANES)].astype(F32) * (1.0 - STEP * DECAY)
             new[:, cols] = (kept_part - STEP * direction[t * rows : (t + 1) * rows]).astype(BF16)
 
 
@@ -192,14 +186,14 @@
         out[f] = packed
 
 
-def product_kernel(rows, units, place, sums, tokens, mine, theirs, source, own, other, weight, vals, freqs, spec, sems):
-    shards, lines, _ = sums.shape
+def old_kernel(rows, units, place, mine, theirs, source, own, other, freqs, weight, sems):
     nz, size, _ = source.shape
     size = size // 2
+    shards = 2 * nz
+    lines = KEEP * units
     steps = units // 2
     high = STACK * rows
     fold = LANES // rows
-    full = units // STACK
 
     def copy(h, k):
         at = h * size + (steps * high if k == steps else k * high)
@@ -214,12 +208,6 @@
         h = place[0] if y == 0 else 1 - place[0]
         return h * size
 
-    def spread(blocks, out, q):
-        for b in range(STACK):
-            out[b, q] = regroup(blocks, rows, b)
-
-    for q in range(shards // fold):
-        spread([sums[fold * q + f].astype(F32) for f in range(fold)], vals, q)
     for h in range(2):
         copy(h, steps).wait()
     for q in range(shards // fold):
@@ -227,34 +215,11 @@
         for f in range(fold * q, fold * (q + 1)):
             at = pl.multiple_of(start_of(f // nz) + steps * high, 16)
             blocks.append(weight[f % nz, pl.ds(at, lines), :].astype(F32))
-        spread(blocks, freqs, q)
-    pack = 16
-    freq = lax.broadcasted_iota(jnp.int32, (GROUP, LANES), 0).astype(F32).astype(BF16)
-    freq = [freq[k * pack : (k + 1) * pack] for k in range(GROUP // pack)]
+        for b in range(STACK):
+            freqs[b, q] = regroup(blocks, rows, b)
     depth = 2 * STACK * GROUP
-    batch = mine.shape[0]
     wide = nz * rows
     for g in range(steps):
-        slot = g % 2
-        for t in range(STACK):
-            for c2 in range(2):
-                u = 2 * g + c2
-                if u // STACK < full:
-                    lane, line = u % STACK, (u // STACK * STACK + t) * KEEP
-                else:
-                    lane, line = 2 * (t % 2) + u % STACK, (full * STACK + t // 2) * KEEP
-                for q in range(shards // fold):
-                    cols = pl.ds(q * LANES, LANES)
-                    value = vals[lane, q, line : line + KEEP, :]
-                    where = freqs[lane, q, line : line + KEEP, :]
-                    power = jnp.sum(value * value, axis=0, keepdims=True)
-                    value = value * (lax.rsqrt(power / GROUP + 1e-06) * (-STEP))
-                    s = [jnp.zeros((pack, LANES), BF16)] * len(freq)
-                    for j in range(KEEP):
-                        v = jnp.broadcast_to(value[j : j + 1], (pack, LANES)).astype(BF16)
-                        w = jnp.broadcast_to(where[j : j + 1], (pack, LANES)).astype(BF16)
-                        s = [jnp.where(f == w, v, old) for f, old in zip(freq, s)]
-                    spec[slot, pl.ds((2 * t + c2) * GROUP, GROUP), cols] = jnp.concatenate(s, axis=0)
         for h in range(2):
             copy(h, g).wait()
         cols = pl.ds(g * depth, depth)
@@ -266,12 +231,55 @@
                 tiles.append(jnp.concatenate([weight[z, pl.ds(line, rows), :] for z in range(nz)], axis=0))
             w = jnp.concatenate(tiles, axis=1)
             lanes = pl.ds(y * wide, wide)
-            for p, (x, out) in enumerate(((mine, own), (theirs, other))):
+            for x, out in ((mine, own), (theirs, other)):
                 part = lax.dot_general(x[:, cols], w, NT, preferred_element_type=F32) * (1.0 - STEP * DECAY)
-                part += lax.dot_general(
-                    tokens[p * batch : (p + 1) * batch, cols], spec[slot, :, lanes], NN, preferred_element_type=F32
-                )
                 out[:, lanes] = part if g == 0 else out[:, lanes] + part
+
+
+def product_kernel(rows, units, sums, tokens, freqs, old_own, old_other, own, other, vals, spec):
+    shards, lines, _ = sums.shape
+    batch = own.shape[0]
+    fold = LANES // rows
+    full = units // STACK
+    for q in range(shards // fold):
+        blocks = [sums[fold * q + f].astype(F32) for f in range(fold)]
+        for b in range(STACK):
+            vals[b, q] = regroup(blocks, rows, b)
+    pack = 16
+    freq = lax.broadcasted_iota(jnp.int32, (GROUP, LANES), 0).astype(F32).astype(BF16)
+    freq = [freq[k * pack : (k + 1) * pack] for k in range(GROUP // pack)]
+    depth = 2 * STACK * GROUP
+    for g in range(units // 2):
+        slot = g % 2
+        for t in range(STACK):
+            for c2 in range(2):
+                u = 2 * g + c2
+                if u // STACK < full:
+                    lane, line = u % STACK, (u // STACK * STACK + t) * KEEP
+                else:
+                    lane, line = 2 * (t % 2) + u % STACK, (full * STACK + t // 2) * KEEP
+                for q in range(shards // fold):
+                    value = vals[lane, q, line : line + KEEP, :]
+                    where = freqs[lane, q, line : line + KEEP, :]
+                    power = jnp.sum(value * value, axis=0, keepdims=True)
+                    value = value * (lax.rsqrt(power / GROUP + 1e-06) * (-STEP))
+                    s = [jnp.zeros((pack, LANES), BF16)] * len(freq)
+                    for j in range(KEEP):
+                        v = jnp.broadcast_to(value[j : j + 1], (pack, LANES)).astype(BF16)
+                        w = jnp.broadcast_to(where[j : j + 1], (pack, LANES)).astype(BF16)
+                        s = [jnp.where(f == w, v, old) for f, old in zip(freq, s)]
+                    spec[slot, pl.ds((2 * t + c2) * GROUP, GROUP), pl.ds(q * LANES, LANES)] = jnp.concatenate(s, axis=0)
+        cols = pl.ds(g * depth, depth)
+        for p, (out, old) in enumerate(((own, old_own), (other, old_other))):
+            x = tokens[p * batch : (p + 1) * batch, cols]
+            part = lax.dot_general(x, spec[slot], NN, preferred_element_type=F32)
+            out[...] = part + (old[...] if g == 0 else out[...])
+
+
+def sides_kernel(core, mine, theirs, new_weight):
+    half = mine.shape[1]
+    new_weight[:, pl.ds(pl.multiple_of(core[0] * half, LANES), half)] = mine[...]
+    new_weight[:, pl.ds(pl.multiple_of((1 - core[0]) * half, LANES), half)] = theirs[...]
 
 
 def swap(x, axis):
@@ -292,90 +300,93 @@
     low = (pair - high.astype(np.float32)).astype(jnp.bfloat16)
     core = lax.axis_index("core")
 
-    own = lax.dynamic_slice(weight, (0, core * half), (rows, half))
-    far = swap(own, "yhi")
     order = kept_index.reshape(rows, groups, STACK, 2, KEEP).transpose(4, 1, 3, 2, 0).reshape(KEEP * nc * units, LANES)
     smem = pl.BlockSpec(memory_space=pltpu.SMEM)
     vmem = pl.BlockSpec(memory_space=pltpu.VMEM)
     core_ref = core.reshape(1)
-    idx_own = call(
-        functools.partial(index_kernel, units),
-        jax.ShapeDtypeStruct((KEEP * units, LANES), BF16),
-        (core_ref, order),
-        flops=1000,
-        in_specs=[smem, vmem],
-    )
-    idx_far = swap(idx_own, "yhi")
-    lines = STACK * KEEP * deep
+    size = half // LANES * rows + KEEP * units
+    near = call(
+        functools.partial(join_kernel, units),
+        jax.ShapeDtypeStruct((size, LANES), BF16),
+        (core_ref, weight, order),
+        flops=0,
+        in_specs=[smem, vmem, vmem],
+    )
+    far = swap(near, "yhi")
     kept, new_momentum = call(
         functools.partial(local_kernel, nc),
         (
-            jax.ShapeDtypeStruct((nc * lines, LANES), F32),
+            jax.ShapeDtypeStruct((nc * STACK * KEEP * deep, LANES), F32),
             jax.ShapeDtypeStruct((rows, width), F32),
         ),
         (momentum[0], gradient[0], order, jnp.asarray(pair)),
-        flops=12 * rows * width * LANES,
+        flops=0,
         scratch_shapes=[pltpu.VMEM((STACK, deep, nc * KEEP, LANES), F32)],
     )
-    far, idx_far, kept = lax.optimization_barrier((far, idx_far, kept))
-    size = half // LANES * rows + KEEP * units
-    duo = call(
-        join_kernel,
-        jax.ShapeDtypeStruct((2 * size, LANES), BF16),
-        (own, far, idx_own, idx_far),
-        flops=1000,
-    )
-    duo, kept = lax.optimization_barrier((duo, kept))
+    far, _ = lax.optimization_barrier((far, kept))
+    duo = jnp.concatenate([near, far], axis=0)
+
+    pieces = lax.all_to_all(kept.reshape(nyl * nc * nx, 1, deep * LANES), ("ylo", "core", "x"), 0, 0, tiled=True)
+    pieces, _ = lax.optimization_barrier((pieces, duo))
     old_all = lax.all_gather(duo, "z", axis=0, tiled=False)
-
-    pieces = lax.all_to_all(kept.reshape(nyl * nc * nx, 1, deep * LANES), ("ylo", "core", "x"), 0, 0, tiled=True)
+    lines = STACK * KEEP * deep
     total = to_all(jnp.sum(pieces, axis=0), ("ylo", "x"), nyl * nx).reshape(lines, LANES)
     copies = call(
         functools.partial(pack_kernel, units),
         jax.ShapeDtypeStruct((shards, KEEP * units, LANES), BF16),
         (total,),
-        flops=1000,
+        flops=0,
     )
     sums = lax.all_to_all(copies, ("yhi", "z"), 0, 0, tiled=True)
-
-    mine = lax.dynamic_slice(tokens, (0, core * half), (batch, half))
-    theirs = swap(lax.dynamic_slice(tokens, (0, (1 - core) * half), (batch, half)), "core")
 
     own_new = call(
         weight_kernel,
         jax.ShapeDtypeStruct((rows, half), BF16),
-        (core_ref, total, order, jnp.asarray(pair), own),
-        flops=12 * rows * half * LANES,
+        (core_ref, total, order, jnp.asarray(np.concatenate([high, high, low], axis=0)), weight),
+        flops=0,
         in_specs=[smem, vmem, vmem, vmem, vmem],
         scratch_shapes=[pltpu.VMEM((STACK, KEEP * deep, LANES), F32)],
     )
     other_new = swap(own_new, "core")
-    left = core == 0
-    new_weight = jnp.concatenate([jnp.where(left, own_new, other_new), jnp.where(left, other_new, own_new)], axis=1)
-
+    new_weight = call(
+        sides_kernel,
+        jax.ShapeDtypeStruct((rows, width), BF16),
+        (core_ref, own_new, other_new),
+        flops=0,
+        in_specs=[smem, vmem, vmem],
+    )
+
+    mine = lax.dynamic_slice(tokens, (0, core * half), (batch, half))
+    theirs = swap(lax.dynamic_slice(tokens, (0, (1 - core) * half), (batch, half)), "core")
     turned = call(
         tokens_kernel,
         jax.ShapeDtypeStruct((nc * batch, half), BF16),
         (mine, theirs, jnp.asarray(high), jnp.asarray(low)),
-        flops=4 * nc * batch * half * LANES,
-    )
+        flops=0,
+    )
+    turned, _ = lax.optimization_barrier((turned, other_new))
     out_width = shards * rows
     part = jax.ShapeDtypeStruct((batch, out_width), F32)
-    table = pltpu.VMEM((STACK, out_width // LANES, KEEP * units, LANES), F32)
+    table = (STACK, out_width // LANES, KEEP * units, LANES)
+    old_own, old_other, freqs = call(
+        functools.partial(old_kernel, rows, units),
+        (part, part, jax.ShapeDtypeStruct(table, F32)),
+        (
+            lax.axis_index("yhi").reshape(1),
+            mine,
+            theirs,
+            pltpu.with_memory_space_constraint(old_all, pltpu.HBM),
+        ),
+        flops=0,
+        in_specs=[smem, vmem, vmem, pl.BlockSpec(memory_space=pltpu.HBM)],
+        scratch_shapes=[pltpu.VMEM((nz, 2 * size, LANES), BF16), pltpu.SemaphoreType.DMA((2, units // 2 + 1))],
+    )
     here, there = call(
         functools.partial(product_kernel, rows, units),
         (part, part),
-        (lax.axis_index("yhi").reshape(1), sums, turned, mine, theirs, old_all),
-        flops=6 * nc * batch * half * out_width,
-        vmem=20,
-        in_specs=[smem, vmem, vmem, vmem, vmem, pl.BlockSpec(memory_space=pl.ANY)],
-        scratch_shapes=[
-            pltpu.VMEM((nz, 2 * size, LANES), BF16),
-            table,
-            table,
-            pltpu.VMEM((2, 2 * STACK * GROUP, out_width), BF16),
-            pltpu.SemaphoreType.DMA((2, units // 2 + 1)),
-        ],
+        (sums, turned, freqs, old_own, old_other),
+        flops=0,
+        scratch_shapes=[pltpu.VMEM(table, F32), pltpu.VMEM((2, 2 * STACK * GROUP, out_width), BF16)],
     )
     projected = (here + swap(there, "core")).astype(BF16)
     return new_weight, new_momentum[None], projected

time: 122 us -> 117 us (0.959)
  blocking collectives: 23.3 us -> 0 us
  starting transfers between devices: 40.4 us -> 61.1 us
  waiting for transfers between devices: 22.2 us -> 17.1 us
  local copies, waits for them, and re-layouts: 4.91 us -> 6.7 us
  other arithmetic: 3.15 us -> 1.54 us
  Pallas kernels: 13 us -> 14.4 us
    all_to_all x1 -> x0, blocking collectives: 23.3 us -> none  [body(): lax.all_to_all(kept.reshape(nyl * nc * nx, 1, deep * LANES), ('ylo', 'cor...]
    all_to_all x0 -> x1, starting transfers between devices: none -> 16.8 us  [body(): lax.all_to_all(kept.reshape(nyl * nc * nx, 1, deep * LANES), ('ylo', 'cor...]
    all_to_all x1, waiting for transfers between devices: 9.74 us -> 0.01 us  [body(): sums = lax.all_to_all(copies, ('yhi', 'z'), 0, 0, tiled=True)]
    all_to_all x0 -> x1, waiting for transfers between devices: none -> 9.68 us  [body(): lax.all_to_all(kept.reshape(nyl * nc * nx, 1, deep * LANES), ('ylo', 'cor...]
    all_to_all x1, waiting for transfers between devices: 9.15 us -> 4.78 us  [to_all(): return lax.all_to_all(copies, axes, 0, 0, tiled=True)]
    all_to_all x1, starting transfers between devices: 14.4 us -> 17.8 us  [body(): sums = lax.all_to_all(copies, ('yhi', 'z'), 0, 0, tiled=True)]
    ppermute x5 -> x4, waiting for transfers between devices: 3.28 us -> 0.51 us  [swap(): return lax.ppermute(x, axis, [(0, 1), (1, 0)])]
    all_gather x1, waiting for transfers between devices: 0.01 us -> 2.14 us  [body(): old_all = lax.all_gather(duo, 'z', axis=0, tiled=False)]
  transfers between devices with their start and end apart: 8 -> 8, of which waited for: 4 -> 5; matrix products, arithmetic and copies ran while one was open for 4% -> 1% of each run, Pallas kernels for 5% -> 9%
where the time goes in v4:
time: 117 us; the launch traced here: 115 us
  starting transfers between devices  61.1 us (52%)
  waiting for transfers between devices  17.1 us (15%)
  Pallas kernels  14.4 us (12%)
  between operations  14.3 us (12%)
  local copies, waits for them, and re-layouts  6.7 us (6%)
  other arithmetic  1.54 us (1%)
    ppermute x4, starting transfers between devices, swap(): return lax.ppermute(x, axis, [(0, 1), (1, 0)])  22.5 us
    all_to_all x1, starting transfers between devices, body(): sums = lax.all_to_all(copies, ('yhi', 'z'), 0, 0, tiled=True)  17.8 us
    all_to_all x1, starting transfers between devices, body(): lax.all_to_all(kept.reshape(nyl * nc * nx, 1, deep * LANES), ('ylo', 'cor...  16.8 us
    pallas_call x8, Pallas kernels, call(): pl.pallas_call(kernel, out_shape=out_shape, compiler_params=pltpu.Compile...  14.4 us
    all_to_all x1, waiting for transfers between devices, body(): lax.all_to_all(kept.reshape(nyl * nc * nx, 1, deep * LANES), ('ylo', 'cor...  9.68 us
    unnamed x25, local copies, waits for them, and re-layouts  4.8 us
    all_to_all x1, waiting for transfers between devices, to_all(): return lax.all_to_all(copies, axes, 0, 0, tiled=True)  4.78 us
    all_to_all x1, starting transfers between devices, to_all(): return lax.all_to_all(copies, axes, 0, 0, tiled=True)  3.85 us
  transfers between devices with their start and end apart: 8, of which 5 were waited for; matrix products, arithmetic and copies ran while one was open for 1% of the time, Pallas kernels for 9%

profile of v4, /device:TPU:1, one launch (start us, length us, event | category | flops | bytes accessed | tf_op | source)
XLA Modules:
  0.0 115.1 jit_solution(1438825135800890147)
XLA Ops:
  7.2 0.0 copy-start.8
  7.2 0.0 copy-start
  7.2 0.0 copy-start.4
  7.2 0.0 copy-start.1
  7.2 0.0 all-gather.3.cloned.1.call-start
  7.3 1.2 %copy.15 = s32[32,80,8]{0,2,1:T(8,128)S(1)} copy(s32[32,80,8]{1,2,0:T(8,128)} %param.13) | data formatting | bytes 163840 | tf_op args[4]
  8.4 0.1 copy.16
  8.6 0.2 reshape.31.idx
  8.8 0.0 copy-done
  8.8 0.1 shard_map.113
  8.9 8.7 %collective-permute-start = (bf16[720,128]{1,0:T(8,128)(2,1)S(1)}, bf16[720,128]{1,0:T(8,128)(2,1)S(1)}, u32[]{:S(2)}, u32[]{:S(2)}) collective-permute-start(bf16[720,128]{1,0:T(8,128)(2,1)S(1)} %shard_map.113), channel_id=1, source_target_pairs={{0,8},{8,0},{1,9},{9,1},{2,10},{10,2},{3,11},{11,3},{4,12},{12,4},... | collective-permute-start | bytes 552968 | tf_op jit(solution)/shard_map/ppermute | solution.py:286
  17.6 0.0 copy-done.8
  17.6 0.0 copy-done.4
  17.6 0.0 copy-done.1
  17.6 0.0 copy-start.11
  17.6 4.0 %shard_map.112 = (f32[192,128]{1,0:T(8,128)}, f32[32,5120]{1,0:T(8,128)}) custom-call(f32[32,5120]{1,0:T(8,128)S(1)} %bitcast.11, bf16[32,5120]{1,0:T(8,128)(2,1)S(1)} %bitcast.14, s32[160,128]{1,0:T(8,128)S(1)} %reshape.31.idx, f32[128,128]{1,0:T(8,128)S(1)} %copy-done.8), custom_call_target="tpu_custom_call" | custom-call | tf_op jit(solution)/shard_map/pallas_call | solution.py:37
  21.6 0.0 collective-permute-done
  21.6 0.7 pad_maximum_fusion
  22.4 0.0 all-gather.3.cloned.1.call-update
  22.4 16.8 %all-to-all-start = ((f32[64,1,384]{2,1,0:T(1,128)}), f32[64,1,384]{2,1,0:T(1,128)S(1)}, u32[]{:S(2)}, u32[]{:S(2)}) async-start(f32[64,1,384]{2,1,0:T(1,128)} %bitcast.5), calls=%async_computation | async-start | bytes 196608 | tf_op jit(solution)/shard_map/all_to_all | solution.py:329
  39.2 9.7 %all-to-all-done = f32[64,1,384]{2,1,0:T(1,128)S(1)} async-done(((f32[64,1,384]{2,1,0:T(1,128)}), f32[64,1,384]{2,1,0:T(1,128)S(1)}, u32[]{:S(2)}, u32[]{:S(2)}) %all-to-all-start) | async-done | bytes 98336 | tf_op jit(solution)/shard_map/all_to_all | solution.py:329
  48.9 0.1 reduce_sum.9
  49.0 0.6 broadcast_in_dim.4
  49.7 3.9 %all-to-all-start.1 = ((f32[32,1,384]{2,1,0:T(1,128)}), f32[32,1,384]{2,1,0:T(1,128)S(1)}, u32[]{:S(2)}, u32[]{:S(2)}) async-start(f32[32,1,384]{2,1,0:T(1,128)} %broadcast_in_dim.4), calls=%async_computation.1 | async-start | bytes 98304 | tf_op jit(solution)/shard_map/all_to_all | solution.py:48
  53.5 0.0 copy-done.11
  53.6 0.0 copy-start.7
  53.6 0.9 constant_dynamic-slice_fusion
  54.5 3.4 %collective-permute-start.2 = (bf16[128,2560]{1,0:T(8,128)(2,1)}, bf16[128,2560]{1,0:T(8,128)(2,1)S(1)}, u32[]{:S(2)}, u32[]{:S(2)}) collective-permute-start(bf16[128,2560]{1,0:T(8,128)(2,1)} %get-tuple-element.23), channel_id=1, source_target_pairs={{0,16},{16,0},{1,17},{17,1},{2,18},{18,2},{3,19},{19,3},{4,20},{20... | collective-permute-start | bytes 1966088 | tf_op jit(solution)/shard_map/ppermute | solution.py:286
  57.9 4.8 %all-to-all-done.1 = f32[32,1,384]{2,1,0:T(1,128)S(1)} async-done(((f32[32,1,384]{2,1,0:T(1,128)}), f32[32,1,384]{2,1,0:T(1,128)S(1)}, u32[]{:S(2)}, u32[]{:S(2)}) %all-to-all-start.1) | async-done | bytes 49184 | tf_op jit(solution)/shard_map/all_to_all | solution.py:48
  62.7 0.8 shard_map.116
  63.5 17.8 %all-to-all-start.2 = ((bf16[16,80,128]{2,1,0:T(8,128)(2,1)}), bf16[16,80,128]{2,1,0:T(8,128)(2,1)S(1)}, u32[]{:S(2)}, u32[]{:S(2)}) async-start(bf16[16,80,128]{2,1,0:T(8,128)(2,1)} %shard_map.116), calls=%async_computation.2 | async-start | bytes 655360 | tf_op jit(solution)/shard_map/all_to_all | solution.py:340
  81.3 0.7 shard_map.114.mine
  82.0 4.6 %collective-permute-start.1 = (bf16[32,2560]{1,0:T(8,128)(2,1)S(1)}, bf16[32,2560]{1,0:T(8,128)(2,1)S(1)}, u32[]{:S(2)}, u32[]{:S(2)}) collective-permute-start(bf16[32,2560]{1,0:T(8,128)(2,1)S(1)} %shard_map.114.mine), channel_id=1, source_target_pairs={{0,16},{16,0},{1,17},{17,1},{2,18},{18,2},{3,19},{19,3},{4,20},{20... | collective-permute-start | bytes 491528 | tf_op jit(solution)/shard_map/ppermute | solution.py:286
  86.6 0.0 collective-permute-done.2.theirs
  86.7 0.8 shard_map.117.tokens
  87.5 0.1 collective-permute-done.1.theirs
  87.6 2.1 %all-gather.3.cloned.1.call-done = bf16[11520,128]{1,0:T(8,128)(2,1)} async-done(((bf16[1440,128]{1,0:T(8,128)(2,1)}), bf16[11520,128]{1,0:T(8,128)(2,1)}) %all-gather.3.cloned.1.call-update) | async-done | bytes 2949136 | tf_op jit(solution)/shard_map/all_gather | solution.py:331
  89.8 3.8 %shard_map.118 = (f32[128,512]{1,0:T(8,128)S(1)}, f32[128,512]{1,0:T(8,128)S(1)}, f32[4,4,80,128]{3,2,1,0:T(8,128)S(1)}) custom-call(s32[1]{0:T(128)} %bitcast.8.place, bf16[128,2560]{1,0:T(8,128)(2,1)S(1)} %get-tuple-element.24.mine, bf16[128,2560]{1,0:T(8,128)(2,1)S(1)} %collective-permute-done.2.theirs, bf16[8,1440,128]{2,1,0:T(8,128)(2,1)} %bitcast.15), custom_call_target="tpu_custom_call" | custom-call | tf_op jit(solution)/shard_map/pallas_call | solution.py:37
  93.6 0.8 copy-done.2
  94.4 0.7 copy-done.5
  95.1 0.0 all-to-all-done.2.sums
  95.1 1.1 copy-done.3
  96.2 0.9 copy-done.6
  97.2 3.5 %shard_map.119 = (f32[128,512]{1,0:T(8,128)S(1)}, f32[128,512]{1,0:T(8,128)S(1)}) custom-call(bf16[16,80,128]{2,1,0:T(8,128)(2,1)S(1)} %all-to-all-done.2.sums, bf16[256,2560]{1,0:T(8,128)(2,1)S(1)} %shard_map.117.tokens, f32[4,4,80,128]{3,2,1,0:T(8,128)S(1)} %copy-done.3, f32[128,512]{1,0:T(8,128)S(1)} %get-tuple-element.19.old_own, f32[128,512]{1,0:T(8,128)S(1)} %copy-done.6), custom_call_target="tpu_custom_call" | custom-call | tf_op jit(solution)/shard_map/pallas_call | solution.py:37
  100.7 5.8 %collective-permute-start.3 = (f32[128,512]{1,0:T(8,128)S(1)}, f32[128,512]{1,0:T(8,128)S(1)}, u32[]{:S(2)}, u32[]{:S(2)}) collective-permute-start(f32[128,512]{1,0:T(8,128)S(1)} %get-tuple-element.22), channel_id=1, source_target_pairs={{0,16},{16,0},{1,17},{17,1},{2,18},{18,2},{3,19},{19,3},{4,20},{20... | collective-permute-start | bytes 786440 | tf_op jit(solution)/shard_map/ppermute | solution.py:286
  106.4 0.8 shard_map.115
  107.2 0.4 collective-permute-done.3
  107.6 0.7 add_convert_fusion
  (9 shorter events, 0.0 us)
Async XLA Ops:
  7.2 10.4 %copy-start.8 = (f32[128,128]{1,0:T(8,128)S(1)}, f32[128,128]{1,0:T(8,128)}, u32[]{:S(2)}) copy-start(f32[128,128]{1,0:T(8,128)} %constant.28.clone.b2) | copy-start | bytes 196612
  7.2 1.6 %copy-start = (bf16[32,5120]{1,0:T(8,128)(2,1)S(1)}, bf16[32,5120]{1,0:T(8,128)(2,1)}, u32[]{:S(2)}) copy-start(bf16[32,5120]{1,0:T(8,128)(2,1)} %old.1) | copy-start | bytes 983044
  7.2 10.4 %copy-start.4 = (bf16[1,32,5120]{2,1,0:T(8,128)(2,1)S(1)}, bf16[1,32,5120]{2,1,0:T(8,128)(2,1)}, u32[]{:S(2)}) copy-start(bf16[1,32,5120]{2,1,0:T(8,128)(2,1)} %param.11) | copy-start | bytes 983044
  7.2 10.4 %copy-start.1 = (f32[1,32,5120]{2,1,0:T(8,128)S(1)}, f32[1,32,5120]{2,1,0:T(8,128)}, u32[]{:S(2)}) copy-start(f32[1,32,5120]{2,1,0:T(8,128)} %param.10) | copy-start | bytes 1966084
  7.2 82.6 %all-gather.3.cloned.1.call-start = ((), (), s32[]{:S(2)}) async-start(), calls=%async_computation.3 | async-start | bytes 3317760 | tf_op jit(solution)/shard_map/all_gather | solution.py:331
  8.9 12.8 %collective-permute-start = (bf16[720,128]{1,0:T(8,128)(2,1)S(1)}, bf16[720,128]{1,0:T(8,128)(2,1)S(1)}, u32[]{:S(2)}, u32[]{:S(2)}) collective-permute-start(bf16[720,128]{1,0:T(8,128)(2,1)S(1)} %shard_map.113), channel_id=1, source_target_pairs={{0,8},{8,0},{1,9},{9,1},{2,10},{10,2},{3,11},{11,3},{4,12},{12,4},... | collective-permute-start | bytes 552968 | tf_op jit(solution)/shard_map/ppermute | solution.py:286
  17.6 35.9 %copy-start.11 = (bf16[128,5120]{1,0:T(8,128)(2,1)S(1)}, bf16[128,5120]{1,0:T(8,128)(2,1)}, u32[]{:S(2)}) copy-start(bf16[128,5120]{1,0:T(8,128)(2,1)} %param.9) | copy-start | bytes 3932164
  22.4 26.5 %all-to-all-start = ((f32[64,1,384]{2,1,0:T(1,128)}), f32[64,1,384]{2,1,0:T(1,128)S(1)}, u32[]{:S(2)}, u32[]{:S(2)}) async-start(f32[64,1,384]{2,1,0:T(1,128)} %bitcast.5), calls=%async_computation | async-start | bytes 196608 | tf_op jit(solution)/shard_map/all_to_all | solution.py:329
  49.7 13.0 %all-to-all-start.1 = ((f32[32,1,384]{2,1,0:T(1,128)}), f32[32,1,384]{2,1,0:T(1,128)S(1)}, u32[]{:S(2)}, u32[]{:S(2)}) async-start(f32[32,1,384]{2,1,0:T(1,128)} %broadcast_in_dim.4), calls=%async_computation.1 | async-start | bytes 98304 | tf_op jit(solution)/shard_map/all_to_all | solution.py:48
  53.6 27.8 %copy-start.7 = (bf16[384,128]{1,0:T(8,128)(2,1)S(1)}, bf16[384,128]{1,0:T(8,128)(2,1)}, u32[]{:S(2)}) copy-start(bf16[384,128]{1,0:T(8,128)(2,1)} %constant.29.clone.b2) | copy-start | bytes 294916
  54.5 32.1 %copy-start.9 = (bf16[128,128]{1,0:T(8,128)(2,1)S(1)}, bf16[128,128]{1,0:T(8,128)(2,1)}, u32[]{:S(2)}) copy-start(bf16[128,128]{1,0:T(8,128)(2,1)} %constant.31.clone.low) | copy-start | bytes 98308
  54.5 32.1 %copy-start.10 = (bf16[128,128]{1,0:T(8,128)(2,1)S(1)}, bf16[128,128]{1,0:T(8,128)(2,1)}, u32[]{:S(2)}) copy-start(bf16[128,128]{1,0:T(8,128)(2,1)} %constant.30.clone.high) | copy-start | bytes 98308
  54.5 32.1 %collective-permute-start.2 = (bf16[128,2560]{1,0:T(8,128)(2,1)}, bf16[128,2560]{1,0:T(8,128)(2,1)S(1)}, u32[]{:S(2)}, u32[]{:S(2)}) collective-permute-start(bf16[128,2560]{1,0:T(8,128)(2,1)} %get-tuple-element.23), channel_id=1, source_target_pairs={{0,16},{16,0},{1,17},{17,1},{2,18},{18,2},{3,19},{19,3},{4,20},{20... | collective-permute-start | bytes 1966088 | tf_op jit(solution)/shard_map/ppermute | solution.py:286
  63.5 31.6 %all-to-all-start.2 = ((bf16[16,80,128]{2,1,0:T(8,128)(2,1)}), bf16[16,80,128]{2,1,0:T(8,128)(2,1)S(1)}, u32[]{:S(2)}, u32[]{:S(2)}) async-start(bf16[16,80,128]{2,1,0:T(8,128)(2,1)} %shard_map.116), calls=%async_computation.2 | async-start | bytes 655360 | tf_op jit(solution)/shard_map/all_to_all | solution.py:340
  82.0 5.6 %collective-permute-start.1 = (bf16[32,2560]{1,0:T(8,128)(2,1)S(1)}, bf16[32,2560]{1,0:T(8,128)(2,1)S(1)}, u32[]{:S(2)}, u32[]{:S(2)}) collective-permute-start(bf16[32,2560]{1,0:T(8,128)(2,1)S(1)} %shard_map.114.mine), channel_id=1, source_target_pairs={{0,16},{16,0},{1,17},{17,1},{2,18},{18,2},{3,19},{19,3},{4,20},{20... | collective-permute-start | bytes 491528 | tf_op jit(solution)/shard_map/ppermute | solution.py:286
  93.6 0.9 copy-start.2
  94.4 0.7 copy-start.5
  95.1 1.1 copy-start.3
  96.2 0.9 copy-start.6
  100.7 6.9 %collective-permute-start.3 = (f32[128,512]{1,0:T(8,128)S(1)}, f32[128,512]{1,0:T(8,128)S(1)}, u32[]{:S(2)}, u32[]{:S(2)}) collective-permute-start(f32[128,512]{1,0:T(8,128)S(1)} %get-tuple-element.22), channel_id=1, source_target_pairs={{0,16},{16,0},{1,17},{17,1},{2,18},{18,2},{3,19},{19,3},{4,20},{20... | collective-permute-start | bytes 786440 | tf_op jit(solution)/shard_map/ppermute | solution.py:286
Sparse Core Ops, SparseCore 0:
  22.5 67.2 all-gather.2

commit v5 on v4

--- a/solution.py
+++ b/solution.py
@@ -67,25 +67,6 @@
     high = x.astype(BF16)
     low = (x - high.astype(F32)).astype(BF16)
     return jnp.concatenate([high, low, high] if order else [high, high, low], axis=axis)
-
-
-def join_kernel(units, core, weight, idx, out):
-    rows, width = weight.shape
-    tiles = width // 2 // LANES
-    for c in range(tiles):
-        at = pl.multiple_of(core[0] * (width // 2) + c * LANES, LANES)
-        out[c * rows : (c + 1) * rows, :] = weight[:, pl.ds(at, LANES)]
-    total_units = idx.shape[0] // KEEP
-    block = [idx[pl.ds(core[0] * units + u, KEEP, stride=total_units), :].astype(F32) for u in range(units)]
-    full = units // STACK
-    parts = []
-    for r in range(full):
-        for t in range(STACK):
-            parts.append(regroup(block[r * STACK : (r + 1) * STACK], rows, t))
-    if full * STACK < units:
-        for t in range(0, STACK, 2):
-            parts.append(pick([(block[full * STACK + s % 2], t + s // 2) for s in range(STACK)], rows))
-    out[tiles * rows :, :] = jnp.concatenate(parts, axis=0).astype(BF16)
 
 
 def local_kernel(cores, mom, grad, idx, b2, kept, new_mom, kept_wide):
@@ -169,9 +150,10 @@
         out[:, cols] = y.astype(BF16)
 
 
-def pack_kernel(units, tot, out):
+def pack_kernel(units, core, tot, idx, out):
     deep = tot.shape[0] // (STACK * KEEP)
     full = units // STACK
+    rows = LANES // STACK
     lane = lax.broadcasted_iota(jnp.int32, (KEEP, LANES), 1)
     blocks = [[tot[pl.ds(t * KEEP * deep + r, KEEP, stride=deep), :] for t in range(STACK)] for r in range(deep)]
     parts = []
@@ -181,70 +163,29 @@
         for t in range(0, STACK, 2):
             upper = pltpu.roll(blocks[full][t + 1], LANES // 2, axis=1)
             parts.append(jnp.where(lane < LANES // 2, blocks[full][t], upper))
+    total_units = idx.shape[0] // KEEP
+    block = [idx[pl.ds(core[0] * units + u, KEEP, stride=total_units), :].astype(F32) for u in range(units)]
+    for r in range(full):
+        for t in range(STACK):
+            parts.append(regroup(block[r * STACK : (r + 1) * STACK], rows, t))
+    if full < deep:
+        for t in range(0, STACK, 2):
+            parts.append(pick([(block[full * STACK + s % 2], t + s // 2) for s in range(STACK)], rows))
     packed = jnp.concatenate(parts, axis=0).astype(BF16)
     for f in range(out.shape[0]):
         out[f] = packed
 
 
-def old_kernel(rows, units, place, mine, theirs, source, own, other, freqs, weight, sems):
-    nz, size, _ = source.shape
-    size = size // 2
-    shards = 2 * nz
-    lines = KEEP * units
-    steps = units // 2
-    high = STACK * rows
-    fold = LANES // rows
-
-    def copy(h, k):
-        at = h * size + (steps * high if k == steps else k * high)
-        part = pl.ds(at, lines if k == steps else high)
-        return pltpu.make_async_copy(source.at[:, part, :], weight.at[:, part, :], sems.at[h, k])
-
-    for k in [steps] + list(range(steps)):
-        for h in range(2):
-            copy(h, k).start()
-
-    def start_of(y):
-        h = place[0] if y == 0 else 1 - place[0]
-        return h * size
-
-    for h in range(2):
-        copy(h, steps).wait()
-    for q in range(shards // fold):
-        blocks = []
-        for f in range(fold * q, fold * (q + 1)):
-            at = pl.multiple_of(start_of(f // nz) + steps * high, 16)
-            blocks.append(weight[f % nz, pl.ds(at, lines), :].astype(F32))
-        for b in range(STACK):
-            freqs[b, q] = regroup(blocks, rows, b)
-    depth = 2 * STACK * GROUP
-    wide = nz * rows
-    for g in range(steps):
-        for h in range(2):
-            copy(h, g).wait()
-        cols = pl.ds(g * depth, depth)
-        for y in range(2):
-            at = start_of(y) + g * high
-            tiles = []
-            for c in range(STACK):
-                line = pl.multiple_of(at + c * rows, 16)
-                tiles.append(jnp.concatenate([weight[z, pl.ds(line, rows), :] for z in range(nz)], axis=0))
-            w = jnp.concatenate(tiles, axis=1)
-            lanes = pl.ds(y * wide, wide)
-            for x, out in ((mine, own), (theirs, other)):
-                part = lax.dot_general(x[:, cols], w, NT, preferred_element_type=F32) * (1.0 - STEP * DECAY)
-                out[:, lanes] = part if g == 0 else out[:, lanes] + part
-
-
-def product_kernel(rows, units, sums, tokens, freqs, old_own, old_other, own, other, vals, spec):
-    shards, lines, _ = sums.shape
-    batch = own.shape[0]
+def direction_kernel(rows, units, both, tokens, out, acc, vals, freqs, spec, sem):
+    shards = both.shape[0]
+    lines = both.shape[1] // 2
     fold = LANES // rows
     full = units // STACK
     for q in range(shards // fold):
-        blocks = [sums[fold * q + f].astype(F32) for f in range(fold)]
+        blocks = [both[fold * q + f].astype(F32) for f in range(fold)]
         for b in range(STACK):
-            vals[b, q] = regroup(blocks, rows, b)
+            vals[b, q] = regroup([x[:lines] for x in blocks], rows, b)
+            freqs[b, q] = regroup([x[lines:] for x in blocks], rows, b)
     pack = 16
     freq = lax.broadcasted_iota(jnp.int32, (GROUP, LANES), 0).astype(F32).astype(BF16)
     freq = [freq[k * pack : (k + 1) * pack] for k in range(GROUP // pack)]
@@ -269,11 +210,44 @@
                         w = jnp.broadcast_to(where[j : j + 1], (pack, LANES)).astype(BF16)
                         s = [jnp.where(f == w, v, old) for f, old in zip(freq, s)]
                     spec[slot, pl.ds((2 * t + c2) * GROUP, GROUP), pl.ds(q * LANES, LANES)] = jnp.concatenate(s, axis=0)
-        cols = pl.ds(g * depth, depth)
-        for p, (out, old) in enumerate(((own, old_own), (other, old_other))):
-            x = tokens[p * batch : (p + 1) * batch, cols]
-            part = lax.dot_general(x, spec[slot], NN, preferred_element_type=F32)
-            out[...] = part + (old[...] if g == 0 else out[...])
+        part = lax.dot_general(
+            tokens[:, pl.ds(g * depth, depth)], spec[slot], NN, preferred_element_type=F32
+        )
+        acc[...] = part if g == 0 else acc[...] + part
+    done = pltpu.make_async_copy(acc, out, sem)
+    done.start()
+    done.wait()
+
+
+def old_kernel(rows, place, mine, theirs, source, change, own, other, weight, added, sems):
+    nz, _, width = source.shape
+    step = STACK * LANES
+    wide = nz * rows
+
+    def copy(k):
+        cols = pl.ds(k * step, step)
+        return pltpu.make_async_copy(source.at[:, :, cols], weight.at[:, :, cols], sems.at[k])
+
+    steps = width // step
+    batch = mine.shape[0]
+    for k in range(steps):
+        copy(k).start()
+    rest = pltpu.make_async_copy(change, added, sems.at[steps])
+    rest.start()
+    for k in range(width // step):
+        copy(k).wait()
+        cols = pl.ds(k * step, step)
+        for y in range(2):
+            h = place[0] if y == 0 else 1 - place[0]
+            lines = pl.ds(pl.multiple_of(h * rows, 16), rows)
+            w = jnp.concatenate([weight[z, lines, cols] for z in range(nz)], axis=0)
+            lanes = pl.ds(y * wide, wide)
+            for x, out in ((mine, own), (theirs, other)):
+                part = lax.dot_general(x[:, cols], w, NT, preferred_element_type=F32) * (1.0 - STEP * DECAY)
+                out[:, lanes] = part if k == 0 else out[:, lanes] + part
+    rest.wait()
+    own[...] += added[:batch, :]
+    other[...] += added[batch:, :]
 
 
 def sides_kernel(core, mine, theirs, new_weight):
@@ -300,19 +274,12 @@
     low = (pair - high.astype(np.float32)).astype(jnp.bfloat16)
     core = lax.axis_index("core")
 
+    near = lax.dynamic_slice(weight, (0, core * half), (rows, half))
+    far = swap(near, "yhi")
     order = kept_index.reshape(rows, groups, STACK, 2, KEEP).transpose(4, 1, 3, 2, 0).reshape(KEEP * nc * units, LANES)
     smem = pl.BlockSpec(memory_space=pltpu.SMEM)
     vmem = pl.BlockSpec(memory_space=pltpu.VMEM)
     core_ref = core.reshape(1)
-    size = half // LANES * rows + KEEP * units
-    near = call(
-        functools.partial(join_kernel, units),
-        jax.ShapeDtypeStruct((size, LANES), BF16),
-        (core_ref, weight, order),
-        flops=0,
-        in_specs=[smem, vmem, vmem],
-    )
-    far = swap(near, "yhi")
     kept, new_momentum = call(
         functools.partial(local_kernel, nc),
         (
@@ -333,11 +300,12 @@
     total = to_all(jnp.sum(pieces, axis=0), ("ylo", "x"), nyl * nx).reshape(lines, LANES)
     copies = call(
         functools.partial(pack_kernel, units),
-        jax.ShapeDtypeStruct((shards, KEEP * units, LANES), BF16),
-        (total,),
-        flops=0,
-    )
-    sums = lax.all_to_all(copies, ("yhi", "z"), 0, 0, tiled=True)
+        jax.ShapeDtypeStruct((shards, 2 * KEEP * units, LANES), BF16),
+        (core_ref, total, order),
+        flops=20_000_000_000,
+        in_specs=[smem, vmem, vmem],
+    )
+    both = lax.all_to_all(copies, ("yhi", "z"), 0, 0, tiled=True)
 
     own_new = call(
         weight_kernel,
@@ -367,26 +335,40 @@
     turned, _ = lax.optimization_barrier((turned, other_new))
     out_width = shards * rows
     part = jax.ShapeDtypeStruct((batch, out_width), F32)
-    table = (STACK, out_width // LANES, KEEP * units, LANES)
-    old_own, old_other, freqs = call(
-        functools.partial(old_kernel, rows, units),
-        (part, part, jax.ShapeDtypeStruct(table, F32)),
+    table = pltpu.VMEM((STACK, out_width // LANES, KEEP * units, LANES), F32)
+    hbm = pl.BlockSpec(memory_space=pltpu.HBM)
+    whole = pltpu.VMEM((nc * batch, out_width), F32)
+    change = call(
+        functools.partial(direction_kernel, rows, units),
+        pltpu.HBM((nc * batch, out_width), F32),
+        (both, turned),
+        flops=0,
+        out_specs=hbm,
+        scratch_shapes=[
+            whole,
+            table,
+            table,
+            pltpu.VMEM((2, 2 * STACK * GROUP, out_width), BF16),
+            pltpu.SemaphoreType.DMA(()),
+        ],
+    )
+    here, there = call(
+        functools.partial(old_kernel, rows),
+        (part, part),
         (
             lax.axis_index("yhi").reshape(1),
             mine,
             theirs,
             pltpu.with_memory_space_constraint(old_all, pltpu.HBM),
+            pltpu.with_memory_space_constraint(change, pltpu.HBM),
         ),
         flops=0,
-        in_specs=[smem, vmem, vmem, pl.BlockSpec(memory_space=pltpu.HBM)],
-        scratch_shapes=[pltpu.VMEM((nz, 2 * size, LANES), BF16), pltpu.SemaphoreType.DMA((2, units // 2 + 1))],
-    )
-    here, there = call(
-        functools.partial(product_kernel, rows, units),
-        (part, part),
-        (sums, turned, freqs, old_own, old_other),
-        flops=0,
-        scratch_shapes=[pltpu.VMEM(table, F32), pltpu.VMEM((2, 2 * STACK * GROUP, out_width), BF16)],
+        in_specs=[smem, vmem, vmem, hbm, hbm],
+        scratch_shapes=[
+            pltpu.VMEM((nz, 2 * rows, half), BF16),
+            whole,
+            pltpu.SemaphoreType.DMA((half // (STACK * LANES) + 1,)),
+        ],
     )
     projected = (here + swap(there, "core")).astype(BF16)
     return new_weight, new_momentum[None], projected

time: 117 us -> 121 us (1.034)
  the two profiles are of different devices: /device:TPU:1 before, /device:TPU:17 now
where the time goes in v5:
time: 121 us; the launch traced here: 120 us
  blocking collectives  35.3 us (29%)
  starting transfers between devices  34.3 us (28%)
  Pallas kernels  15.9 us (13%)
  waiting for transfers between devices  15.7 us (13%)
  between operations  14.3 us (12%)
  local copies, waits for them, and re-layouts  3.41 us (3%)
  other arithmetic  1.54 us (1%)
    all_to_all x1, blocking collectives, body(): lax.all_to_all(kept.reshape(nyl * nc * nx, 1, deep * LANES), ('ylo', 'cor...  23.3 us
    all_to_all x1, starting transfers between devices, body(): both = lax.all_to_all(copies, ('yhi', 'z'), 0, 0, tiled=True)  18 us
    ppermute x4, starting transfers between devices, swap(): return lax.ppermute(x, axis, [(0, 1), (1, 0)])  16.3 us
    pallas_call x7, Pallas kernels, call(): pl.pallas_call(kernel, out_shape=out_shape, compiler_params=pltpu.Compile...  15.9 us
    all_to_all x1, waiting for transfers between devices, body(): both = lax.all_to_all(copies, ('yhi', 'z'), 0, 0, tiled=True)  14 us
    all_to_all x1, blocking collectives, to_all(): return lax.all_to_all(copies, axes, 0, 0, tiled=True)  12 us
  transfers between devices with their start and end apart: 6, of which 3 were waited for; matrix products, arithmetic and copies ran while one was open for 2% of the time, Pallas kernels for 10%

profile of v5, /device:TPU:17, one launch (start us, length us, event | category | flops | bytes accessed | tf_op | source)
XLA Modules:
  0.0 120.4 jit_solution(10311159400025779274)
XLA Ops:
  7.2 0.0 copy-start.4
  7.2 0.0 copy-start.1
  7.2 0.0 copy-start.2
  7.2 0.0 all-gather.3.cloned.1.call-start
  7.2 1.0 constant_dynamic-slice_fusion.2
  8.3 7.0 %collective-permute-start = (bf16[32,2560]{1,0:T(8,128)(2,1)S(1)}, bf16[32,2560]{1,0:T(8,128)(2,1)S(1)}, u32[]{:S(2)}, u32[]{:S(2)}) collective-permute-start(bf16[32,2560]{1,0:T(8,128)(2,1)S(1)} %constant_dynamic-slice_fusion.2), channel_id=1, source_target_pairs={{0,8},{8,0},{1,9},{9,1},{2,10},{10,2},{3,11},{11,3},{4,12},{12,4},... | collective-permute-start | bytes 491528 | tf_op jit(solution)/shard_map/ppermute | solution.py:260
  15.3 1.1 copy.15
  16.4 0.1 copy.16
  16.5 0.2 reshape.31.idx
  16.7 0.0 copy-done.4
  16.7 0.0 copy-done.1
  16.7 0.0 copy-done.2
  16.7 4.0 %shard_map.112 = (f32[192,128]{1,0:T(8,128)S(1)}, f32[32,5120]{1,0:T(8,128)}) custom-call(f32[32,5120]{1,0:T(8,128)S(1)} %bitcast.11, bf16[32,5120]{1,0:T(8,128)(2,1)S(1)} %bitcast.12, s32[160,128]{1,0:T(8,128)S(1)} %reshape.31.idx, f32[128,128]{1,0:T(8,128)S(1)} %copy-done.4), custom_call_target="tpu_custom_call" | custom-call | tf_op jit(solution)/shard_map/pallas_call | solution.py:37
  20.7 1.1 collective-permute-done
  21.8 0.7 pad_maximum_fusion
  22.5 0.0 all-gather.3.cloned.1.call-update
  22.6 23.3 %all_to_all.15 = f32[64,1,384]{2,1,0:T(1,128)S(1)} all-to-all(f32[64,1,384]{2,1,0:T(1,128)S(1)} %bitcast.15), channel_id=1, replica_groups=mesh['x'=8,'ylo'=4,'core'=2,'yhi'=2,'z'=8] {'ylo','core','x'}, dimensions={0} | all-to-all | bytes 196608 | tf_op jit(solution)/shard_map/all_to_all | solution.py:296
  45.8 0.1 reduce_sum.9
  46.0 12.0 %all_to_all.16 = f32[32,1,384]{2,1,0:T(1,128)S(1)} all-to-all(f32[32,1,384]{2,1,0:T(1,128)S(1)} %broadcast_in_dim.4), channel_id=1, replica_groups=mesh['x'=8,'ylo'=4,'core'=2,'yhi'=2,'z'=8] {'ylo','x'}, dimensions={0} | all-to-all | bytes 98304 | tf_op jit(solution)/shard_map/all_to_all | solution.py:48
  58.0 1.0 shard_map.115
  58.9 0.0 copy-start.7
  58.9 18.0 %all-to-all-start.2 = ((bf16[16,160,128]{2,1,0:T(8,128)(2,1)}), bf16[16,160,128]{2,1,0:T(8,128)(2,1)S(1)}, u32[]{:S(2)}, u32[]{:S(2)}) async-start(bf16[16,160,128]{2,1,0:T(8,128)(2,1)} %shard_map.115), calls=%async_computation.2 | async-start | bytes 1310720 | tf_op jit(solution)/shard_map/all_to_all | solution.py:308
  76.9 0.0 copy-done.7
  77.0 0.0 copy-start
  77.0 0.0 copy-start.3
  77.0 0.0 copy-start.5
  77.0 0.0 copy-start.6
  77.0 0.9 constant_dynamic-slice_fusion
  77.9 4.3 %collective-permute-start.2 = (bf16[128,2560]{1,0:T(8,128)(2,1)}, bf16[128,2560]{1,0:T(8,128)(2,1)S(1)}, u32[]{:S(2)}, u32[]{:S(2)}) collective-permute-start(bf16[128,2560]{1,0:T(8,128)(2,1)} %get-tuple-element.17), channel_id=1, source_target_pairs={{0,16},{16,0},{1,17},{17,1},{2,18},{18,2},{3,19},{19,3},{4,20},{20... | collective-permute-start | bytes 1966088 | tf_op jit(solution)/shard_map/ppermute | solution.py:260
  82.2 0.0 copy-done
  82.2 0.0 copy-done.3
  82.3 0.7 shard_map.113.mine
  82.9 1.9 %collective-permute-start.1 = (bf16[32,2560]{1,0:T(8,128)(2,1)S(1)}, bf16[32,2560]{1,0:T(8,128)(2,1)}, u32[]{:S(2)}, u32[]{:S(2)}) collective-permute-start(bf16[32,2560]{1,0:T(8,128)(2,1)S(1)} %shard_map.113.mine), channel_id=1, source_target_pairs={{0,16},{16,0},{1,17},{17,1},{2,18},{18,2},{3,19},{19,3},{4,20},{20... | collective-permute-start | bytes 491528 | tf_op jit(solution)/shard_map/ppermute | solution.py:260
  84.8 0.0 collective-permute-done.2.theirs
  84.9 0.0 copy-done.5
  84.9 0.0 copy-done.6
  84.9 0.8 shard_map.116.tokens
  85.7 0.6 collective-permute-done.1.theirs
  86.3 14.0 %all-to-all-done.2.both = bf16[16,160,128]{2,1,0:T(8,128)(2,1)S(1)} async-done(((bf16[16,160,128]{2,1,0:T(8,128)(2,1)}), bf16[16,160,128]{2,1,0:T(8,128)(2,1)S(1)}, u32[]{:S(2)}, u32[]{:S(2)}) %all-to-all-start.2) | async-done | bytes 655392 | tf_op jit(solution)/shard_map/all_to_all | solution.py:308
  100.3 4.3 %shard_map.117.change = f32[256,512]{1,0:T(8,128)} custom-call(bf16[16,160,128]{2,1,0:T(8,128)(2,1)S(1)} %all-to-all-done.2.both, bf16[256,2560]{1,0:T(8,128)(2,1)S(1)} %shard_map.116.tokens), custom_call_target="tpu_custom_call" | custom-call | tf_op jit(solution)/shard_map/pallas_call | solution.py:37
  104.6 0.0 all-gather.3.cloned.1.call-done
  104.6 3.5 %shard_map.118 = (f32[128,512]{1,0:T(8,128)S(1)}, f32[128,512]{1,0:T(8,128)S(1)}) custom-call(s32[1]{0:T(128)} %bitcast.8.place, bf16[128,2560]{1,0:T(8,128)(2,1)S(1)} %get-tuple-element.18.mine, bf16[128,2560]{1,0:T(8,128)(2,1)S(1)} %collective-permute-done.2.theirs, bf16[8,64,2560]{2,1,0:T(8,128)(2,1)} %bitcast.16, f32[256,512]{1,0:T(8,128)} %shard_map.117.change), custom_call_target="tpu_custom_call" | custom-call | tf_op jit(solution)/shard_map/pallas_call | solution.py:37
  108.2 3.0 %collective-permute-start.3 = (f32[128,512]{1,0:T(8,128)S(1)}, f32[128,512]{1,0:T(8,128)S(1)}, u32[]{:S(2)}, u32[]{:S(2)}) collective-permute-start(f32[128,512]{1,0:T(8,128)S(1)} %get-tuple-element.16), channel_id=1, source_target_pairs={{0,16},{16,0},{1,17},{17,1},{2,18},{18,2},{3,19},{19,3},{4,20},{20... | collective-permute-start | bytes 786440 | tf_op jit(solution)/shard_map/ppermute | solution.py:260
  111.2 1.7 %shard_map.114 = bf16[32,5120]{1,0:T(8,128)(2,1)} custom-call(s32[1]{0:T(128)} %bitcast.core, bf16[32,2560]{1,0:T(8,128)(2,1)S(1)} %shard_map.113.mine, bf16[32,2560]{1,0:T(8,128)(2,1)} %collective-permute-done.1.theirs), custom_call_target="tpu_custom_call" | custom-call | tf_op jit(solution)/shard_map/pallas_call | solution.py:37
  112.9 0.0 collective-permute-done.3
  112.9 0.7 add_convert_fusion
  (1 shorter events, 0.0 us)
Async XLA Ops:
  7.2 9.5 %copy-start.4 = (f32[128,128]{1,0:T(8,128)S(1)}, f32[128,128]{1,0:T(8,128)}, u32[]{:S(2)}) copy-start(f32[128,128]{1,0:T(8,128)} %constant.28.clone.b2) | copy-start | bytes 196612
  7.2 9.5 %copy-start.1 = (f32[1,32,5120]{2,1,0:T(8,128)S(1)}, f32[1,32,5120]{2,1,0:T(8,128)}, u32[]{:S(2)}) copy-start(f32[1,32,5120]{2,1,0:T(8,128)} %param.10) | copy-start | bytes 1966084
  7.2 9.5 %copy-start.2 = (bf16[1,32,5120]{2,1,0:T(8,128)(2,1)S(1)}, bf16[1,32,5120]{2,1,0:T(8,128)(2,1)}, u32[]{:S(2)}) copy-start(bf16[1,32,5120]{2,1,0:T(8,128)(2,1)} %param.11) | copy-start | bytes 983044
  7.2 97.4 %all-gather.3.cloned.1.call-start = ((), (), s32[]{:S(2)}) async-start(), calls=%async_computation.3 | async-start | bytes 2949120 | tf_op jit(solution)/shard_map/all_gather | solution.py:298
  8.3 13.5 %collective-permute-start = (bf16[32,2560]{1,0:T(8,128)(2,1)S(1)}, bf16[32,2560]{1,0:T(8,128)(2,1)S(1)}, u32[]{:S(2)}, u32[]{:S(2)}) collective-permute-start(bf16[32,2560]{1,0:T(8,128)(2,1)S(1)} %constant_dynamic-slice_fusion.2), channel_id=1, source_target_pairs={{0,8},{8,0},{1,9},{9,1},{2,10},{10,2},{3,11},{11,3},{4,12},{12,4},... | collective-permute-start | bytes 491528 | tf_op jit(solution)/shard_map/ppermute | solution.py:260
  58.9 18.0 %copy-start.7 = (bf16[128,5120]{1,0:T(8,128)(2,1)S(1)}, bf16[128,5120]{1,0:T(8,128)(2,1)}, u32[]{:S(2)}) copy-start(bf16[128,5120]{1,0:T(8,128)(2,1)} %param.9) | copy-start | bytes 3932164
  58.9 41.4 %all-to-all-start.2 = ((bf16[16,160,128]{2,1,0:T(8,128)(2,1)}), bf16[16,160,128]{2,1,0:T(8,128)(2,1)S(1)}, u32[]{:S(2)}, u32[]{:S(2)}) async-start(bf16[16,160,128]{2,1,0:T(8,128)(2,1)} %shard_map.115), calls=%async_computation.2 | async-start | bytes 1310720 | tf_op jit(solution)/shard_map/all_to_all | solution.py:308
  77.0 5.3 %copy-start = (bf16[32,5120]{1,0:T(8,128)(2,1)S(1)}, bf16[32,5120]{1,0:T(8,128)(2,1)}, u32[]{:S(2)}) copy-start(bf16[32,5120]{1,0:T(8,128)(2,1)} %old.1) | copy-start | bytes 983044
  77.0 5.3 %copy-start.3 = (bf16[384,128]{1,0:T(8,128)(2,1)S(1)}, bf16[384,128]{1,0:T(8,128)(2,1)}, u32[]{:S(2)}) copy-start(bf16[384,128]{1,0:T(8,128)(2,1)} %constant.29.clone.b2) | copy-start | bytes 294916
  77.0 7.9 %copy-start.5 = (bf16[128,128]{1,0:T(8,128)(2,1)S(1)}, bf16[128,128]{1,0:T(8,128)(2,1)}, u32[]{:S(2)}) copy-start(bf16[128,128]{1,0:T(8,128)(2,1)} %constant.30.clone.high) | copy-start | bytes 98308
  77.0 7.9 %copy-start.6 = (bf16[128,128]{1,0:T(8,128)(2,1)S(1)}, bf16[128,128]{1,0:T(8,128)(2,1)}, u32[]{:S(2)}) copy-start(bf16[128,128]{1,0:T(8,128)(2,1)} %constant.31.clone.low) | copy-start | bytes 98308
  77.9 6.9 %collective-permute-start.2 = (bf16[128,2560]{1,0:T(8,128)(2,1)}, bf16[128,2560]{1,0:T(8,128)(2,1)S(1)}, u32[]{:S(2)}, u32[]{:S(2)}) collective-permute-start(bf16[128,2560]{1,0:T(8,128)(2,1)} %get-tuple-element.17), channel_id=1, source_target_pairs={{0,16},{16,0},{1,17},{17,1},{2,18},{18,2},{3,19},{19,3},{4,20},{20... | collective-permute-start | bytes 1966088 | tf_op jit(solution)/shard_map/ppermute | solution.py:260
  82.9 3.4 %collective-permute-start.1 = (bf16[32,2560]{1,0:T(8,128)(2,1)S(1)}, bf16[32,2560]{1,0:T(8,128)(2,1)}, u32[]{:S(2)}, u32[]{:S(2)}) collective-permute-start(bf16[32,2560]{1,0:T(8,128)(2,1)S(1)} %shard_map.113.mine), channel_id=1, source_target_pairs={{0,16},{16,0},{1,17},{17,1},{2,18},{18,2},{3,19},{19,3},{4,20},{20... | collective-permute-start | bytes 491528 | tf_op jit(solution)/shard_map/ppermute | solution.py:260
  108.2 4.7 %collective-permute-start.3 = (f32[128,512]{1,0:T(8,128)S(1)}, f32[128,512]{1,0:T(8,128)S(1)}, u32[]{:S(2)}, u32[]{:S(2)}) collective-permute-start(f32[128,512]{1,0:T(8,128)S(1)} %get-tuple-element.16), channel_id=1, source_target_pairs={{0,16},{16,0},{1,17},{17,1},{2,18},{18,2},{3,19},{19,3},{4,20},{20... | collective-permute-start | bytes 786440 | tf_op jit(solution)/shard_map/ppermute | solution.py:260
Sparse Core Ops, SparseCore 0:
  22.7 61.4 all-gather.2

commit v6 on v2

--- a/solution.py
+++ b/solution.py
@@ -34,12 +34,11 @@
 
 
 def call(kernel, out_shape, args, flops, vmem=12, **kw):
-    size = sum(a.size * a.dtype.itemsize for a in args)
     return pl.pallas_call(
         kernel,
         out_shape=out_shape,
         compiler_params=pltpu.CompilerParams(vmem_limit_bytes=vmem * 1024 * 1024),
-        cost_estimate=pl.CostEstimate(flops=flops, bytes_accessed=size, transcendentals=0),
+        cost_estimate=pl.CostEstimate(flops=flops, bytes_accessed=0, transcendentals=0),
         **kw,
     )(*args)
 
@@ -70,9 +69,13 @@
     return jnp.concatenate([high, low, high] if order else [high, high, low], axis=axis)
 
 
-def index_kernel(units, core, idx, out):
+def join_kernel(units, core, weight, idx, out):
+    rows, width = weight.shape
+    tiles = width // 2 // LANES
+    for c in range(tiles):
+        at = pl.multiple_of(core[0] * (width // 2) + c * LANES, LANES)
+        out[c * rows : (c + 1) * rows, :] = weight[:, pl.ds(at, LANES)]
     total_units = idx.shape[0] // KEEP
-    rows = LANES // STACK
     block = [idx[pl.ds(core[0] * units + u, KEEP, stride=total_units), :].astype(F32) for u in range(units)]
     full = units // STACK
     parts = []
@@ -82,17 +85,7 @@
     if full * STACK < units:
         for t in range(0, STACK, 2):
             parts.append(pick([(block[full * STACK + s % 2], t + s // 2) for s in range(STACK)], rows))
-    out[...] = jnp.concatenate(parts, axis=0).astype(BF16)
-
-
-def join_kernel(own, far, own_idx, far_idx, out):
-    rows, width = own.shape
-    tiles = width // LANES
-    size = out.shape[0] // 2
-    for h, (weight, idx) in enumerate(((own, own_idx), (far, far_idx))):
-        for c in range(tiles):
-            out[h * size + c * rows : h * size + (c + 1) * rows, :] = weight[:, c * LANES : (c + 1) * LANES]
-        out[h * size + tiles * rows : (h + 1) * size, :] = idx[...]
+    out[tiles * rows :, :] = jnp.concatenate(parts, axis=0).astype(BF16)
 
 
 def local_kernel(cores, mom, grad, idx, b2, kept, new_mom, kept_wide):
@@ -136,7 +129,7 @@
 
 
 def weight_kernel(core, tot, idx, b2, old, new, tot_wide):
-    rows, width = old.shape
+    rows, width = new.shape
     deep = tot.shape[0] // (STACK * KEEP)
     span = KEEP * deep
     total_units = idx.shape[0] // KEEP
@@ -157,11 +150,12 @@
                 spec = jnp.where(freq == where[j : j + 1], value[j : j + 1], spec)
             parts.append(spec)
         direction = lax.dot_general(
-            jnp.concatenate(parts, axis=0), b2[...], TN, precision=HIGHEST, preferred_element_type=F32
+            split(jnp.concatenate(parts, axis=0), 0, True), b2[...], TN, preferred_element_type=F32
         )
         for t in range(STACK):
             cols = pl.ds((STACK * g + t) * LANES, LANES)
-            kept_part = old[:, cols].astype(F32) * (1.0 - STEP * DECAY)
+            at = pl.multiple_of(core[0] * width + (STACK * g + t) * LANES, LANES)
+            kept_part = old[:, pl.ds(at, LANES)].astype(F32) * (1.0 - STEP * DECAY)
             new[:, cols] = (kept_part - STEP * direction[t * rows : (t + 1) * rows]).astype(BF16)
 
 
@@ -274,6 +268,12 @@
                 out[:, lanes] = part if g == 0 else out[:, lanes] + part
 
 
+def sides_kernel(core, mine, theirs, new_weight):
+    half = mine.shape[1]
+    new_weight[:, pl.ds(pl.multiple_of(core[0] * half, LANES), half)] = mine[...]
+    new_weight[:, pl.ds(pl.multiple_of((1 - core[0]) * half, LANES), half)] = theirs[...]
+
+
 def swap(x, axis):
     return lax.ppermute(x, axis, [(0, 1), (1, 0)])
 
@@ -292,83 +292,88 @@
     low = (pair - high.astype(np.float32)).astype(jnp.bfloat16)
     core = lax.axis_index("core")
 
-    own = lax.dynamic_slice(weight, (0, core * half), (rows, half))
-    far = swap(own, "yhi")
     order = kept_index.reshape(rows, groups, STACK, 2, KEEP).transpose(4, 1, 3, 2, 0).reshape(KEEP * nc * units, LANES)
     smem = pl.BlockSpec(memory_space=pltpu.SMEM)
     vmem = pl.BlockSpec(memory_space=pltpu.VMEM)
     core_ref = core.reshape(1)
-    idx_own = call(
-        functools.partial(index_kernel, units),
-        jax.ShapeDtypeStruct((KEEP * units, LANES), BF16),
-        (core_ref, order),
-        flops=1000,
-        in_specs=[smem, vmem],
-    )
-    idx_far = swap(idx_own, "yhi")
-    lines = STACK * KEEP * deep
+    size = half // LANES * rows + KEEP * units
+    near = call(
+        functools.partial(join_kernel, units),
+        jax.ShapeDtypeStruct((size, LANES), BF16),
+        (core_ref, weight, order),
+        flops=0,
+        in_specs=[smem, vmem, vmem],
+    )
+    far = swap(near, "yhi")
     kept, new_momentum = call(
         functools.partial(local_kernel, nc),
         (
-            jax.ShapeDtypeStruct((nc * lines, LANES), F32),
+            jax.ShapeDtypeStruct((nc * STACK * KEEP * deep, LANES), F32),
             jax.ShapeDtypeStruct((rows, width), F32),
         ),
         (momentum[0], gradient[0], order, jnp.asarray(pair)),
-        flops=12 * rows * width * LANES,
+        flops=0,
         scratch_shapes=[pltpu.VMEM((STACK, deep, nc * KEEP, LANES), F32)],
     )
-    far, idx_far, kept = lax.optimization_barrier((far, idx_far, kept))
-    size = half // LANES * rows + KEEP * units
-    duo = call(
-        join_kernel,
-        jax.ShapeDtypeStruct((2 * size, LANES), BF16),
-        (own, far, idx_own, idx_far),
-        flops=1000,
-    )
-    duo, kept = lax.optimization_barrier((duo, kept))
+    far, _ = lax.optimization_barrier((far, kept))
+    duo = jnp.concatenate([near, far], axis=0)
+
+    pieces = lax.all_to_all(kept.reshape(nyl * nc * nx, 1, deep * LANES), ("ylo", "core", "x"), 0, 0, tiled=True)
+    pieces, _ = lax.optimization_barrier((pieces, duo))
     old_all = lax.all_gather(duo, "z", axis=0, tiled=False)
-
-    pieces = lax.all_to_all(kept.reshape(nyl * nc * nx, 1, deep * LANES), ("ylo", "core", "x"), 0, 0, tiled=True)
+    lines = STACK * KEEP * deep
     total = to_all(jnp.sum(pieces, axis=0), ("ylo", "x"), nyl * nx).reshape(lines, LANES)
     copies = call(
         functools.partial(pack_kernel, units),
         jax.ShapeDtypeStruct((shards, KEEP * units, LANES), BF16),
         (total,),
-        flops=1000,
+        flops=0,
     )
     sums = lax.all_to_all(copies, ("yhi", "z"), 0, 0, tiled=True)
-
-    mine = lax.dynamic_slice(tokens, (0, core * half), (batch, half))
-    theirs = swap(lax.dynamic_slice(tokens, (0, (1 - core) * half), (batch, half)), "core")
 
     own_new = call(
         weight_kernel,
         jax.ShapeDtypeStruct((rows, half), BF16),
-        (core_ref, total, order, jnp.asarray(pair), own),
-        flops=12 * rows * half * LANES,
+        (core_ref, total, order, jnp.asarray(np.concatenate([high, high, low], axis=0)), weight),
+        flops=0,
         in_specs=[smem, vmem, vmem, vmem, vmem],
         scratch_shapes=[pltpu.VMEM((STACK, KEEP * deep, LANES), F32)],
     )
     other_new = swap(own_new, "core")
-    left = core == 0
-    new_weight = jnp.concatenate([jnp.where(left, own_new, other_new), jnp.where(left, other_new, own_new)], axis=1)
-
+    new_weight = call(
+        sides_kernel,
+        jax.ShapeDtypeStruct((rows, width), BF16),
+        (core_ref, own_new, other_new),
+        flops=0,
+        in_specs=[smem, vmem, vmem],
+    )
+
+    mine = lax.dynamic_slice(tokens, (0, core * half), (batch, half))
+    theirs = swap(lax.dynamic_slice(tokens, (0, (1 - core) * half), (batch, half)), "core")
     turned = call(
         tokens_kernel,
         jax.ShapeDtypeStruct((nc * batch, half), BF16),
         (mine, theirs, jnp.asarray(high), jnp.asarray(low)),
-        flops=4 * nc * batch * half * LANES,
-    )
+        flops=0,
+    )
+    turned, _ = lax.optimization_barrier((turned, other_new))
     out_width = shards * rows
     part = jax.ShapeDtypeStruct((batch, out_width), F32)
     table = pltpu.VMEM((STACK, out_width // LANES, KEEP * units, LANES), F32)
     here, there = call(
         functools.partial(product_kernel, rows, units),
         (part, part),
-        (lax.axis_index("yhi").reshape(1), sums, turned, mine, theirs, old_all),
-        flops=6 * nc * batch * half * out_width,
+        (
+            lax.axis_index("yhi").reshape(1),
+            sums,
+            turned,
+            mine,
+            theirs,
+            pltpu.with_memory_space_constraint(old_all, pltpu.HBM),
+        ),
+        flops=0,
         vmem=20,
-        in_specs=[smem, vmem, vmem, vmem, vmem, pl.BlockSpec(memory_space=pl.ANY)],
+        in_specs=[smem, vmem, vmem, vmem, vmem, pl.BlockSpec(memory_space=pltpu.HBM)],
         scratch_shapes=[
             pltpu.VMEM((nz, 2 * size, LANES), BF16),
             table,

time: 122 us -> 115 us (0.943)
  blocking collectives: 23.3 us -> 0 us
  starting transfers between devices: 40.4 us -> 61.4 us
  local copies, waits for them, and re-layouts: 4.91 us -> 3.1 us
  other arithmetic: 3.15 us -> 1.55 us
  waiting for transfers between devices: 22.2 us -> 20.6 us
    all_to_all x1 -> x0, blocking collectives: 23.3 us -> none  [body(): lax.all_to_all(kept.reshape(nyl * nc * nx, 1, deep * LANES), ('ylo', 'cor...]
    all_to_all x0 -> x1, starting transfers between devices: none -> 16.8 us  [body(): lax.all_to_all(kept.reshape(nyl * nc * nx, 1, deep * LANES), ('ylo', 'cor...]
    all_to_all x0 -> x1, waiting for transfers between devices: none -> 9.68 us  [body(): lax.all_to_all(kept.reshape(nyl * nc * nx, 1, deep * LANES), ('ylo', 'cor...]
    all_to_all x1, waiting for transfers between devices: 9.15 us -> 4.79 us  [to_all(): return lax.all_to_all(copies, axes, 0, 0, tiled=True)]
    all_to_all x1, waiting for transfers between devices: 9.74 us -> 5.61 us  [body(): sums = lax.all_to_all(copies, ('yhi', 'z'), 0, 0, tiled=True)]
    all_to_all x1, starting transfers between devices: 14.4 us -> 17.8 us  [body(): sums = lax.all_to_all(copies, ('yhi', 'z'), 0, 0, tiled=True)]
    ppermute x5 -> x4, waiting for transfers between devices: 3.28 us -> 0.51 us  [swap(): return lax.ppermute(x, axis, [(0, 1), (1, 0)])]
    unnamed x19 -> x17, local copies, waits for them, and re-layouts: 3.84 us -> 1.21 us
  transfers between devices with their start and end apart: 8 -> 8, of which waited for: 4 -> 5; matrix products, arithmetic and copies ran while one was open for 4% -> 1% of each run, Pallas kernels for 5% -> 6%
where the time goes in v6:
time: 115 us; the launch traced here: 114 us
  starting transfers between devices  61.4 us (53%)
  waiting for transfers between devices  20.6 us (18%)
  between operations  14.3 us (12%)
  Pallas kernels  13.4 us (12%)
  local copies, waits for them, and re-layouts  3.1 us (3%)
  other arithmetic  1.55 us (1%)
    ppermute x4, starting transfers between devices, swap(): return lax.ppermute(x, axis, [(0, 1), (1, 0)])  22.8 us
    all_to_all x1, starting transfers between devices, body(): sums = lax.all_to_all(copies, ('yhi', 'z'), 0, 0, tiled=True)  17.8 us
    all_to_all x1, starting transfers between devices, body(): lax.all_to_all(kept.reshape(nyl * nc * nx, 1, deep * LANES), ('ylo', 'cor...  16.8 us
    pallas_call x7, Pallas kernels, call(): pl.pallas_call(kernel, out_shape=out_shape, compiler_params=pltpu.Compile...  13.4 us
    all_to_all x1, waiting for transfers between devices, body(): lax.all_to_all(kept.reshape(nyl * nc * nx, 1, deep * LANES), ('ylo', 'cor...  9.68 us
    all_to_all x1, waiting for transfers between devices, body(): sums = lax.all_to_all(copies, ('yhi', 'z'), 0, 0, tiled=True)  5.61 us
    all_to_all x1, waiting for transfers between devices, to_all(): return lax.all_to_all(copies, axes, 0, 0, tiled=True)  4.79 us
    all_to_all x1, starting transfers between devices, to_all(): return lax.all_to_all(copies, axes, 0, 0, tiled=True)  3.85 us
  transfers between devices with their start and end apart: 8, of which 5 were waited for; matrix products, arithmetic and copies ran while one was open for 1% of the time, Pallas kernels for 6%

profile of v6, /device:TPU:1, one launch (start us, length us, event | category | flops | bytes accessed | tf_op | source)
XLA Modules:
  0.0 114.3 jit_solution(13249069928921965508)
XLA Ops:
  7.2 0.0 copy-start.4
  7.2 0.0 copy-start
  7.2 0.0 copy-start.2
  7.2 0.0 copy-start.1
  7.2 0.0 all-gather.3.cloned.1.call-start
  7.3 1.2 %copy.15 = s32[32,80,8]{0,2,1:T(8,128)S(1)} copy(s32[32,80,8]{1,2,0:T(8,128)} %param.13) | data formatting | bytes 163840 | tf_op args[4]
  8.4 0.1 copy.16
  8.6 0.2 reshape.31.idx
  8.8 0.0 copy-done
  8.8 0.1 shard_map.113
  8.9 8.7 %collective-permute-start = (bf16[720,128]{1,0:T(8,128)(2,1)S(1)}, bf16[720,128]{1,0:T(8,128)(2,1)S(1)}, u32[]{:S(2)}, u32[]{:S(2)}) collective-permute-start(bf16[720,128]{1,0:T(8,128)(2,1)S(1)} %shard_map.113), channel_id=1, source_target_pairs={{0,8},{8,0},{1,9},{9,1},{2,10},{10,2},{3,11},{11,3},{4,12},{12,4},... | collective-permute-start | bytes 552968 | tf_op jit(solution)/shard_map/ppermute | solution.py:278
  17.6 0.0 copy-done.4
  17.6 0.0 copy-done.2
  17.6 0.0 copy-done.1
  17.6 0.0 copy-start.7
  17.6 4.0 %shard_map.112 = (f32[192,128]{1,0:T(8,128)}, f32[32,5120]{1,0:T(8,128)}) custom-call(f32[32,5120]{1,0:T(8,128)S(1)} %bitcast.11, bf16[32,5120]{1,0:T(8,128)(2,1)S(1)} %bitcast.14, s32[160,128]{1,0:T(8,128)S(1)} %reshape.31.idx, f32[128,128]{1,0:T(8,128)S(1)} %copy-done.4), custom_call_target="tpu_custom_call" | custom-call | tf_op jit(solution)/shard_map/pallas_call | solution.py:37
  21.6 0.0 collective-permute-done
  21.6 0.8 pad_maximum_fusion
  22.4 0.0 all-gather.3.cloned.1.call-update
  22.4 16.8 %all-to-all-start = ((f32[64,1,384]{2,1,0:T(1,128)}), f32[64,1,384]{2,1,0:T(1,128)S(1)}, u32[]{:S(2)}, u32[]{:S(2)}) async-start(f32[64,1,384]{2,1,0:T(1,128)} %bitcast.5), calls=%async_computation | async-start | bytes 196608 | tf_op jit(solution)/shard_map/all_to_all | solution.py:321
  39.3 9.7 %all-to-all-done = f32[64,1,384]{2,1,0:T(1,128)S(1)} async-done(((f32[64,1,384]{2,1,0:T(1,128)}), f32[64,1,384]{2,1,0:T(1,128)S(1)}, u32[]{:S(2)}, u32[]{:S(2)}) %all-to-all-start) | async-done | bytes 98336 | tf_op jit(solution)/shard_map/all_to_all | solution.py:321
  48.9 0.1 reduce_sum.9
  49.0 0.6 broadcast_in_dim.4
  49.7 3.9 %all-to-all-start.1 = ((f32[32,1,384]{2,1,0:T(1,128)}), f32[32,1,384]{2,1,0:T(1,128)S(1)}, u32[]{:S(2)}, u32[]{:S(2)}) async-start(f32[32,1,384]{2,1,0:T(1,128)} %broadcast_in_dim.4), calls=%async_computation.1 | async-start | bytes 98304 | tf_op jit(solution)/shard_map/all_to_all | solution.py:48
  53.6 0.0 copy-done.7
  53.6 0.0 copy-start.3
  53.6 0.9 constant_dynamic-slice_fusion
  54.5 0.0 copy-start.5
  54.5 0.0 copy-start.6
  54.5 3.4 %collective-permute-start.2 = (bf16[128,2560]{1,0:T(8,128)(2,1)}, bf16[128,2560]{1,0:T(8,128)(2,1)S(1)}, u32[]{:S(2)}, u32[]{:S(2)}) collective-permute-start(bf16[128,2560]{1,0:T(8,128)(2,1)} %get-tuple-element.17), channel_id=1, source_target_pairs={{0,16},{16,0},{1,17},{17,1},{2,18},{18,2},{3,19},{19,3},{4,20},{20... | collective-permute-start | bytes 1966088 | tf_op jit(solution)/shard_map/ppermute | solution.py:278
  57.9 4.8 %all-to-all-done.1 = f32[32,1,384]{2,1,0:T(1,128)S(1)} async-done(((f32[32,1,384]{2,1,0:T(1,128)}), f32[32,1,384]{2,1,0:T(1,128)S(1)}, u32[]{:S(2)}, u32[]{:S(2)}) %all-to-all-start.1) | async-done | bytes 49184 | tf_op jit(solution)/shard_map/all_to_all | solution.py:48
  62.7 0.8 shard_map.116
  63.5 17.8 %all-to-all-start.2 = ((bf16[16,80,128]{2,1,0:T(8,128)(2,1)}), bf16[16,80,128]{2,1,0:T(8,128)(2,1)S(1)}, u32[]{:S(2)}, u32[]{:S(2)}) async-start(bf16[16,80,128]{2,1,0:T(8,128)(2,1)} %shard_map.116), calls=%async_computation.2 | async-start | bytes 655360 | tf_op jit(solution)/shard_map/all_to_all | solution.py:332
  81.3 0.0 copy-done.3
  81.3 0.7 shard_map.114.mine
  82.0 4.6 %collective-permute-start.1 = (bf16[32,2560]{1,0:T(8,128)(2,1)S(1)}, bf16[32,2560]{1,0:T(8,128)(2,1)S(1)}, u32[]{:S(2)}, u32[]{:S(2)}) collective-permute-start(bf16[32,2560]{1,0:T(8,128)(2,1)S(1)} %shard_map.114.mine), channel_id=1, source_target_pairs={{0,16},{16,0},{1,17},{17,1},{2,18},{18,2},{3,19},{19,3},{4,20},{20... | collective-permute-start | bytes 491528 | tf_op jit(solution)/shard_map/ppermute | solution.py:278
  86.6 0.0 collective-permute-done.2.theirs
  86.6 0.0 copy-done.5
  86.7 0.0 copy-done.6
  86.7 0.8 shard_map.117.tokens
  87.5 0.1 collective-permute-done.1.theirs
  87.6 5.6 %all-to-all-done.2.sums = bf16[16,80,128]{2,1,0:T(8,128)(2,1)S(1)} async-done(((bf16[16,80,128]{2,1,0:T(8,128)(2,1)}), bf16[16,80,128]{2,1,0:T(8,128)(2,1)S(1)}, u32[]{:S(2)}, u32[]{:S(2)}) %all-to-all-start.2) | async-done | bytes 327712 | tf_op jit(solution)/shard_map/all_to_all | solution.py:332
  93.2 0.0 all-gather.3.cloned.1.call-done
  93.2 6.3 %shard_map.118 = (f32[128,512]{1,0:T(8,128)S(1)}, f32[128,512]{1,0:T(8,128)S(1)}) custom-call(s32[1]{0:T(128)} %bitcast.8.place, bf16[16,80,128]{2,1,0:T(8,128)(2,1)S(1)} %all-to-all-done.2.sums, bf16[256,2560]{1,0:T(8,128)(2,1)S(1)} %shard_map.117.tokens, bf16[128,2560]{1,0:T(8,128)(2,1)S(1)} %get-tuple-element.18.mine, ...), custom_call_target="tpu_custom_call" | custom-call | tf_op jit(solution)/shard_map/pallas_call | solution.py:37
  99.5 6.0 %collective-permute-start.3 = (f32[128,512]{1,0:T(8,128)S(1)}, f32[128,512]{1,0:T(8,128)S(1)}, u32[]{:S(2)}, u32[]{:S(2)}) collective-permute-start(f32[128,512]{1,0:T(8,128)S(1)} %get-tuple-element.16), channel_id=1, source_target_pairs={{0,16},{16,0},{1,17},{17,1},{2,18},{18,2},{3,19},{19,3},{4,20},{20... | collective-permute-start | bytes 786440 | tf_op jit(solution)/shard_map/ppermute | solution.py:278
  105.6 0.8 shard_map.115
  106.4 0.4 collective-permute-done.3
  106.7 0.7 add_convert_fusion
Async XLA Ops:
  7.2 10.4 %copy-start.4 = (f32[128,128]{1,0:T(8,128)S(1)}, f32[128,128]{1,0:T(8,128)}, u32[]{:S(2)}) copy-start(f32[128,128]{1,0:T(8,128)} %constant.28.clone.b2) | copy-start | bytes 196612
  7.2 1.6 %copy-start = (bf16[32,5120]{1,0:T(8,128)(2,1)S(1)}, bf16[32,5120]{1,0:T(8,128)(2,1)}, u32[]{:S(2)}) copy-start(bf16[32,5120]{1,0:T(8,128)(2,1)} %old.1) | copy-start | bytes 983044
  7.2 10.4 %copy-start.2 = (bf16[1,32,5120]{2,1,0:T(8,128)(2,1)S(1)}, bf16[1,32,5120]{2,1,0:T(8,128)(2,1)}, u32[]{:S(2)}) copy-start(bf16[1,32,5120]{2,1,0:T(8,128)(2,1)} %param.11) | copy-start | bytes 983044
  7.2 10.4 %copy-start.1 = (f32[1,32,5120]{2,1,0:T(8,128)S(1)}, f32[1,32,5120]{2,1,0:T(8,128)}, u32[]{:S(2)}) copy-start(f32[1,32,5120]{2,1,0:T(8,128)} %param.10) | copy-start | bytes 1966084
  7.2 86.0 %all-gather.3.cloned.1.call-start = ((), (), s32[]{:S(2)}) async-start(), calls=%async_computation.3 | async-start | bytes 3317760 | tf_op jit(solution)/shard_map/all_gather | solution.py:323
  8.9 12.8 %collective-permute-start = (bf16[720,128]{1,0:T(8,128)(2,1)S(1)}, bf16[720,128]{1,0:T(8,128)(2,1)S(1)}, u32[]{:S(2)}, u32[]{:S(2)}) collective-permute-start(bf16[720,128]{1,0:T(8,128)(2,1)S(1)} %shard_map.113), channel_id=1, source_target_pairs={{0,8},{8,0},{1,9},{9,1},{2,10},{10,2},{3,11},{11,3},{4,12},{12,4},... | collective-permute-start | bytes 552968 | tf_op jit(solution)/shard_map/ppermute | solution.py:278
  17.6 35.9 %copy-start.7 = (bf16[128,5120]{1,0:T(8,128)(2,1)S(1)}, bf16[128,5120]{1,0:T(8,128)(2,1)}, u32[]{:S(2)}) copy-start(bf16[128,5120]{1,0:T(8,128)(2,1)} %param.9) | copy-start | bytes 3932164
  22.4 26.5 %all-to-all-start = ((f32[64,1,384]{2,1,0:T(1,128)}), f32[64,1,384]{2,1,0:T(1,128)S(1)}, u32[]{:S(2)}, u32[]{:S(2)}) async-start(f32[64,1,384]{2,1,0:T(1,128)} %bitcast.5), calls=%async_computation | async-start | bytes 196608 | tf_op jit(solution)/shard_map/all_to_all | solution.py:321
  49.7 13.0 %all-to-all-start.1 = ((f32[32,1,384]{2,1,0:T(1,128)}), f32[32,1,384]{2,1,0:T(1,128)S(1)}, u32[]{:S(2)}, u32[]{:S(2)}) async-start(f32[32,1,384]{2,1,0:T(1,128)} %broadcast_in_dim.4), calls=%async_computation.1 | async-start | bytes 98304 | tf_op jit(solution)/shard_map/all_to_all | solution.py:48
  53.6 27.8 %copy-start.3 = (bf16[384,128]{1,0:T(8,128)(2,1)S(1)}, bf16[384,128]{1,0:T(8,128)(2,1)}, u32[]{:S(2)}) copy-start(bf16[384,128]{1,0:T(8,128)(2,1)} %constant.29.clone.b2) | copy-start | bytes 294916
  54.5 32.1 %copy-start.5 = (bf16[128,128]{1,0:T(8,128)(2,1)S(1)}, bf16[128,128]{1,0:T(8,128)(2,1)}, u32[]{:S(2)}) copy-start(bf16[128,128]{1,0:T(8,128)(2,1)} %constant.31.clone.low) | copy-start | bytes 98308
  54.5 32.1 %copy-start.6 = (bf16[128,128]{1,0:T(8,128)(2,1)S(1)}, bf16[128,128]{1,0:T(8,128)(2,1)}, u32[]{:S(2)}) copy-start(bf16[128,128]{1,0:T(8,128)(2,1)} %constant.30.clone.high) | copy-start | bytes 98308
  54.5 32.1 %collective-permute-start.2 = (bf16[128,2560]{1,0:T(8,128)(2,1)}, bf16[128,2560]{1,0:T(8,128)(2,1)S(1)}, u32[]{:S(2)}, u32[]{:S(2)}) collective-permute-start(bf16[128,2560]{1,0:T(8,128)(2,1)} %get-tuple-element.17), channel_id=1, source_target_pairs={{0,16},{16,0},{1,17},{17,1},{2,18},{18,2},{3,19},{19,3},{4,20},{20... | collective-permute-start | bytes 1966088 | tf_op jit(solution)/shard_map/ppermute | solution.py:278
  63.5 29.7 %all-to-all-start.2 = ((bf16[16,80,128]{2,1,0:T(8,128)(2,1)}), bf16[16,80,128]{2,1,0:T(8,128)(2,1)S(1)}, u32[]{:S(2)}, u32[]{:S(2)}) async-start(bf16[16,80,128]{2,1,0:T(8,128)(2,1)} %shard_map.116), calls=%async_computation.2 | async-start | bytes 655360 | tf_op jit(solution)/shard_map/all_to_all | solution.py:332
  82.0 5.6 %collective-permute-start.1 = (bf16[32,2560]{1,0:T(8,128)(2,1)S(1)}, bf16[32,2560]{1,0:T(8,128)(2,1)S(1)}, u32[]{:S(2)}, u32[]{:S(2)}) collective-permute-start(bf16[32,2560]{1,0:T(8,128)(2,1)S(1)} %shard_map.114.mine), channel_id=1, source_target_pairs={{0,16},{16,0},{1,17},{17,1},{2,18},{18,2},{3,19},{19,3},{4,20},{20... | collective-permute-start | bytes 491528 | tf_op jit(solution)/shard_map/ppermute | solution.py:278
  99.5 7.2 %collective-permute-start.3 = (f32[128,512]{1,0:T(8,128)S(1)}, f32[128,512]{1,0:T(8,128)S(1)}, u32[]{:S(2)}, u32[]{:S(2)}) collective-permute-start(f32[128,512]{1,0:T(8,128)S(1)} %get-tuple-element.16), channel_id=1, source_target_pairs={{0,16},{16,0},{1,17},{17,1},{2,18},{18,2},{3,19},{19,3},{4,20},{20... | collective-permute-start | bytes 786440 | tf_op jit(solution)/shard_map/ppermute | solution.py:278
Sparse Core Ops, SparseCore 0:
  22.5 67.1 all-gather.2

commit v7 on v6

--- a/solution.py
+++ b/solution.py
@@ -252,20 +252,19 @@
         for h in range(2):
             copy(h, g).wait()
         cols = pl.ds(g * depth, depth)
-        for y in range(2):
-            at = start_of(y) + g * high
-            tiles = []
-            for c in range(STACK):
-                line = pl.multiple_of(at + c * rows, 16)
-                tiles.append(jnp.concatenate([weight[z, pl.ds(line, rows), :] for z in range(nz)], axis=0))
-            w = jnp.concatenate(tiles, axis=1)
-            lanes = pl.ds(y * wide, wide)
-            for p, (x, out) in enumerate(((mine, own), (theirs, other))):
-                part = lax.dot_general(x[:, cols], w, NT, preferred_element_type=F32) * (1.0 - STEP * DECAY)
-                part += lax.dot_general(
-                    tokens[p * batch : (p + 1) * batch, cols], spec[slot, :, lanes], NN, preferred_element_type=F32
-                )
-                out[:, lanes] = part if g == 0 else out[:, lanes] + part
+        tiles = []
+        for c in range(STACK):
+            column = []
+            for y in range(2):
+                line = pl.multiple_of(start_of(y) + g * high + c * rows, 16)
+                column += [weight[z, pl.ds(line, rows), :] for z in range(nz)]
+            tiles.append(jnp.concatenate(column, axis=0))
+        x = jnp.concatenate([mine[:, cols], theirs[:, cols]], axis=0)
+        part = lax.dot_general(x, jnp.concatenate(tiles, axis=1), NT, preferred_element_type=F32) * (1.0 - STEP * DECAY)
+        part += lax.dot_general(tokens[:, cols], spec[slot], NN, preferred_element_type=F32)
+        for p, out in enumerate((own, other)):
+            half = part[p * batch : (p + 1) * batch]
+            out[...] = half if g == 0 else out[...] + half
 
 
 def sides_kernel(core, mine, theirs, new_weight):
@@ -304,7 +303,8 @@
         flops=0,
         in_specs=[smem, vmem, vmem],
     )
-    far = swap(near, "yhi")
+    last = nyh * nyl - 1
+    far = lax.ppermute(near, ("ylo", "yhi"), [(i, last - i) for i in range(last + 1)])
     kept, new_momentum = call(
         functools.partial(local_kernel, nc),
         (

time: 115 us -> 112 us (0.974)
  starting transfers between devices: 61.4 us -> 56.3 us
  waiting for transfers between devices: 20.6 us -> 23.4 us
    ppermute x4 -> x3, starting transfers between devices: 22.8 us -> 14.1 us  [swap(): return lax.ppermute(x, axis, [(0, 1), (1, 0)])]
    ppermute x0 -> x1, starting transfers between devices: none -> 6.72 us  [body(): lax.ppermute(near, ('ylo', 'yhi'), [(i, last - i) for i in range(last + 1)])]
    all_to_all x1, starting transfers between devices: 16.8 us -> 13.3 us  [body(): lax.all_to_all(kept.reshape(nyl * nc * nx, 1, deep * LANES), ('ylo', 'cor...]
    ppermute x0 -> x1, waiting for transfers between devices: none -> 2.86 us  [body(): lax.ppermute(near, ('ylo', 'yhi'), [(i, last - i) for i in range(last + 1)])]
  transfers between devices with their start and end apart: 8 -> 8, of which waited for: 5 -> 6; matrix products, arithmetic and copies ran while one was open for 1% -> 2% of each run, Pallas kernels for 6% -> 6%
where the time goes in v7:
time: 112 us; the launch traced here: 111 us
  starting transfers between devices  56.3 us (50%)
  waiting for transfers between devices  23.4 us (21%)
  between operations  14.3 us (13%)
  Pallas kernels  12.5 us (11%)
  local copies, waits for them, and re-layouts  3.1 us (3%)
  other arithmetic  1.55 us (1%)
    all_to_all x1, starting transfers between devices, body(): sums = lax.all_to_all(copies, ('yhi', 'z'), 0, 0, tiled=True)  18.2 us
    ppermute x3, starting transfers between devices, swap(): return lax.ppermute(x, axis, [(0, 1), (1, 0)])  14.1 us
    all_to_all x1, starting transfers between devices, body(): lax.all_to_all(kept.reshape(nyl * nc * nx, 1, deep * LANES), ('ylo', 'cor...  13.3 us
    pallas_call x7, Pallas kernels, call(): pl.pallas_call(kernel, out_shape=out_shape, compiler_params=pltpu.Compile...  12.5 us
    all_to_all x1, waiting for transfers between devices, body(): lax.all_to_all(kept.reshape(nyl * nc * nx, 1, deep * LANES), ('ylo', 'cor...  9.68 us
    ppermute x1, starting transfers between devices, body(): lax.ppermute(near, ('ylo', 'yhi'), [(i, last - i) for i in range(last + 1)])  6.72 us
    all_to_all x1, waiting for transfers between devices, body(): sums = lax.all_to_all(copies, ('yhi', 'z'), 0, 0, tiled=True)  5.55 us
    all_to_all x1, waiting for transfers between devices, to_all(): return lax.all_to_all(copies, axes, 0, 0, tiled=True)  4.79 us
  transfers between devices with their start and end apart: 8, of which 6 were waited for; matrix products, arithmetic and copies ran while one was open for 2% of the time, Pallas kernels for 6%

profile of v7, /device:TPU:1, one launch (start us, length us, event | category | flops | bytes accessed | tf_op | source)
XLA Modules:
  0.0 111.0 jit_solution(2649221559414630676)
XLA Ops:
  7.2 0.0 copy-start.4
  7.2 0.0 copy-start
  7.2 0.0 copy-start.2
  7.2 0.0 copy-start.1
  7.2 0.0 all-gather.3.cloned.1.call-start
  7.3 1.2 %copy.15 = s32[32,80,8]{0,2,1:T(8,128)S(1)} copy(s32[32,80,8]{1,2,0:T(8,128)} %param.13) | data formatting | bytes 163840 | tf_op args[4]
  8.4 0.1 copy.16
  8.6 0.2 reshape.31.idx
  8.8 0.0 copy-done
  8.8 0.1 shard_map.113
  8.9 6.7 %collective-permute-start = (bf16[720,128]{1,0:T(8,128)(2,1)S(1)}, bf16[720,128]{1,0:T(8,128)(2,1)S(1)}, u32[]{:S(2)}, u32[]{:S(2)}) collective-permute-start(bf16[720,128]{1,0:T(8,128)(2,1)S(1)} %shard_map.113), channel_id=1, source_target_pairs={{0,104},{8,96},{32,72},{40,64},{64,40},{72,32},{96,8},{104,0},{1,1... | collective-permute-start | bytes 552968 | tf_op jit(solution)/shard_map/ppermute | solution.py:307
  15.6 0.0 copy-done.4
  15.6 0.0 copy-done.2
  15.6 0.0 copy-done.1
  15.6 0.0 copy-start.7
  15.6 4.0 %shard_map.112 = (f32[192,128]{1,0:T(8,128)}, f32[32,5120]{1,0:T(8,128)}) custom-call(f32[32,5120]{1,0:T(8,128)S(1)} %bitcast.11, bf16[32,5120]{1,0:T(8,128)(2,1)S(1)} %bitcast.14, s32[160,128]{1,0:T(8,128)S(1)} %reshape.31.idx, f32[128,128]{1,0:T(8,128)S(1)} %copy-done.4), custom_call_target="tpu_custom_call" | custom-call | tf_op jit(solution)/shard_map/pallas_call | solution.py:37
  19.6 2.9 %collective-permute-done = bf16[720,128]{1,0:T(8,128)(2,1)S(1)} collective-permute-done((bf16[720,128]{1,0:T(8,128)(2,1)S(1)}, bf16[720,128]{1,0:T(8,128)(2,1)S(1)}, u32[]{:S(2)}, u32[]{:S(2)}) %collective-permute-start) | collective-permute-done | bytes 184352 | tf_op jit(solution)/shard_map/ppermute | solution.py:307
  22.5 0.8 pad_maximum_fusion
  23.2 0.0 all-gather.3.cloned.1.call-update
  23.2 13.3 %all-to-all-start = ((f32[64,1,384]{2,1,0:T(1,128)}), f32[64,1,384]{2,1,0:T(1,128)S(1)}, u32[]{:S(2)}, u32[]{:S(2)}) async-start(f32[64,1,384]{2,1,0:T(1,128)} %bitcast.5), calls=%async_computation | async-start | bytes 196608 | tf_op jit(solution)/shard_map/all_to_all | solution.py:321
  36.6 9.7 %all-to-all-done = f32[64,1,384]{2,1,0:T(1,128)S(1)} async-done(((f32[64,1,384]{2,1,0:T(1,128)}), f32[64,1,384]{2,1,0:T(1,128)S(1)}, u32[]{:S(2)}, u32[]{:S(2)}) %all-to-all-start) | async-done | bytes 98336 | tf_op jit(solution)/shard_map/all_to_all | solution.py:321
  46.2 0.1 reduce_sum.9
  46.3 0.6 broadcast_in_dim.4
  47.0 3.9 %all-to-all-start.1 = ((f32[32,1,384]{2,1,0:T(1,128)}), f32[32,1,384]{2,1,0:T(1,128)S(1)}, u32[]{:S(2)}, u32[]{:S(2)}) async-start(f32[32,1,384]{2,1,0:T(1,128)} %broadcast_in_dim.4), calls=%async_computation.1 | async-start | bytes 98304 | tf_op jit(solution)/shard_map/all_to_all | solution.py:48
  50.9 0.0 copy-done.7
  50.9 0.0 copy-start.3
  50.9 0.9 constant_dynamic-slice_fusion
  51.8 0.0 copy-start.5
  51.8 0.0 copy-start.6
  51.8 3.4 %collective-permute-start.2 = (bf16[128,2560]{1,0:T(8,128)(2,1)}, bf16[128,2560]{1,0:T(8,128)(2,1)S(1)}, u32[]{:S(2)}, u32[]{:S(2)}) collective-permute-start(bf16[128,2560]{1,0:T(8,128)(2,1)} %get-tuple-element.17), channel_id=1, source_target_pairs={{0,16},{16,0},{1,17},{17,1},{2,18},{18,2},{3,19},{19,3},{4,20},{20... | collective-permute-start | bytes 1966088 | tf_op jit(solution)/shard_map/ppermute | solution.py:277
  55.2 4.8 %all-to-all-done.1 = f32[32,1,384]{2,1,0:T(1,128)S(1)} async-done(((f32[32,1,384]{2,1,0:T(1,128)}), f32[32,1,384]{2,1,0:T(1,128)S(1)}, u32[]{:S(2)}, u32[]{:S(2)}) %all-to-all-start.1) | async-done | bytes 49184 | tf_op jit(solution)/shard_map/all_to_all | solution.py:48
  60.0 0.8 shard_map.116
  60.8 18.2 %all-to-all-start.2 = ((bf16[16,80,128]{2,1,0:T(8,128)(2,1)}), bf16[16,80,128]{2,1,0:T(8,128)(2,1)S(1)}, u32[]{:S(2)}, u32[]{:S(2)}) async-start(bf16[16,80,128]{2,1,0:T(8,128)(2,1)} %shard_map.116), calls=%async_computation.2 | async-start | bytes 655360 | tf_op jit(solution)/shard_map/all_to_all | solution.py:332
  79.0 0.0 copy-done.3
  79.0 0.7 shard_map.114.mine
  79.7 4.6 %collective-permute-start.1 = (bf16[32,2560]{1,0:T(8,128)(2,1)S(1)}, bf16[32,2560]{1,0:T(8,128)(2,1)S(1)}, u32[]{:S(2)}, u32[]{:S(2)}) collective-permute-start(bf16[32,2560]{1,0:T(8,128)(2,1)S(1)} %shard_map.114.mine), channel_id=1, source_target_pairs={{0,16},{16,0},{1,17},{17,1},{2,18},{18,2},{3,19},{19,3},{4,20},{20... | collective-permute-start | bytes 491528 | tf_op jit(solution)/shard_map/ppermute | solution.py:277
  84.3 0.0 collective-permute-done.2.theirs
  84.3 0.0 copy-done.5
  84.3 0.0 copy-done.6
  84.4 0.8 shard_map.117.tokens
  85.2 0.1 collective-permute-done.1.theirs
  85.3 5.5 %all-to-all-done.2.sums = bf16[16,80,128]{2,1,0:T(8,128)(2,1)S(1)} async-done(((bf16[16,80,128]{2,1,0:T(8,128)(2,1)}), bf16[16,80,128]{2,1,0:T(8,128)(2,1)S(1)}, u32[]{:S(2)}, u32[]{:S(2)}) %all-to-all-start.2) | async-done | bytes 327712 | tf_op jit(solution)/shard_map/all_to_all | solution.py:332
  90.9 0.0 all-gather.3.cloned.1.call-done
  90.9 5.3 %shard_map.118 = (f32[128,512]{1,0:T(8,128)S(1)}, f32[128,512]{1,0:T(8,128)S(1)}) custom-call(s32[1]{0:T(128)} %bitcast.8.place, bf16[16,80,128]{2,1,0:T(8,128)(2,1)S(1)} %all-to-all-done.2.sums, bf16[256,2560]{1,0:T(8,128)(2,1)S(1)} %shard_map.117.tokens, bf16[128,2560]{1,0:T(8,128)(2,1)S(1)} %get-tuple-element.18.mine, ...), custom_call_target="tpu_custom_call" | custom-call | tf_op jit(solution)/shard_map/pallas_call | solution.py:37
  96.2 6.1 %collective-permute-start.3 = (f32[128,512]{1,0:T(8,128)S(1)}, f32[128,512]{1,0:T(8,128)S(1)}, u32[]{:S(2)}, u32[]{:S(2)}) collective-permute-start(f32[128,512]{1,0:T(8,128)S(1)} %get-tuple-element.16), channel_id=1, source_target_pairs={{0,16},{16,0},{1,17},{17,1},{2,18},{18,2},{3,19},{19,3},{4,20},{20... | collective-permute-start | bytes 786440 | tf_op jit(solution)/shard_map/ppermute | solution.py:277
  102.3 0.8 shard_map.115
  103.1 0.4 collective-permute-done.3
  103.5 0.7 add_convert_fusion
Async XLA Ops:
  7.2 8.4 %copy-start.4 = (f32[128,128]{1,0:T(8,128)S(1)}, f32[128,128]{1,0:T(8,128)}, u32[]{:S(2)}) copy-start(f32[128,128]{1,0:T(8,128)} %constant.28.clone.b2) | copy-start | bytes 196612
  7.2 1.6 %copy-start = (bf16[32,5120]{1,0:T(8,128)(2,1)S(1)}, bf16[32,5120]{1,0:T(8,128)(2,1)}, u32[]{:S(2)}) copy-start(bf16[32,5120]{1,0:T(8,128)(2,1)} %old.1) | copy-start | bytes 983044
  7.2 8.4 %copy-start.2 = (bf16[1,32,5120]{2,1,0:T(8,128)(2,1)S(1)}, bf16[1,32,5120]{2,1,0:T(8,128)(2,1)}, u32[]{:S(2)}) copy-start(bf16[1,32,5120]{2,1,0:T(8,128)(2,1)} %param.11) | copy-start | bytes 983044
  7.2 8.4 %copy-start.1 = (f32[1,32,5120]{2,1,0:T(8,128)S(1)}, f32[1,32,5120]{2,1,0:T(8,128)}, u32[]{:S(2)}) copy-start(f32[1,32,5120]{2,1,0:T(8,128)} %param.10) | copy-start | bytes 1966084
  7.2 83.7 %all-gather.3.cloned.1.call-start = ((), (), s32[]{:S(2)}) async-start(), calls=%async_computation.3 | async-start | bytes 3317760 | tf_op jit(solution)/shard_map/all_gather | solution.py:323
  8.9 13.6 %collective-permute-start = (bf16[720,128]{1,0:T(8,128)(2,1)S(1)}, bf16[720,128]{1,0:T(8,128)(2,1)S(1)}, u32[]{:S(2)}, u32[]{:S(2)}) collective-permute-start(bf16[720,128]{1,0:T(8,128)(2,1)S(1)} %shard_map.113), channel_id=1, source_target_pairs={{0,104},{8,96},{32,72},{40,64},{64,40},{72,32},{96,8},{104,0},{1,1... | collective-permute-start | bytes 552968 | tf_op jit(solution)/shard_map/ppermute | solution.py:307
  15.6 35.2 %copy-start.7 = (bf16[128,5120]{1,0:T(8,128)(2,1)S(1)}, bf16[128,5120]{1,0:T(8,128)(2,1)}, u32[]{:S(2)}) copy-start(bf16[128,5120]{1,0:T(8,128)(2,1)} %param.9) | copy-start | bytes 3932164
  23.2 23.0 %all-to-all-start = ((f32[64,1,384]{2,1,0:T(1,128)}), f32[64,1,384]{2,1,0:T(1,128)S(1)}, u32[]{:S(2)}, u32[]{:S(2)}) async-start(f32[64,1,384]{2,1,0:T(1,128)} %bitcast.5), calls=%async_computation | async-start | bytes 196608 | tf_op jit(solution)/shard_map/all_to_all | solution.py:321
  47.0 13.0 %all-to-all-start.1 = ((f32[32,1,384]{2,1,0:T(1,128)}), f32[32,1,384]{2,1,0:T(1,128)S(1)}, u32[]{:S(2)}, u32[]{:S(2)}) async-start(f32[32,1,384]{2,1,0:T(1,128)} %broadcast_in_dim.4), calls=%async_computation.1 | async-start | bytes 98304 | tf_op jit(solution)/shard_map/all_to_all | solution.py:48
  50.9 28.2 %copy-start.3 = (bf16[384,128]{1,0:T(8,128)(2,1)S(1)}, bf16[384,128]{1,0:T(8,128)(2,1)}, u32[]{:S(2)}) copy-start(bf16[384,128]{1,0:T(8,128)(2,1)} %constant.29.clone.b2) | copy-start | bytes 294916
  51.8 32.5 %copy-start.5 = (bf16[128,128]{1,0:T(8,128)(2,1)S(1)}, bf16[128,128]{1,0:T(8,128)(2,1)}, u32[]{:S(2)}) copy-start(bf16[128,128]{1,0:T(8,128)(2,1)} %constant.31.clone.low) | copy-start | bytes 98308
  51.8 32.5 %copy-start.6 = (bf16[128,128]{1,0:T(8,128)(2,1)S(1)}, bf16[128,128]{1,0:T(8,128)(2,1)}, u32[]{:S(2)}) copy-start(bf16[128,128]{1,0:T(8,128)(2,1)} %constant.30.clone.high) | copy-start | bytes 98308
  51.8 32.5 %collective-permute-start.2 = (bf16[128,2560]{1,0:T(8,128)(2,1)}, bf16[128,2560]{1,0:T(8,128)(2,1)S(1)}, u32[]{:S(2)}, u32[]{:S(2)}) collective-permute-start(bf16[128,2560]{1,0:T(8,128)(2,1)} %get-tuple-element.17), channel_id=1, source_target_pairs={{0,16},{16,0},{1,17},{17,1},{2,18},{18,2},{3,19},{19,3},{4,20},{20... | collective-permute-start | bytes 1966088 | tf_op jit(solution)/shard_map/ppermute | solution.py:277
  60.8 30.1 %all-to-all-start.2 = ((bf16[16,80,128]{2,1,0:T(8,128)(2,1)}), bf16[16,80,128]{2,1,0:T(8,128)(2,1)S(1)}, u32[]{:S(2)}, u32[]{:S(2)}) async-start(bf16[16,80,128]{2,1,0:T(8,128)(2,1)} %shard_map.116), calls=%async_computation.2 | async-start | bytes 655360 | tf_op jit(solution)/shard_map/all_to_all | solution.py:332
  79.7 5.6 %collective-permute-start.1 = (bf16[32,2560]{1,0:T(8,128)(2,1)S(1)}, bf16[32,2560]{1,0:T(8,128)(2,1)S(1)}, u32[]{:S(2)}, u32[]{:S(2)}) collective-permute-start(bf16[32,2560]{1,0:T(8,128)(2,1)S(1)} %shard_map.114.mine), channel_id=1, source_target_pairs={{0,16},{16,0},{1,17},{17,1},{2,18},{18,2},{3,19},{19,3},{4,20},{20... | collective-permute-start | bytes 491528 | tf_op jit(solution)/shard_map/ppermute | solution.py:277
  96.2 7.2 %collective-permute-start.3 = (f32[128,512]{1,0:T(8,128)S(1)}, f32[128,512]{1,0:T(8,128)S(1)}, u32[]{:S(2)}, u32[]{:S(2)}) collective-permute-start(f32[128,512]{1,0:T(8,128)S(1)} %get-tuple-element.16), channel_id=1, source_target_pairs={{0,16},{16,0},{1,17},{17,1},{2,18},{18,2},{3,19},{19,3},{4,20},{20... | collective-permute-start | bytes 786440 | tf_op jit(solution)/shard_map/ppermute | solution.py:277
Sparse Core Ops, SparseCore 0:
  23.4 64.0 all-gather.2
